TPU v7x, 32 devices: a whole 2x2x4 slice. The times are simulated.
32 devices in a mesh: seq: 8 (over z, y), head: 4 (over x, core).
Axes of the slice: x: 2, y: 2, z: 4, core: 2. Of those that a mesh axis runs over, the one named last changes fastest.
Arguments:
- tokens: bfloat16 [2048, 2048], P('seq'), may hold values from -6 to 6
- attn_gain: bfloat16 [2048], P('seq'), may hold values from 0.5 to 1.5
- query_weight: bfloat16 [2048, 2048], P('seq', 'head'), may hold values from -0.15625 to 0.15625
- key_weight: bfloat16 [2048, 2048], P('seq', 'head'), may hold values from -0.15625 to 0.15625
- value_weight: bfloat16 [2048, 2048], P('seq', 'head'), may hold values from -0.125 to 0.125
- out_weight: bfloat16 [2048, 2048], P('head', 'seq'), may hold values from -1.796875 to 1.796875
- mlp_gain: bfloat16 [2048], P('seq'), may hold values from 0.5 to 1.5
- gate_weight: bfloat16 [2048, 8192], P('seq', 'head'), may hold values from -0.125 to 0.125
- up_weight: bfloat16 [2048, 8192], P('seq', 'head'), may hold values from -0.125 to 0.125
- down_weight: bfloat16 [8192, 2048], P('head', 'seq'), may hold values from -0.0625 to 0.0625
- cotangent: bfloat16 [2048, 2048], P('seq'), may hold values from -6 to 6
Outputs:
- output: bfloat16 [2048, 2048], P('seq')
- input_grad: bfloat16 [2048, 2048], P('seq')
- attn_gain_grad: float32 [2048], P('seq')
- query_weight_grad: float32 [2048, 2048], P('seq', 'head')
- key_weight_grad: float32 [2048, 2048], P('seq', 'head')
- value_weight_grad: float32 [2048, 2048], P('seq', 'head')
- out_weight_grad: float32 [2048, 2048], P('head', 'seq')
- mlp_gain_grad: float32 [2048], P('seq')
- gate_weight_grad: float32 [2048, 8192], P('seq', 'head')
- up_weight_grad: float32 [2048, 8192], P('seq', 'head')
- down_weight_grad: float32 [8192, 2048], P('head', 'seq')
All inputs are finite; a program needn't handle non-finite values.
Results may differ from a plain program's by a relative error of at most 0.015.
Values may be sent and summed in bfloat16 or wider, within the bound.
A program may use at most 192 MiB of HBM per device.

v0:
```python
import math

import jax
import jax.numpy as jnp
from jax import lax
from jax.sharding import PartitionSpec as P

HD = 128


epsilon = 1e-05
block_limit = 512


def tables(offset, length, half_width):
    places = (offset + jnp.arange(length, dtype=jnp.int32)).astype(jnp.float32)
    frequency = jnp.exp(
        jnp.arange(half_width, dtype=jnp.float32) * (-math.log(10000.0) / half_width)
    )
    angles = places[:, None] * frequency[None, :]
    return (jnp.cos(angles)[:, None, :], jnp.sin(angles)[:, None, :])


def rotary(values, cos_table, sin_table):
    half_width = values.shape[-1] // 2
    front = values[..., :half_width]
    back_half = values[..., half_width:]
    return jnp.concatenate(
        [front * cos_table - back_half * sin_table, back_half * cos_table + front * sin_table],
        axis=-1,
    )


def unrotary(gradient, cos_table, sin_table):
    half_width = gradient.shape[-1] // 2
    front = gradient[..., :half_width]
    back_half = gradient[..., half_width:]
    return jnp.concatenate(
        [front * cos_table + back_half * sin_table, back_half * cos_table - front * sin_table],
        axis=-1,
    )


def norm_back(values, inverse, gain_vector, upstream):
    scaled = upstream * gain_vector
    gain_grad = jnp.sum(upstream * values * inverse, axis=0)
    value_grad = inverse * scaled - values * inverse**3 * jnp.mean(
        scaled * values, axis=1, keepdims=True
    )
    return (value_grad, gain_grad)


def on_device(
    tokens,
    attn_gain,
    query_weight,
    key_weight,
    value_weight,
    out_weight,
    mlp_gain,
    gate_weight,
    up_weight,
    down_weight,
    cotangent,
):
    row_count = tokens.shape[0]
    total_rows = row_count * lax.axis_size("seq")
    row_start = lax.axis_index("seq") * row_count
    local_width = query_weight.shape[1]
    local_heads = local_width // HD
    score_scale = 1.0 / math.sqrt(HD)
    score_shift = math.log(total_rows)
    block_rows = math.gcd(total_rows, block_limit)
    block_count = total_rows // block_rows
    attn_gain_full, query_full, key_full, value_full, out_full = (
        lax.all_gather(attn_gain, "seq", axis=0, tiled=True),
        lax.all_gather(query_weight, "seq", axis=0, tiled=True),
        lax.all_gather(key_weight, "seq", axis=0, tiled=True),
        lax.all_gather(value_weight, "seq", axis=0, tiled=True),
        lax.all_gather(out_weight, "seq", axis=1, tiled=True),
    )
    mlp_gain_full, gate_full, up_full, down_full = (
        lax.all_gather(mlp_gain, "seq", axis=0, tiled=True),
        lax.all_gather(gate_weight, "seq", axis=0, tiled=True),
        lax.all_gather(up_weight, "seq", axis=0, tiled=True),
        lax.all_gather(down_weight, "seq", axis=1, tiled=True),
    )
    token_values = tokens.astype(jnp.float32)
    inverse_one = lax.rsqrt(jnp.mean(token_values * token_values, axis=1, keepdims=True) + epsilon)
    normed_one = (token_values * inverse_one * attn_gain_full.astype(jnp.float32)).astype(
        jnp.bfloat16
    )
    query_pre = jnp.dot(normed_one, query_full, preferred_element_type=jnp.float32)
    key_pre = jnp.dot(normed_one, key_full, preferred_element_type=jnp.float32)
    value_rows = (
        jnp.dot(normed_one, value_full, preferred_element_type=jnp.float32)
        .astype(jnp.bfloat16)
        .reshape(row_count, local_heads, HD)
    )
    cos_table, sin_table = tables(row_start, row_count, HD // 2)
    query_rows = (
        rotary(query_pre.reshape(row_count, local_heads, HD), cos_table, sin_table)
        .astype(jnp.bfloat16)
        .reshape(row_count, local_width)
    )
    key_rows = rotary(key_pre.reshape(row_count, local_heads, HD), cos_table, sin_table).astype(
        jnp.bfloat16
    )
    all_queries = lax.all_gather(query_rows, "seq", axis=0, tiled=True)
    key_places = row_start + jnp.arange(row_count, dtype=jnp.int32)

    def weights_for(query_block, block_start):
        scores = (
            jnp.einsum("qhd,khd->hqk", query_block, key_rows, preferred_element_type=jnp.float32)
            * score_scale
            - score_shift
        )
        query_places = block_start + jnp.arange(query_block.shape[0], dtype=jnp.int32)
        visible = key_places[None, :] <= query_places[:, None]
        return jnp.where(visible[None], jax.nn.sigmoid(scores), 0.0)

    step_rows = math.gcd(row_count * lax.axis_size("seq"), block_limit)
    step_count = row_count * lax.axis_size("seq") // step_rows
    picked = all_queries.reshape(step_count, step_rows, local_heads, HD)
    starts = jnp.arange(step_count, dtype=jnp.int32) * step_rows

    def one_block(packed):
        query_block, block_start = packed
        weights = weights_for(query_block, block_start).astype(jnp.bfloat16)
        return jnp.einsum(
            "hqk,khd->qhd", weights, value_rows, preferred_element_type=jnp.float32
        ).reshape(step_rows, local_width)

    attn_mix = lax.psum_scatter(
        lax.map(one_block, (picked, starts)).reshape(row_count * lax.axis_size("seq"), local_width),
        "seq",
        scatter_dimension=0,
        tiled=True,
    ).astype(jnp.bfloat16)
    attn_branch = lax.psum(jnp.dot(attn_mix, out_full, preferred_element_type=jnp.float32), "head")
    hidden = token_values + attn_branch
    inverse_two = lax.rsqrt(jnp.mean(hidden * hidden, axis=1, keepdims=True) + epsilon)
    normed_two = (hidden * inverse_two * mlp_gain_full.astype(jnp.float32)).astype(jnp.bfloat16)
    gate_pre = jnp.dot(normed_two, gate_full, preferred_element_type=jnp.float32)
    up_pre = jnp.dot(normed_two, up_full, preferred_element_type=jnp.float32)
    gate_act = jax.nn.silu(gate_pre)
    mixed = (gate_act * up_pre).astype(jnp.bfloat16)
    mlp_branch = lax.psum(
        jnp.dot(mixed, down_full, preferred_element_type=jnp.float32).astype(jnp.bfloat16), "head"
    ).astype(jnp.float32)
    result = (hidden + mlp_branch).astype(jnp.bfloat16)
    kept_weights = (
        lax.all_gather(attn_gain, "seq", axis=0, tiled=True),
        lax.all_gather(query_weight, "seq", axis=0, tiled=True),
        lax.all_gather(key_weight, "seq", axis=0, tiled=True),
        lax.all_gather(value_weight, "seq", axis=0, tiled=True),
        lax.all_gather(out_weight, "seq", axis=1, tiled=True),
        lax.all_gather(mlp_gain, "seq", axis=0, tiled=True),
        lax.all_gather(gate_weight, "seq", axis=0, tiled=True),
        lax.all_gather(up_weight, "seq", axis=0, tiled=True),
        lax.all_gather(down_weight, "seq", axis=1, tiled=True),
    )
    (
        attn_gain_back,
        query_back,
        key_back,
        value_back,
        out_back,
        mlp_gain_back,
        gate_back,
        up_back,
        down_back,
    ) = kept_weights
    attn_gain_f = attn_gain_back.astype(jnp.float32)
    mlp_gain_f = mlp_gain_back.astype(jnp.float32)
    grad_values = cotangent.astype(jnp.float32)
    grad_down = jnp.einsum("tf,td->fd", mixed, cotangent, preferred_element_type=jnp.float32)
    dmixed = jnp.einsum("td,fd->tf", cotangent, down_back, preferred_element_type=jnp.float32)
    gate_sig = jax.nn.sigmoid(gate_pre)
    dgate = (dmixed * up_pre * gate_sig * (1.0 + gate_pre * (1.0 - gate_sig))).astype(jnp.bfloat16)
    dup = (dmixed * gate_act).astype(jnp.bfloat16)
    grad_gate = jnp.einsum("tk,tf->kf", normed_two, dgate, preferred_element_type=jnp.float32)
    grad_up = jnp.einsum("tk,tf->kf", normed_two, dup, preferred_element_type=jnp.float32)
    dnormed_two = lax.psum(
        jnp.einsum("tf,kf->tk", dgate, gate_back, preferred_element_type=jnp.float32)
        + jnp.einsum("tf,kf->tk", dup, up_back, preferred_element_type=jnp.float32),
        "head",
    )
    dhidden_norm, grad_mlp_gain = norm_back(hidden, inverse_two, mlp_gain_f, dnormed_two)
    dhidden = grad_values + dhidden_norm
    mlp_sums = (grad_mlp_gain, grad_gate, grad_up, grad_down)
    dhidden_low = dhidden.astype(jnp.bfloat16)
    grad_out = jnp.einsum("tc,td->cd", attn_mix, dhidden_low, preferred_element_type=jnp.float32)
    dmix = jnp.einsum(
        "td,cd->tc", dhidden_low, out_back, preferred_element_type=jnp.float32
    ).astype(jnp.bfloat16)
    all_dmix = lax.all_gather(dmix, "seq", axis=0, tiled=True)

    def backward_block(carry, packed):
        key_accum, value_accum = carry
        query_block, grad_block, block_start = packed
        weights = weights_for(query_block, block_start)
        grad_weights = jnp.einsum(
            "qhd,khd->hqk", grad_block, value_rows, preferred_element_type=jnp.float32
        )
        grad_scores = (grad_weights * weights * (1.0 - weights)).astype(jnp.bfloat16)
        value_accum = value_accum + jnp.einsum(
            "hqk,qhd->khd",
            weights.astype(jnp.bfloat16),
            grad_block,
            preferred_element_type=jnp.float32,
        )
        key_accum = key_accum + jnp.einsum(
            "hqk,qhd->khd", grad_scores, query_block, preferred_element_type=jnp.float32
        )
        query_part = (
            jnp.einsum("hqk,khd->qhd", grad_scores, key_rows, preferred_element_type=jnp.float32)
            * score_scale
        )
        return ((key_accum, value_accum), query_part.reshape(block_rows, local_width))

    zero_rows = jnp.zeros((row_count, local_heads, HD), jnp.float32)
    block_starts = jnp.arange(block_count, dtype=jnp.int32) * block_rows
    (key_accum, value_accum), query_parts = lax.scan(
        backward_block,
        (zero_rows, zero_rows),
        (
            all_queries.reshape(block_count, block_rows, local_heads, HD),
            all_dmix.reshape(block_count, block_rows, local_heads, HD),
            block_starts,
        ),
    )
    query_sum = lax.psum_scatter(
        query_parts.reshape(total_rows, local_width), "seq", scatter_dimension=0, tiled=True
    )
    dquery_pre = (
        unrotary(query_sum.reshape(row_count, local_heads, HD), cos_table, sin_table)
        .reshape(row_count, local_width)
        .astype(jnp.bfloat16)
    )
    dkey_pre = (
        unrotary(key_accum * score_scale, cos_table, sin_table)
        .reshape(row_count, local_width)
        .astype(jnp.bfloat16)
    )
    dvalue = value_accum.reshape(row_count, local_width).astype(jnp.bfloat16)
    grad_query = jnp.einsum("tk,tc->kc", normed_one, dquery_pre, preferred_element_type=jnp.float32)
    grad_key = jnp.einsum("tk,tc->kc", normed_one, dkey_pre, preferred_element_type=jnp.float32)
    grad_value = jnp.einsum("tk,tc->kc", normed_one, dvalue, preferred_element_type=jnp.float32)
    dnormed_one = lax.psum(
        jnp.einsum("tc,kc->tk", dquery_pre, query_back, preferred_element_type=jnp.float32)
        + jnp.einsum("tc,kc->tk", dkey_pre, key_back, preferred_element_type=jnp.float32)
        + jnp.einsum("tc,kc->tk", dvalue, value_back, preferred_element_type=jnp.float32),
        "head",
    )
    dinput_norm, grad_attn_gain = norm_back(token_values, inverse_one, attn_gain_f, dnormed_one)
    input_grad = (dhidden + dinput_norm).astype(jnp.bfloat16)
    every_sum = (
        lax.psum_scatter(grad_attn_gain, "seq", scatter_dimension=0, tiled=True),
        lax.psum_scatter(grad_query, "seq", scatter_dimension=0, tiled=True),
        lax.psum_scatter(grad_key, "seq", scatter_dimension=0, tiled=True),
        lax.psum_scatter(grad_value, "seq", scatter_dimension=0, tiled=True),
        lax.psum_scatter(grad_out, "seq", scatter_dimension=1, tiled=True),
        lax.psum_scatter(grad_mlp_gain, "seq", scatter_dimension=0, tiled=True),
        lax.psum_scatter(grad_gate, "seq", scatter_dimension=0, tiled=True),
        lax.psum_scatter(grad_up, "seq", scatter_dimension=0, tiled=True),
        lax.psum_scatter(grad_down, "seq", scatter_dimension=1, tiled=True),
    )
    attn_sums = every_sum[:5]
    mlp_sums = every_sum[5:]
    return (
        result,
        input_grad,
        attn_sums[0],
        attn_sums[1],
        attn_sums[2],
        attn_sums[3],
        attn_sums[4],
        mlp_sums[0],
        mlp_sums[1],
        mlp_sums[2],
        mlp_sums[3],
    )


def solution(mesh):
    in_specs = (
        P("seq", None),
        P("seq"),
        P("seq", "head"),
        P("seq", "head"),
        P("seq", "head"),
        P("head", "seq"),
        P("seq"),
        P("seq", "head"),
        P("seq", "head"),
        P("head", "seq"),
        P("seq", None),
    )
    out_specs = (
        P("seq", None),
        P("seq", None),
        P("seq"),
        P("seq", "head"),
        P("seq", "head"),
        P("seq", "head"),
        P("head", "seq"),
        P("seq"),
        P("seq", "head"),
        P("seq", "head"),
        P("head", "seq"),
    )
    return jax.shard_map(
        on_device, mesh=mesh, in_specs=in_specs, out_specs=out_specs, check_vma=False
    )
```

profile of v0, /device:TPU:0, one launch (start us, length us, event | category | flops | bytes accessed | tf_op | source)
XLA Modules:
  0.0 2380.9 jit_solution(6191785137841903795)
XLA Ops:
  10.1 22.3 all-gather
  34.8 27.3 %all-gather.16.cloned.1.call-done = bf16[2048,512]{1,0:T(8,128)(2,1)} async-done(((bf16[256,512]{1,0:T(8,128)(2,1)}), bf16[2048,512]{1,0:T(8,128)(2,1)}) %all-gather.16.cloned.1.call-update) | async-done | bytes 2097168 | tf_op jit(solution)/shard_map/all_gather | solution.py:78
  62.2 3.0 fusion.53
  65.2 46.9 %all-gather.12.cloned.1.call-done = bf16[2048,512]{1,0:T(8,128)(2,1)} async-done(((bf16[256,512]{1,0:T(8,128)(2,1)}), bf16[2048,512]{1,0:T(8,128)(2,1)}) %all-gather.12.cloned.1.call-update) | async-done | bytes 2097168 | tf_op jit(solution)/shard_map/all_gather | solution.py:77
  112.1 2.6 fusion.55
  117.3 44.8 %all-gather.18.cloned.1.call-done = bf16[2048,512]{1,0:T(8,128)(2,1)} async-done(((bf16[256,512]{1,0:T(8,128)(2,1)}), bf16[2048,512]{1,0:T(8,128)(2,1)}) %all-gather.18.cloned.1.call-update) | async-done | bytes 2097168 | tf_op jit(solution)/shard_map/all_gather | solution.py:79
  165.2 47.2 %all-gather.14.cloned.1.call-done = bf16[2048,512]{1,0:T(8,128)(2,1)} async-done(((bf16[256,512]{1,0:T(8,128)(2,1)}), bf16[2048,512]{1,0:T(8,128)(2,1)}) %all-gather.14.cloned.1.call-update) | async-done | bytes 2097168 | tf_op jit(solution)/shard_map/all_gather | solution.py:109
  212.4 2.5 reshape.222
  219.2 19.7 while.30
  239.5 24.4 %all-gather.20.cloned.1.call-done = bf16[512,2048]{1,0:T(8,128)(2,1)} async-done(((bf16[512,256]{1,0:T(8,128)(2,1)}), bf16[512,2048]{1,0:T(8,128)(2,1)}) %all-gather.20.cloned.1.call-update) | async-done | bytes 2097168 | tf_op jit(solution)/shard_map/all_gather | solution.py:80
  263.9 89.6 %reduce-scatter.10.cloned.1.call-done = f32[256,512]{1,0:T(8,128)} async-done(((f32[2048,512]{1,0:T(8,128)}), f32[256,512]{1,0:T(8,128)}) %reduce-scatter.10.cloned.1.call-update) | async-done | bytes 524304 | tf_op jit(solution)/shard_map/reduce_scatter | solution.py:134
  353.5 3.8 fusion.44
  359.5 19.5 all-gather.1
  379.0 29.6 %all-reduce.8.cloned.1.call-done = f32[256,2048]{1,0:T(8,128)} async-done(((f32[256,2048]{1,0:T(8,128)}), f32[256,2048]{1,0:T(8,128)}) %all-reduce.8.cloned.1.call-update) | async-done | bytes 2097168 | tf_op jit(solution)/shard_map/psum | solution.py:140
  412.1 123.7 %all-gather.22.cloned.1.call-done = bf16[2048,2048]{1,0:T(8,128)(2,1)} async-done(((bf16[256,2048]{1,0:T(8,128)(2,1)}), bf16[2048,2048]{1,0:T(8,128)(2,1)}) %all-gather.22.cloned.1.call-update) | async-done | bytes 8388624 | tf_op jit(solution)/shard_map/all_gather | solution.py:84
  535.8 7.0 fusion.57
  542.8 118.2 %all-gather.24.cloned.1.call-done = bf16[2048,2048]{1,0:T(8,128)(2,1)} async-done(((bf16[256,2048]{1,0:T(8,128)(2,1)}), bf16[2048,2048]{1,0:T(8,128)(2,1)}) %all-gather.24.cloned.1.call-update) | async-done | bytes 8388624 | tf_op jit(solution)/shard_map/all_gather | solution.py:85
  661.0 7.0 fusion.58
  668.1 118.5 %all-gather.26.cloned.1.call-done = bf16[2048,2048]{1,0:T(8,128)(2,1)} async-done(((bf16[2048,256]{1,0:T(8,128)(2,1)}), bf16[2048,2048]{1,0:T(8,128)(2,1)}) %all-gather.26.cloned.1.call-update) | async-done | bytes 8388624 | tf_op jit(solution)/shard_map/all_gather | solution.py:86
  786.5 8.7 multiply_convert_fusion.1
  795.2 6.6 fusion.59
  801.8 3.7 convolution_add_fusion.2
  805.8 7.4 convolution_convert_fusion
  813.3 41.9 %all-reduce.12.cloned.1.call-done = f32[256,2048]{1,0:T(8,128)} async-done(((f32[256,2048]{1,0:T(8,128)}), f32[256,2048]{1,0:T(8,128)}) %all-reduce.12.cloned.1.call-update) | async-done | bytes 2097168 | tf_op jit(solution)/shard_map/psum | solution.py:184
  855.2 2.8 multiply_reduce_fusion
  858.6 35.7 %all-reduce.10.cloned.1.call-done = bf16[256,2048]{1,0:T(8,128)(2,1)} async-done(((bf16[256,2048]{1,0:T(8,128)(2,1)}), bf16[256,2048]{1,0:T(8,128)(2,1)}) %all-reduce.10.cloned.1.call-update) | async-done | bytes 1048592 | tf_op jit(solution)/shard_map/psum | solution.py:148
  894.3 3.8 subtract_add_fusion
  901.7 49.0 %all-gather.28.cloned.1.call-done = bf16[2048,512]{1,0:T(8,128)(2,1)} async-done(((bf16[256,512]{1,0:T(8,128)(2,1)}), bf16[2048,512]{1,0:T(8,128)(2,1)}) %all-gather.28.cloned.1.call-update) | async-done | bytes 2097168 | tf_op jit(solution)/shard_map/all_gather | solution.py:197
  950.7 4.0 reshape.226
  957.2 43.0 %while.31 = (s32[]{:T(128)}, f32[256,4,128]{0,2,1:T(8,128)}, f32[256,4,128]{0,2,1:T(8,128)}, f32[4,512,512]{2,1,0:T(8,128)}, bf16[4,512,4,128]{3,1,2,0:T(8,128)(...) while((s32[]{:T(128)}, f32[256,4,128]{0,2,1:T(8,128)}, ...), condition=%wide.region_10.11_spmd.clone, body=%wide.region_9.10_spmd.clone.sunk | while | flops 677774080 | bytes 30415160 | solution.py:224
  1001.4 85.5 %reduce-scatter.12.cloned.1.call-done = f32[256,512]{1,0:T(8,128)} async-done(((f32[2048,512]{1,0:T(8,128)}), f32[256,512]{1,0:T(8,128)}) %reduce-scatter.12.cloned.1.call-update) | async-done | bytes 524304 | tf_op jit(solution)/shard_map/reduce_scatter | solution.py:233
  1095.5 2.8 fusion.40
  1099.8 2.8 fusion.46
  1103.6 2.9 fusion.50
  1107.4 2.9 fusion.48
  1110.3 9.7 fusion.61
  1120.2 10.0 fusion.62
  1130.3 9.7 fusion.63
  1141.9 3.3 all-reduce.14.cloned.1.call-done
  1147.3 38.8 %all-reduce.2 = (f32[2048]{0:T(1024)S(1)}, f32[2048]{0:T(1024)S(1)}) all-reduce(f32[2048]{0:T(1024)S(1)} %get-tuple-element.337, f32[2048]{0:T(1024)S(1)} %copy-done.30), channel_id=4, replica_groups=mesh['seq'=8,'head'=4] {'seq'}, use_global_device_ids=true, to_apply=%region_15.16.clone | all-reduce | flops 4096 | bytes 32768
  1187.4 3.2 fusion.35
  1190.6 47.5 %reduce-scatter.20.cloned.1.call-done = f32[512,256]{1,0:T(8,128)} async-done(((f32[512,2048]{1,0:T(8,128)}), f32[512,256]{1,0:T(8,128)}) %reduce-scatter.20.cloned.1.call-update) | async-done | bytes 524304 | tf_op jit(solution)/shard_map/reduce_scatter | solution.py:263
  1238.1 92.2 %reduce-scatter.18.cloned.1.call-done = f32[256,512]{1,0:T(8,128)} async-done(((f32[2048,512]{1,0:T(8,128)}), f32[256,512]{1,0:T(8,128)}) %reduce-scatter.18.cloned.1.call-update) | async-done | bytes 524304 | tf_op jit(solution)/shard_map/reduce_scatter | solution.py:262
  1330.3 91.7 %reduce-scatter.14.cloned.1.call-done = f32[256,512]{1,0:T(8,128)} async-done(((f32[2048,512]{1,0:T(8,128)}), f32[256,512]{1,0:T(8,128)}) %reduce-scatter.14.cloned.1.call-update) | async-done | bytes 524304 | tf_op jit(solution)/shard_map/reduce_scatter | solution.py:260
  1422.0 92.3 %reduce-scatter.16.cloned.1.call-done = f32[256,512]{1,0:T(8,128)} async-done(((f32[2048,512]{1,0:T(8,128)}), f32[256,512]{1,0:T(8,128)}) %reduce-scatter.16.cloned.1.call-update) | async-done | bytes 524304 | tf_op jit(solution)/shard_map/reduce_scatter | solution.py:261
  1514.3 286.7 %reduce-scatter.22.cloned.1.call-done = f32[256,2048]{1,0:T(8,128)} async-done(((f32[2048,2048]{1,0:T(8,128)}), f32[256,2048]{1,0:T(8,128)}) %reduce-scatter.22.cloned.1.call-update) | async-done | bytes 2097168 | tf_op jit(solution)/shard_map/reduce_scatter | solution.py:265
  1801.0 286.4 %reduce-scatter.24.cloned.1.call-done = f32[256,2048]{1,0:T(8,128)} async-done(((f32[2048,2048]{1,0:T(8,128)}), f32[256,2048]{1,0:T(8,128)}) %reduce-scatter.24.cloned.1.call-update) | async-done | bytes 2097168 | tf_op jit(solution)/shard_map/reduce_scatter | solution.py:266
  2087.4 286.2 %reduce-scatter.26.cloned.1.call-done = f32[2048,256]{1,0:T(8,128)} async-done(((f32[2048,2048]{1,0:T(8,128)}), f32[2048,256]{1,0:T(8,128)}) %reduce-scatter.26.cloned.1.call-update) | async-done | bytes 2097168 | tf_op jit(solution)/shard_map/reduce_scatter | solution.py:267
  (267 shorter events, 108.4 us)
Async XLA Ops:
  7.2 55.0 %all-gather.16.cloned.1.call-start = ((), (), s32[]{:S(2)}) async-start(), calls=%async_computation.11 | async-start | bytes 2359296 | tf_op jit(solution)/shard_map/all_gather | solution.py:78
  7.9 104.2 %all-gather.12.cloned.1.call-start = ((), (), s32[]{:S(2)}) async-start(), calls=%async_computation.9 | async-start | bytes 2359296 | tf_op jit(solution)/shard_map/all_gather | solution.py:77
  8.7 153.4 %all-gather.18.cloned.1.call-start = ((), (), s32[]{:S(2)}) async-start(), calls=%async_computation.12 | async-start | bytes 2359296 | tf_op jit(solution)/shard_map/all_gather | solution.py:79
  9.4 203.0 %all-gather.14.cloned.1.call-start = ((), (), s32[]{:S(2)}) async-start(), calls=%async_computation.10 | async-start | bytes 2359296 | tf_op jit(solution)/shard_map/all_gather | solution.py:109
  34.5 127.5 %copy-start.28 = (f32[256]{0:T(256)}, f32[256]{0:T(256)S(1)}, u32[]{:S(2)}) copy-start(f32[256]{0:T(256)S(1)} %get-tuple-element.397) | copy-start | bytes 3076
  62.2 49.9 %copy-start.2 = (bf16[256,2048]{1,0:T(8,128)(2,1)S(1)}, bf16[256,2048]{1,0:T(8,128)(2,1)}, u32[]{:S(2)}) copy-start(bf16[256,2048]{1,0:T(8,128)(2,1)} %param.15) | copy-start | bytes 3145732
  115.8 148.1 %all-gather.20.cloned.1.call-start = ((), (), s32[]{:S(2)}) async-start(), calls=%async_computation.14 | async-start | bytes 2359296 | tf_op jit(solution)/shard_map/all_gather | solution.py:80
  116.4 237.1 %reduce-scatter.10.cloned.1.call-start = ((), (), s32[]{:S(2)}) async-start(), calls=%async_computation.13 | async-start | bytes 4718592 | tf_op jit(solution)/shard_map/reduce_scatter | solution.py:134
  239.5 169.1 %all-reduce.8.cloned.1.call-start = ((), (), s32[]{:S(2)}) async-start(), calls=%async_computation.15 | async-start | bytes 4194304 | tf_op jit(solution)/shard_map/psum | solution.py:140
  357.3 178.4 %all-gather.22.cloned.1.call-start = ((), (), s32[]{:S(2)}) async-start(), calls=%async_computation.16 | async-start | bytes 9437184 | tf_op jit(solution)/shard_map/all_gather | solution.py:84
  358.1 303.0 %all-gather.24.cloned.1.call-start = ((), (), s32[]{:S(2)}) async-start(), calls=%async_computation.17 | async-start | bytes 9437184 | tf_op jit(solution)/shard_map/all_gather | solution.py:85
  358.8 427.7 %all-gather.26.cloned.1.call-start = ((), (), s32[]{:S(2)}) async-start(), calls=%async_computation.18 | async-start | bytes 9437184 | tf_op jit(solution)/shard_map/all_gather | solution.py:86
  359.4 495.9 %all-reduce.12.cloned.1.call-start = ((), (), s32[]{:S(2)}) async-start(), calls=%async_computation.20 | async-start | bytes 4194304 | tf_op jit(solution)/shard_map/psum | solution.py:184
  412.1 248.9 %copy-start.12 = (bf16[256,2048]{1,0:T(8,128)(2,1)}, bf16[256,2048]{1,0:T(8,128)(2,1)S(1)}, u32[]{:S(2)}) copy-start(bf16[256,2048]{1,0:T(8,128)(2,1)S(1)} %multiply_convert_fusion.4) | copy-start | bytes 3145732
  542.8 243.7 %copy-start.15 = (bf16[256,2048]{1,0:T(8,128)(2,1)S(1)}, bf16[256,2048]{1,0:T(8,128)(2,1)}, u32[]{:S(2)}) copy-start(bf16[256,2048]{1,0:T(8,128)(2,1)} %param.25) | copy-start | bytes 3145732
  795.2 6.6 copy-start.25
  795.2 6.6 copy-start.24
  795.2 6.6 copy-start.33
  805.5 88.8 %all-reduce.10.cloned.1.call-start = ((), (), s32[]{:S(2)}) async-start(), calls=%async_computation.19 | async-start | bytes 2097152 | tf_op jit(solution)/shard_map/psum | solution.py:148
  805.8 49.5 %copy-start.7 = (f32[256,2048]{1,0:T(8,128)S(1)}, f32[256,2048]{1,0:T(8,128)}, u32[]{:S(2)}) copy-start(f32[256,2048]{1,0:T(8,128)} %copy-done.6) | copy-start | bytes 6291460
  813.3 137.4 %all-gather.28.cloned.1.call-start = ((), (), s32[]{:S(2)}) async-start(), calls=%async_computation.21 | async-start | bytes 2359296 | tf_op jit(solution)/shard_map/all_gather | solution.py:197
  894.3 5.1 copy-start.14
  900.9 186.0 %reduce-scatter.12.cloned.1.call-start = ((), (), s32[]{:S(2)}) async-start(), calls=%async_computation.22 | async-start | bytes 4718592 | tf_op jit(solution)/shard_map/reduce_scatter | solution.py:233
  954.6 2.5 copy-start.37
  958.6 3.9 copy-start.13
  962.9 2.3 copy-start.1
  962.9 2.3 copy-start.9
  969.2 3.9 copy-start.13
  973.6 2.5 copy-start.1
  973.6 2.5 copy-start.9
  980.0 3.9 copy-start.13
  984.3 2.5 copy-start.1
  984.3 2.4 copy-start.9
  990.8 3.9 copy-start.13
  995.1 2.5 copy-start.1
  995.1 2.5 copy-start.9
  1000.2 145.0 %all-reduce.14.cloned.1.call-start = ((), (), s32[]{:S(2)}) async-start(), calls=%async_computation.23 | async-start | bytes 4194304 | tf_op jit(solution)/shard_map/psum | solution.py:250
  1001.4 87.0 %copy-start.22 = (bf16[2048,512]{1,0:T(8,128)(2,1)S(1)}, bf16[2048,512]{1,0:T(8,128)(2,1)}, u32[]{:S(2)}) copy-start(bf16[2048,512]{1,0:T(8,128)(2,1)} %all-gather.12.cloned.1.call-done) | copy-start | bytes 6291460
  1091.7 2.2 copy-start.23
  1093.9 144.1 %reduce-scatter.20.cloned.1.call-start = ((), (), s32[]{:S(2)}) async-start(), calls=%async_computation.27 | async-start | bytes 4718592 | tf_op jit(solution)/shard_map/reduce_scatter | solution.py:263
  1098.3 231.9 %reduce-scatter.18.cloned.1.call-start = ((), (), s32[]{:S(2)}) async-start(), calls=%async_computation.26 | async-start | bytes 4718592 | tf_op jit(solution)/shard_map/reduce_scatter | solution.py:262
  1102.6 319.3 %reduce-scatter.14.cloned.1.call-start = ((), (), s32[]{:S(2)}) async-start(), calls=%async_computation.24 | async-start | bytes 4718592 | tf_op jit(solution)/shard_map/reduce_scatter | solution.py:260
  1106.4 407.9 %reduce-scatter.16.cloned.1.call-start = ((), (), s32[]{:S(2)}) async-start(), calls=%async_computation.25 | async-start | bytes 4718592 | tf_op jit(solution)/shard_map/reduce_scatter | solution.py:261
  1110.3 690.7 %reduce-scatter.22.cloned.1.call-start = ((), (), s32[]{:S(2)}) async-start(), calls=%async_computation.28 | async-start | bytes 18874368 | tf_op jit(solution)/shard_map/reduce_scatter | solution.py:265
  1120.1 967.3 %reduce-scatter.24.cloned.1.call-start = ((), (), s32[]{:S(2)}) async-start(), calls=%async_computation.29 | async-start | bytes 18874368 | tf_op jit(solution)/shard_map/reduce_scatter | solution.py:266
  1130.2 1243.4 %reduce-scatter.26.cloned.1.call-start = ((), (), s32[]{:S(2)}) async-start(), calls=%async_computation.30 | async-start | bytes 18874368 | tf_op jit(solution)/shard_map/reduce_scatter | solution.py:267
  1140.0 7.3 copy-start.30
  1140.0 47.4 %copy-start.32 = (f32[256]{0:T(256)S(1)}, f32[256]{0:T(256)}, u32[]{:S(2)}) copy-start(f32[256]{0:T(256)} %get-tuple-element.396) | copy-start | bytes 3076
  (27 other events, 29.1 us)
Sparse Core Ops, SparseCore 0:
  10.1 51.9 all-gather.15
  64.3 47.7 all-gather.11
  114.2 47.7 all-gather.17
  164.6 47.7 all-gather.13
  214.3 49.5 all-gather.19
  267.4 86.0 reduce-scatter.9
  357.4 51.1 all-reduce.7
  410.7 125.0 all-gather.21
  537.9 123.1 all-gather.23
  662.9 123.5 all-gather.25
  805.7 49.5 all-reduce.11
  858.2 36.0 all-reduce.9
  901.0 49.6 all-gather.27
  1000.3 86.5 reduce-scatter.11
  1094.0 51.1 all-reduce.13
  1149.3 88.7 reduce-scatter.19
  1242.6 87.6 reduce-scatter.17
  1334.3 87.6 reduce-scatter.13
  1426.6 87.6 reduce-scatter.15
  1518.5 282.4 reduce-scatter.21
  1805.9 281.5 reduce-scatter.23
  2091.8 281.7 reduce-scatter.25
where the time goes:
time: 2390 us; the launch traced here: 2380 us
  waiting for transfers between devices  2070 us (87%)
  matrix products  129 us (5%)
  blocking collectives  80.6 us (3%)
  local copies, waits for them, and re-layouts  56 us (2%)
  other arithmetic  24.4 us (1%)
    reduce_scatter x1, waiting for transfers between devices, on_device(): lax.psum_scatter(grad_gate, 'seq', scatter_dimension=0, tiled=True)  287 us
    reduce_scatter x1, waiting for transfers between devices, on_device(): lax.psum_scatter(grad_up, 'seq', scatter_dimension=0, tiled=True)  286 us
    reduce_scatter x1, waiting for transfers between devices, on_device(): lax.psum_scatter(grad_down, 'seq', scatter_dimension=1, tiled=True)  286 us
    all_gather x1, waiting for transfers between devices, on_device(): lax.all_gather(gate_weight, 'seq', axis=0, tiled=True)  124 us
    all_gather x1, waiting for transfers between devices, on_device(): lax.all_gather(down_weight, 'seq', axis=1, tiled=True)  118 us
    all_gather x1, waiting for transfers between devices, on_device(): lax.all_gather(up_weight, 'seq', axis=0, tiled=True)  118 us
    reduce_scatter x1, waiting for transfers between devices, on_device(): lax.psum_scatter(grad_key, 'seq', scatter_dimension=0, tiled=True)  92.3 us
    reduce_scatter x1, waiting for transfers between devices, on_device(): lax.psum_scatter(grad_value, 'seq', scatter_dimension=0, tiled=True)  92.2 us
  transfers between devices with their start and end apart: 22, of which 22 were waited for; matrix products, arithmetic and copies ran while one was open for 5% of the time, Pallas kernels for 0%

commit v1 on v0

--- a/solution.py
+++ b/solution.py
@@ -1,9 +1,15 @@
+import functools
 import math
 
 import jax
 import jax.numpy as jnp
 from jax import lax
+from jax.experimental import pallas as pl
+from jax.experimental.pallas import tpu as pltpu
 from jax.sharding import PartitionSpec as P
+
+MESH = pl.DeviceIdType.MESH
+F32, BF16 = jnp.float32, jnp.bfloat16
 
 HD = 128
 
@@ -50,7 +56,7 @@
     return (value_grad, gain_grad)
 
 
-def on_device(
+def gathered_weights(
     tokens,
     attn_gain,
     query_weight,
@@ -283,6 +289,506 @@
     )
 
 
+def place():
+    return lax.axis_index("seq"), lax.axis_index("head")
+
+
+def enter(peers):
+    barrier = pltpu.get_barrier_semaphore()
+    for peer in peers:
+        pl.semaphore_signal(barrier, inc=1, device_id=peer, device_id_type=MESH)
+    pl.semaphore_wait(barrier, len(peers))
+
+
+class Net:
+    def __init__(self, send, receive):
+        self.send, self.receive, self.copies = send, receive, []
+
+    def put(self, source, target, device):
+        i = len(self.copies)
+        copy = pltpu.make_async_remote_copy(
+            src_ref=source,
+            dst_ref=target,
+            send_sem=self.send.at[i],
+            recv_sem=self.receive.at[i],
+            device_id=device,
+            device_id_type=MESH,
+        )
+        copy.start()
+        self.copies.append(copy)
+        return copy
+
+    def sent(self):
+        for copy in self.copies:
+            copy.wait_send()
+
+
+def whole(space):
+    return pl.BlockSpec(memory_space=space)
+
+
+def talk(body, ins, outs, scratch, ident, space=pl.ANY, copies=64):
+    return pl.pallas_call(
+        body,
+        out_shape=outs,
+        in_specs=[whole(space)] * len(ins),
+        out_specs=[whole(space)] * len(outs),
+        scratch_shapes=[
+            *scratch,
+            pltpu.SemaphoreType.DMA((copies,)),
+            pltpu.SemaphoreType.DMA((copies,)),
+            pltpu.SemaphoreType.DMA((16,)),
+        ],
+        compiler_params=pltpu.CompilerParams(
+            collective_id=ident, has_side_effects=True, vmem_limit_bytes=56 * 2**20
+        ),
+    )(*ins)
+
+
+def lane(start, size):
+    return pl.ds(pl.multiple_of(start, 128), size)
+
+
+def row(start, size):
+    return pl.ds(pl.multiple_of(start, 64), size)
+
+
+def fetch_body(groups, ranks, *refs):
+    (tok, cot, gains, q, k, v, o, gate, up, down) = refs[:10]
+    (tok_all, cot_all, gains_all, q_all, k_all, v_all, o_all, gate_all, up_all, down_all) = refs[10:20]
+    send, receive, local = refs[20:]
+    s, h = place()
+    g = s // ranks
+    enter([(s ^ m, h) for m in range(1, groups * ranks)] + [(s, h ^ 1), (s, h ^ 2)])
+    net = Net(send, receive)
+    quarter = tok.shape[0] // 4
+    width = gains.shape[1]
+
+    def source(ref, group, by_row):
+        if by_row:
+            size = ref.shape[0] // groups
+            return ref.at[pl.ds(pl.multiple_of(group * size, 128), size), :]
+        size = ref.shape[1] // groups
+        return ref.at[:, lane(group * size, size)]
+
+    def target(ref, shard, by_row):
+        if by_row:
+            return ref.at[:, lane(shard * width, width)]
+        return ref.at[shard]
+
+    mine = []
+
+    def keep(a, b):
+        copy = pltpu.make_async_copy(a, b, local.at[len(mine)])
+        copy.start()
+        mine.append(copy)
+
+    gains_moves = [
+        net.put(gains, gains_all.at[:, lane(s * width, width)], (s ^ m, h))
+        for m in range(1, groups * ranks)
+    ]
+    keep(gains, gains_all.at[:, lane(s * width, width)])
+    strip = row(h * quarter, quarter)
+    pairs = ((tok, tok_all), (cot, cot_all))
+    row_moves = {
+        (i, m): net.put(a.at[strip], b.at[g, strip], (s ^ (m * ranks), h))
+        for i, (a, b) in enumerate(pairs)
+        for m in range(1, groups)
+    }
+    for a, b in pairs:
+        keep(a, b.at[g])
+    weights = (
+        (q, q_all, False),
+        (k, k_all, False),
+        (v, v_all, False),
+        (o, o_all, True),
+        (gate, gate_all, False),
+        (up, up_all, False),
+        (down, down_all, True),
+    )
+    moves = {}
+    for i, (a, b, by_row) in enumerate(weights):
+        for m in range(1, groups):
+            moves[i, m] = net.put(
+                source(a, g ^ m, by_row), target(b, s, by_row), (s ^ (m * ranks), h)
+            )
+        keep(source(a, g, by_row), target(b, s, by_row))
+    arrivals = []
+    for i, (a, b, by_row) in enumerate(weights):
+        arrivals.append(net.put(source(a, g, by_row), target(b, s, by_row), (s ^ 1, h)))
+    across = {}
+    for i, (a, b) in enumerate(pairs):
+        for m in range(1, groups):
+            row_moves[i, m].wait_recv()
+            block = b.at[g ^ m, strip]
+            across[i, m] = net.put(block, block, (s, h ^ 2))
+            arrivals.append(net.put(block, block, (s, h ^ 1)))
+    other = row((h ^ 2) * quarter, quarter)
+    for i, (a, b) in enumerate(pairs):
+        for m in range(1, groups):
+            across[i, m].wait_recv()
+            block = b.at[g ^ m, other]
+            arrivals.append(net.put(block, block, (s, h ^ 1)))
+    for i, (a, b, by_row) in enumerate(weights):
+        for m in range(1, groups):
+            moves[i, m].wait_recv()
+            block = target(b, s ^ (m * ranks), by_row)
+            arrivals.append(net.put(block, block, (s ^ 1, h)))
+    for copy in gains_moves + arrivals:
+        copy.wait_recv()
+    net.sent()
+    for copy in mine:
+        copy.wait()
+
+
+def spread_body(groups, ranks, own, out, send, receive, local):
+    s, h = place()
+    g = s // ranks
+    enter([(s ^ (m * ranks), h) for m in range(1, groups)] + [(s, h ^ 1), (s, h ^ 2)])
+    net = Net(send, receive)
+    quarter = own.shape[0]
+    strip, other = row(h * quarter, quarter), row((h ^ 2) * quarter, quarter)
+    keep = pltpu.make_async_copy(own, out.at[g, strip], local.at[0])
+    keep.start()
+    along = {
+        m: net.put(own, out.at[g, strip], (s ^ (m * ranks), h)) for m in range(1, groups)
+    }
+    across = {0: net.put(own, out.at[g, strip], (s, h ^ 2))}
+    last = [net.put(own, out.at[g, strip], (s, h ^ 1))]
+    for m in range(1, groups):
+        along[m].wait_recv()
+        block = out.at[g ^ m, strip]
+        across[m] = net.put(block, block, (s, h ^ 2))
+        last.append(net.put(block, block, (s, h ^ 1)))
+    for m in range(groups):
+        across[m].wait_recv()
+        block = out.at[g ^ m, other]
+        last.append(net.put(block, block, (s, h ^ 1)))
+    for copy in last:
+        copy.wait_recv()
+    net.sent()
+    keep.wait()
+
+
+def collect_body(
+    groups, ranks, part, out, near, mid, across_send, across_in, along_send, along_in, send, receive, local
+):
+    s, h = place()
+    g = s // ranks
+    enter([(s ^ (m * ranks), h) for m in range(1, groups)] + [(s, h ^ 1), (s, h ^ 2)])
+    net = Net(send, receive)
+    order = list(range(groups - 1, -1, -1))
+    first = {}
+    for m in order:
+        d = g ^ m
+        first[m] = (
+            net.put(part.at[d, h ^ 3], near.at[d, 1], (s, h ^ 1)),
+            net.put(part.at[d, h ^ 1], near.at[d, 0], (s, h ^ 1)),
+        )
+    second, third = {}, {}
+    for m in order:
+        d = g ^ m
+        first[m][0].wait_recv()
+        across_send[d] = (part[d, h ^ 2].astype(F32) + near[d, 1].astype(F32)).astype(BF16)
+        second[m] = net.put(across_send.at[d], across_in.at[d], (s, h ^ 2))
+    for m in order:
+        d = g ^ m
+        first[m][1].wait_recv()
+        mid[...] = part[d, h].astype(F32) + near[d, 0].astype(F32)
+        second[m].wait_recv()
+        total = mid[...] + across_in[d].astype(F32)
+        if m:
+            along_send[m - 1] = total.astype(BF16)
+            third[m] = net.put(along_send.at[m - 1], along_in.at[m - 1], (s ^ (m * ranks), h))
+        else:
+            out[...] = total
+    for m in order[:-1]:
+        third[m].wait_recv()
+        out[...] += along_in[m - 1].astype(F32)
+    net.sent()
+
+
+def swap_body(ranks, own, out, send, receive, local):
+    s, h = place()
+    r = s % ranks
+    enter([(s ^ 1, h)])
+    net = Net(send, receive)
+    keep = pltpu.make_async_copy(own, out.at[:, r], local.at[0])
+    keep.start()
+    net.put(own, out.at[:, r], (s ^ 1, h)).wait_recv()
+    net.sent()
+    keep.wait()
+
+
+def hand_body(ranks, own, out, send, receive, local):
+    s, h = place()
+    r = s % ranks
+    enter([(s ^ 1, h)])
+    net = Net(send, receive)
+    net.put(own.at[:, r ^ 1], out, (s ^ 1, h)).wait_recv()
+    net.sent()
+
+
+def finish_body(groups, ranks, *refs):
+    parts, (result, rows_grad, gains) = refs[:7], refs[7:10]
+    outs, (result_all, rows_grad_all, gains_out) = refs[10:17], refs[17:20]
+    peers, sums, (gains_in, gains_mid, gains_near) = refs[20:27], refs[27:34], refs[34:37]
+    send, receive, local = refs[37:]
+    s, h = place()
+    g, r = s // ranks, s % ranks
+    size = groups * ranks
+    enter([(s ^ m, h) for m in range(1, size)] + [(s, h ^ m) for m in range(1, 4)])
+    net = Net(send, receive)
+    quarter = result.shape[0]
+    width = gains_out.shape[1]
+    strip = row(h * quarter, quarter)
+    to_peer = []
+    for i, part in enumerate(parts):
+        to_peer.append(net.put(part.at[:, r ^ 1], peers[i], (s ^ 1, h)))
+    rest = []
+    for a, b in ((result, result_all), (rows_grad, rows_grad_all)):
+        b[strip, :] = a[...]
+        for m in range(1, 4):
+            rest.append(net.put(a, b.at[strip], (s, h ^ m)))
+    gains_moves = [
+        net.put(gains.at[:, lane((s ^ m) * width, width)], gains_in.at[m - 1], (s ^ m, h))
+        for m in range(1, size)
+    ]
+
+    def target(i, group):
+        if outs[i].shape[0] != width:
+            n = outs[i].shape[0] // groups
+            return outs[i].at[pl.ds(pl.multiple_of(group * n, 128), n), :]
+        n = outs[i].shape[1] // groups
+        return outs[i].at[:, lane(group * n, n)]
+
+    for i, part in enumerate(parts):
+        to_peer[i].wait_recv()
+        for m in range(groups - 1, -1, -1):
+            d = g ^ m
+            total = part[d, r].astype(F32) + peers[i][d].astype(F32)
+            sums[i][d] = total.astype(BF16)
+            if m:
+                rest.append(net.put(sums[i].at[d], target(i, g), (s ^ (m * ranks), h)))
+            else:
+                keep = pltpu.make_async_copy(sums[i].at[d], target(i, g), local.at[i])
+                keep.start()
+    total = gains[:, lane(s * width, width)]
+    for m in range(1, size):
+        gains_moves[m - 1].wait_recv()
+        total += gains_in[m - 1]
+    gains_mid[...] = total
+    near = [net.put(gains_mid, gains_near.at[m - 1], (s, h ^ m)) for m in range(1, 4)]
+    for m in range(1, 4):
+        near[m - 1].wait_recv()
+        total += gains_near[m - 1]
+    gains_out[...] = total
+    for copy in rest:
+        copy.wait_recv()
+    net.sent()
+    for i in range(len(parts)):
+        pltpu.make_async_copy(sums[i].at[g], target(i, g), local.at[i]).wait()
+
+
+def rotate(values, cos_table, sin_table):
+    return values * cos_table + jnp.roll(values, HD // 2, axis=1) * sin_table
+
+
+def rows_plan(
+    groups,
+    ranks,
+    tokens,
+    attn_gain,
+    query_weight,
+    key_weight,
+    value_weight,
+    out_weight,
+    mlp_gain,
+    gate_weight,
+    up_weight,
+    down_weight,
+    cotangent,
+):
+    count, depth = tokens.shape
+    shards = groups * ranks
+    quarter = count // 4
+    width = query_weight.shape[0]
+    units = gate_weight.shape[1] // groups
+    total_rows = count * shards
+    here = groups * count
+    s, h = place()
+    r = s % ranks
+    shape = jax.ShapeDtypeStruct
+    bind = functools.partial
+
+    gains = jnp.zeros((8, width), F32)
+    gains = gains.at[0].set(attn_gain.astype(F32)).at[1].set(mlp_gain.astype(F32))
+    ins = (tokens, cotangent, gains, query_weight, key_weight, value_weight, out_weight, gate_weight, up_weight, down_weight)
+    heads = shape((shards, width, HD), BF16)
+    hidden_units = shape((shards, width, units), BF16)
+    outs = (
+        shape((groups, count, depth), BF16),
+        shape((groups, count, depth), BF16),
+        shape((8, depth), F32),
+        heads,
+        heads,
+        heads,
+        shape((HD, depth), BF16),
+        hidden_units,
+        hidden_units,
+        shape((units, depth), BF16),
+    )
+    tok, cot, gains, wq, wk, wv, wo, wg, wu, wd = talk(bind(fetch_body, groups, ranks), ins, outs, [], 1, copies=96)
+    wq, wk, wv = (w.reshape(depth, HD) for w in (wq, wk, wv))
+    wg, wu = (w.reshape(depth, units) for w in (wg, wu))
+    tok, cot = tok.reshape(here, depth), cot.reshape(here, depth)
+    gain_one, gain_two = gains[0], gains[1]
+
+    def collect(part, ident):
+        part = part.astype(BF16).reshape(groups, 4, quarter, depth)
+        piece = (quarter, depth)
+        return talk(
+            bind(collect_body, groups, ranks),
+            (part,),
+            [shape(piece, F32)],
+            [
+                pltpu.VMEM((groups, 2, *piece), BF16),
+                pltpu.VMEM(piece, F32),
+                pltpu.VMEM((groups, *piece), BF16),
+                pltpu.VMEM((groups, *piece), BF16),
+                pltpu.VMEM((groups - 1, *piece), BF16),
+                pltpu.VMEM((groups - 1, *piece), BF16),
+            ],
+            ident,
+            space=pltpu.VMEM,
+        )[0]
+
+    def spread(own, ident):
+        return talk(
+            bind(spread_body, groups, ranks), (own,), [shape((groups, count, depth), BF16)], [], ident
+        )[0].reshape(here, depth)
+
+    def dot(a, b):
+        return jnp.dot(a, b, preferred_element_type=F32)
+
+    def dot_nt(a, b):
+        return lax.dot_general(a, b, (((1,), (1,)), ((), ())), preferred_element_type=F32)
+
+    def dot_tn(a, b):
+        return lax.dot_general(a, b, (((0,), (0,)), ((), ())), preferred_element_type=F32)
+
+    x = tok.astype(F32)
+    inv = lax.rsqrt(jnp.mean(x * x, axis=1, keepdims=True) + epsilon)
+    normed_one = (x * inv * gain_one).astype(BF16)
+    own_rows = lax.dynamic_slice_in_dim(tokens, h * quarter, quarter, 0).astype(F32)
+    places = (
+        (jnp.arange(groups, dtype=jnp.int32) * ranks + r)[:, None] * count
+        + jnp.arange(count, dtype=jnp.int32)[None, :]
+    ).reshape(here)
+    half = HD // 2
+    frequency = jnp.exp(jnp.arange(half, dtype=F32) * (-math.log(10000.0) / half))
+    angles = places.astype(F32)[:, None] * frequency[None, :]
+    cosines, sines = jnp.cos(angles), jnp.sin(angles)
+    cos_table = jnp.concatenate([cosines, cosines], 1)
+    sin_table = jnp.concatenate([-sines, sines], 1)
+    query = rotate(dot(normed_one, wq), cos_table, sin_table).astype(BF16)
+    key = rotate(dot(normed_one, wk), cos_table, sin_table).astype(BF16)
+    value = dot(normed_one, wv).astype(BF16)
+    both = jnp.concatenate([key, value], 1).reshape(groups, count, 2 * HD)
+    both = talk(bind(swap_body, ranks), (both,), [shape((groups, ranks, count, 2 * HD), BF16)], [], 2)[0]
+    both = both.reshape(total_rows, 2 * HD)
+    keys, values = both[:, :HD], both[:, HD:]
+    score_scale = 1.0 / math.sqrt(HD)
+    score_shift = math.log(total_rows)
+    visible = jnp.arange(total_rows, dtype=jnp.int32)[None, :] <= places[:, None]
+    weight = jnp.where(visible, jax.nn.sigmoid(dot_nt(query, keys) * score_scale - score_shift), 0.0)
+    weight_low = weight.astype(BF16)
+    mix = dot(weight_low, values).astype(BF16)
+    hidden = own_rows + collect(dot(mix, wo), 3)
+    inv_two = lax.rsqrt(jnp.mean(hidden * hidden, axis=1, keepdims=True) + epsilon)
+    normed_two = spread((hidden * inv_two * gain_two).astype(BF16), 4)
+    gate = dot(normed_two, wg)
+    up = dot(normed_two, wu)
+    sig = jax.nn.sigmoid(gate)
+    act = gate * sig
+    mixed = (act * up).astype(BF16)
+    result = (hidden + collect(dot(mixed, wd), 5)).astype(BF16)
+    grad_down = dot_tn(mixed, cot)
+    dmixed = dot_nt(cot, wd)
+    dgate = (dmixed * up * sig * (1.0 + gate * (1.0 - sig))).astype(BF16)
+    dup = (dmixed * act).astype(BF16)
+    dnormed_two = collect(dot_nt(dgate, wg) + dot_nt(dup, wu), 6)
+    grad_gate = dot_tn(normed_two, dgate)
+    grad_up = dot_tn(normed_two, dup)
+    own_cot = lax.dynamic_slice_in_dim(cotangent, h * quarter, quarter, 0).astype(F32)
+    back, grad_gain_two = norm_back(hidden, inv_two, gain_two, dnormed_two)
+    dhidden = own_cot + back
+    dhidden_low = spread(dhidden.astype(BF16), 7)
+    grad_out = dot_tn(mix, dhidden_low)
+    dmix = dot_nt(dhidden_low, wo).astype(BF16)
+    dweight = dot_nt(dmix, values)
+    dscore = (dweight * weight * (1.0 - weight)).astype(BF16)
+    dvalues = dot_tn(weight_low, dmix)
+    dkeys = dot_tn(dscore, query) * score_scale
+    dquery = dot(dscore, keys) * score_scale
+    both_back = jnp.concatenate([dkeys, dvalues], 1).reshape(groups, ranks, count, 2 * HD)
+    other = talk(
+        bind(hand_body, ranks), (both_back.astype(BF16),), [shape((groups, count, 2 * HD), BF16)], [], 8
+    )[0]
+    both_back = lax.dynamic_index_in_dim(both_back, r, 1, keepdims=False) + other.astype(F32)
+    both_back = both_back.reshape(here, 2 * HD)
+    dquery_pre = rotate(dquery, cos_table, -sin_table).astype(BF16)
+    dkey_pre = rotate(both_back[:, :HD], cos_table, -sin_table).astype(BF16)
+    dvalue = both_back[:, HD:].astype(BF16)
+    dnormed_one = collect(
+        dot_nt(dquery_pre, wq) + dot_nt(dkey_pre, wk) + dot_nt(dvalue, wv), 9
+    )
+    grad_query = dot_tn(normed_one, dquery_pre)
+    grad_key = dot_tn(normed_one, dkey_pre)
+    grad_value = dot_tn(normed_one, dvalue)
+    own_inv = lax.rsqrt(jnp.mean(own_rows * own_rows, axis=1, keepdims=True) + epsilon)
+    back, grad_gain_one = norm_back(own_rows, own_inv, gain_one, dnormed_one)
+    rows_grad = (dhidden + back).astype(BF16)
+    by_row = [
+        w.astype(BF16).reshape(groups, ranks, width, w.shape[1])
+        for w in (grad_query, grad_key, grad_value, grad_gate, grad_up)
+    ]
+    by_column = [
+        w.astype(BF16).reshape(w.shape[0], groups, ranks, width).transpose(1, 2, 0, 3)
+        for w in (grad_out, grad_down)
+    ]
+    parts = (*by_row[:3], by_column[0], *by_row[3:], by_column[1])
+    gain_grads = jnp.zeros((8, depth), F32).at[0].set(grad_gain_one).at[1].set(grad_gain_two)
+    owners = (query_weight, key_weight, value_weight, out_weight, gate_weight, up_weight, down_weight)
+    rows_all = shape((count, depth), BF16)
+    moved = [pltpu.VMEM((groups, *p.shape[2:]), BF16) for p in parts]
+    *grads, result, rows_grad, gain_grads = talk(
+        bind(finish_body, groups, ranks),
+        (*parts, result, rows_grad, gain_grads),
+        [*(shape(w.shape, BF16) for w in owners), rows_all, rows_all, shape((8, width), F32)],
+        [
+            *moved,
+            *moved,
+            pltpu.VMEM((shards - 1, 8, width), F32),
+            pltpu.VMEM((8, width), F32),
+            pltpu.VMEM((3, 8, width), F32),
+        ],
+        10,
+        space=pltpu.VMEM,
+        copies=64,
+    )
+    grads = [w.astype(F32) for w in grads]
+    return (result, rows_grad, gain_grads[0], *grads[:4], gain_grads[1], *grads[4:])
+
+
+def on_device(tokens, attn_gain, query_weight, *rest):
+    groups = query_weight.shape[1] // HD
+    ranks = lax.axis_size("seq") // groups
+    fits = lax.axis_size("head") == 4 and groups == 4 and ranks == 2 and query_weight.shape[0] % 128 == 0
+    plan = functools.partial(rows_plan, groups, ranks) if fits else gathered_weights
+    return plan(tokens, attn_gain, query_weight, *rest)
+
+
 def solution(mesh):
     in_specs = (
         P("seq", None),

time: 2390 us -> 721 us (0.30)
  waiting for transfers between devices: 2070 us -> 0 us
  Pallas kernels: 0 us -> 555 us
  blocking collectives: 80.6 us -> 0 us
  matrix products: 129 us -> 93.6 us
  local copies, waits for them, and re-layouts: 56 us -> 23.7 us
    reduce_scatter x9 -> x0, waiting for transfers between devices: 1360 us -> none  [the longest x1 287 us: on_device(): lax.psum_scatter(grad_gate, 'seq', scatter_dimension=0, tiled=True)]
    all_gather x9 -> x0, waiting for transfers between devices: 600 us -> none  [the longest x1 124 us: on_device(): lax.all_gather(gate_weight, 'seq', axis=0, tiled=True)]
    pallas_call x0 -> x10, Pallas kernels: none -> 555 us  [talk(): pl.pallas_call(body, out_shape=outs, in_specs=[whole(space)] * len(ins),...]
    psum x4 -> x0, waiting for transfers between devices: 111 us -> none  [the longest x1 41.9 us: on_device(): lax.psum(jnp.einsum('tf,kf->tk', dgate, gate_back, preferred_element_type...]
    all_gather x2 -> x0, blocking collectives: 41.7 us -> none  [the longest x1 22.3 us: on_device(): lax.all_gather(attn_gain, 'seq', axis=0, tiled=True)]
    unnamed x1 -> x0, blocking collectives: 38.8 us -> none
    dot_general x43 -> x27, matrix products: 123 us -> 93.6 us  [the longest x9 37.1 us: dot_tn(): lax.dot_general(a, b, (((0,), (0,)), ((), ())), preferred_element_type=F32)]
  transfers between devices with their start and end apart: 22 -> 0, of which waited for: 22 -> 0; matrix products, arithmetic and copies ran while one was open for 5% -> 0% of each run, Pallas kernels for 0% -> 0%
where the time goes in v1:
time: 721 us; the launch traced here: 712 us
  Pallas kernels  555 us (77%)
  matrix products  93.6 us (13%)
  other arithmetic  37.8 us (5%)
  local copies, waits for them, and re-layouts  23.7 us (3%)
    pallas_call x10, Pallas kernels, talk(): pl.pallas_call(body, out_shape=outs, in_specs=[whole(space)] * len(ins),...  555 us
    dot_general x9, matrix products, dot_tn(): lax.dot_general(a, b, (((0,), (0,)), ((), ())), preferred_element_type=F32)  37.1 us
    dot_general x9, matrix products, dot_nt(): lax.dot_general(a, b, (((1,), (1,)), ((), ())), preferred_element_type=F32)  30.5 us
    dot_general x9, matrix products, dot(): return jnp.dot(a, b, preferred_element_type=F32)  26 us

profile of v1, /device:TPU:0, one launch (start us, length us, event | category | flops | bytes accessed | tf_op | source)
XLA Modules:
  0.0 711.5 jit_solution(1651992683711315519)
XLA Ops:
  3.2 163.3 %shard_map.194 = (bf16[4,256,2048]{2,1,0:T(8,128)(2,1)}, bf16[4,256,2048]{2,1,0:T(8,128)(2,1)}, f32[8,2048]{1,0:T(8,128)}, bf16[8,256,128]{2,1,0:T(8,128)(2,1)},...) custom-call(bf16[256,2048]{1,0:T(8,128)(2,1)} %refs_0_.1, ...), custom_call_target="tpu_custom_call" | custom-call | tf_op jit(solution)/shard_map/pallas_call | solution.py:331
  167.5 3.3 multiply_reduce_fusion
  170.9 5.4 fusion.45
  176.3 3.0 fusion.1
  180.5 1.5 convolution_convert_fusion.10
  182.0 1.5 fusion.44
  183.5 1.5 fusion.43
  186.5 20.1 %shard_map.195 = bf16[4,2,256,256]{3,2,1,0:T(8,128)(2,1)} custom-call(bf16[4,256,256]{2,1,0:T(8,128)(2,1)} %bitcast.128), custom_call_target="tpu_custom_call" | custom-call | tf_op jit(solution)/shard_map/pallas_call | solution.py:331
  206.6 4.4 divide_select_fusion
  212.3 2.0 copy-done
  214.3 3.2 convolution_convert_fusion.1
  217.5 38.3 %shard_map.196 = f32[64,2048]{1,0:T(8,128)} custom-call(bf16[4,4,64,2048]{3,2,1,0:T(8,128)(2,1)} %bitcast.96), custom_call_target="tpu_custom_call" | custom-call | tf_op jit(solution)/shard_map/pallas_call | solution.py:331
  258.1 36.9 %shard_map.197 = bf16[4,256,2048]{2,1,0:T(8,128)(2,1)} custom-call(bf16[64,2048]{1,0:T(8,128)(2,1)} %multiply_convert_fusion.5.own), custom_call_target="tpu_custom_call" | custom-call | tf_op jit(solution)/shard_map/pallas_call | solution.py:331
  295.0 4.7 fusion.46
  299.7 4.5 multiply_convert_fusion.2
  305.2 13.1 %convolution_convert_fusion.2 = bf16[512,2048]{1,0:T(8,128)(2,1)} fusion(bf16[1024,512]{1,0:T(8,128)(2,1)S(1)} %get-tuple-element.107, bf16[1024,2048]{1,0:T(8,128)(2,1)S(1)} %bitcast.148), kind=kOutput, calls=%fused_computation.12 | convolution fusion | flops 2148532224 | bytes 7340032 | tf_op jit(solution)/shard_map/dot_general | solution.py:678
  318.3 2.9 copy.34
  321.2 2.4 copy.35
  323.6 6.3 convolution_convert_fusion
  329.9 40.2 %shard_map.201 = f32[64,2048]{1,0:T(8,128)} custom-call(bf16[4,4,64,2048]{3,2,1,0:T(8,128)(2,1)} %bitcast.113), custom_call_target="tpu_custom_call" | custom-call | tf_op jit(solution)/shard_map/pallas_call | solution.py:331
  370.1 3.7 convolution_convert_fusion.4
  373.8 3.7 convolution_convert_fusion.3
  377.5 2.4 fusion.47
  379.9 4.3 add_convert_fusion.1
  384.2 37.6 %shard_map.198 = f32[64,2048]{1,0:T(8,128)} custom-call(bf16[4,4,64,2048]{3,2,1,0:T(8,128)(2,1)} %bitcast.112), custom_call_target="tpu_custom_call" | custom-call | tf_op jit(solution)/shard_map/pallas_call | solution.py:331
  421.8 2.0 multiply_reduce_fusion.1
  423.9 2.2 fusion.36
  426.1 37.5 %shard_map.199 = bf16[4,256,2048]{2,1,0:T(8,128)(2,1)} custom-call(bf16[64,2048]{1,0:T(8,128)(2,1)} %get-tuple-element.103.own), custom_call_target="tpu_custom_call" | custom-call | tf_op jit(solution)/shard_map/pallas_call | solution.py:331
  463.6 3.6 convolution_convert_fusion.9
  469.3 4.2 fusion.3
  473.5 4.7 multiply_convert_fusion
  482.0 2.2 copy.28
  486.1 15.9 %shard_map.200 = bf16[4,256,256]{2,1,0:T(8,128)(2,1)} custom-call(bf16[4,2,256,256]{3,2,1,0:T(8,128)(2,1)} %convert_element_type.170.own), custom_call_target="tpu_custom_call" | custom-call | tf_op jit(solution)/shard_map/pallas_call | solution.py:331
  503.4 4.4 convolution_convert_fusion.6
  508.8 1.9 copy.37
  511.6 1.6 fusion.29
  513.2 4.3 convolution_convert_fusion.7
  517.6 2.1 convolution_convert_fusion.8
  522.3 3.2 add_convert_fusion
  525.6 39.1 %shard_map.202 = f32[64,2048]{1,0:T(8,128)} custom-call(bf16[4,4,64,2048]{3,2,1,0:T(8,128)(2,1)} %bitcast.99), custom_call_target="tpu_custom_call" | custom-call | tf_op jit(solution)/shard_map/pallas_call | solution.py:331
  566.0 2.0 fusion.14.refs_8_
  568.9 125.7 %shard_map.203 = (bf16[256,512]{1,0:T(8,128)(2,1)}, bf16[256,512]{1,0:T(8,128)(2,1)}, bf16[256,512]{1,0:T(8,128)(2,1)}, bf16[512,256]{1,0:T(8,128)(2,1)}, bf16[2...) custom-call(bf16[4,2,256,128]{3,2,1,0:T(8,128)(2,1)} %bitcast.131, ...), custom_call_target="tpu_custom_call" | custom-call | tf_op jit(solution)/shard_map/pallas_call | solution.py:331
  696.0 1.8 convert_element_type.184
  697.8 1.9 convert_element_type.185
  699.7 1.8 convert_element_type.186
  701.5 1.8 convert_element_type.187
  703.2 2.9 convert_element_type.188
  706.1 1.6 convert_element_type.189
  (134 shorter events, 31.1 us)
Async XLA Ops:
  2.1 1.0 copy-start.32
  3.1 182.0 %copy-start.11 = (f32[1024,64]{0,1:T(8,128)}, f32[1024,64]{0,1:T(8,128)S(1)}, u32[]{:S(2)}) copy-start(f32[1024,64]{0,1:T(8,128)S(1)} %get-tuple-element.129) | copy-start | bytes 786436
  3.2 182.0 %copy-start.13 = (f32[1024,64]{0,1:T(8,128)}, f32[1024,64]{0,1:T(8,128)S(1)}, u32[]{:S(2)}) copy-start(f32[1024,64]{0,1:T(8,128)S(1)} %get-tuple-element.130) | copy-start | bytes 786436
  166.5 4.4 copy-start.33
  170.9 5.4 copy-start.1
  179.4 1.0 copy-start.15
  180.4 1.6 copy-start.17
  180.4 3.1 copy-start.19
  185.5 25.5 %copy-start.27 = (bf16[1024,128]{0,1:T(8,128)(2,1)}, bf16[1024,128]{0,1:T(8,128)(2,1)S(1)}, u32[]{:S(2)}) copy-start(bf16[1024,128]{0,1:T(8,128)(2,1)S(1)} %get-tuple-element.116) | copy-start | bytes 786436
  206.6 4.4 copy-start.4
  211.0 3.3 copy-start
  211.0 3.3 copy-start.29
  255.8 39.2 %copy-start.37 = (bf16[8,256,512]{2,1,0:T(8,128)(2,1)S(1)}, bf16[8,256,512]{2,1,0:T(8,128)(2,1)}, u32[]{:S(2)}) copy-start(bf16[8,256,512]{2,1,0:T(8,128)(2,1)} %get-tuple-element.88) | copy-start | bytes 6291460
  295.0 4.7 copy-start.8
  295.0 4.7 copy-start.35
  295.0 4.7 copy-start.43
  299.7 5.5 copy-start.34
  304.3 1.0 copy-start.42
  323.6 46.5 %copy-start.40 = (bf16[1024,512]{1,0:T(8,128)(2,1)S(1)}, bf16[1024,512]{1,0:T(8,128)(2,1)}, u32[]{:S(2)}) copy-start(bf16[1024,512]{1,0:T(8,128)(2,1)} %get-tuple-element.108) | copy-start | bytes 3145732
  329.9 40.2 %copy-start.9 = (bf16[4,256,2048]{2,1,0:T(8,128)(2,1)S(1)}, bf16[4,256,2048]{2,1,0:T(8,128)(2,1)}, u32[]{:S(2)}) copy-start(bf16[4,256,2048]{2,1,0:T(8,128)(2,1)} %shard_map.197) | copy-start | bytes 12582916
  370.1 3.7 copy-start.39
  373.8 3.7 copy-start.38
  373.8 3.7 copy-start.41
  377.5 2.4 copy-start.36
  384.2 37.6 %copy-start.21 = (f32[64,2048]{1,0:T(8,128)S(1)}, f32[64,2048]{1,0:T(8,128)}, u32[]{:S(2)}) copy-start(f32[64,2048]{1,0:T(8,128)} %shard_map.201) | copy-start | bytes 1572868
  421.8 41.8 %copy-start.30 = (bf16[128,2048]{1,0:T(8,128)(2,1)S(1)}, bf16[128,2048]{1,0:T(8,128)(2,1)}, u32[]{:S(2)}) copy-start(bf16[128,2048]{1,0:T(8,128)(2,1)} %get-tuple-element.84) | copy-start | bytes 1572868
  463.6 3.6 copy-start.3
  469.3 4.2 copy-start.5
  478.2 1.5 copy-start.28
  479.7 4.4 copy-start.6
  503.4 8.2 %copy-start.7 = (f32[1024,128]{0,1:T(8,128)S(1)}, f32[1024,128]{0,1:T(8,128)}, u32[]{:S(2)}) copy-start(f32[1024,128]{0,1:T(8,128)} %copy-done.6) | copy-start | bytes 1572868
  503.4 8.2 %copy-start.12 = (f32[1024,64]{0,1:T(8,128)S(1)}, f32[1024,64]{0,1:T(8,128)}, u32[]{:S(2)}) copy-start(f32[1024,64]{0,1:T(8,128)} %copy-done.11) | copy-start | bytes 786436
  503.4 8.2 %copy-start.14 = (f32[1024,64]{0,1:T(8,128)S(1)}, f32[1024,64]{0,1:T(8,128)}, u32[]{:S(2)}) copy-start(f32[1024,64]{0,1:T(8,128)} %copy-done.13) | copy-start | bytes 786436
  511.6 6.0 copy-start.2
  513.2 6.5 copy-start.20
  519.7 1.3 copy-start.18
  521.0 1.3 copy-start.16
  525.6 39.2 %copy-start.10 = (bf16[256,2048]{1,0:T(8,128)(2,1)S(1)}, bf16[256,2048]{1,0:T(8,128)(2,1)}, u32[]{:S(2)}) copy-start(bf16[256,2048]{1,0:T(8,128)(2,1)} %refs_0_.1) | copy-start | bytes 3145732
  525.6 40.5 %copy-start.22 = (f32[64,2048]{1,0:T(8,128)S(1)}, f32[64,2048]{1,0:T(8,128)}, u32[]{:S(2)}) copy-start(f32[64,2048]{1,0:T(8,128)} %get-tuple-element.104) | copy-start | bytes 1572868
  568.2 0.6 copy-start.31
  694.6 11.5 %copy-start.24 = (bf16[256,2048]{1,0:T(8,128)(2,1)S(1)}, bf16[256,2048]{1,0:T(8,128)(2,1)}, u32[]{:S(2)}) copy-start(bf16[256,2048]{1,0:T(8,128)(2,1)} %get-tuple-element.97) | copy-start | bytes 3145732
  697.8 9.9 %copy-start.23 = (bf16[2048,256]{1,0:T(8,128)(2,1)S(1)}, bf16[2048,256]{1,0:T(8,128)(2,1)}, u32[]{:S(2)}) copy-start(bf16[2048,256]{1,0:T(8,128)(2,1)} %get-tuple-element.98) | copy-start | bytes 3145732
  703.2 5.9 copy-start.26
  706.1 4.0 copy-start.25

commit v2 on v0

--- a/solution.py
+++ b/solution.py
@@ -1,15 +1,22 @@
+import functools
 import math
 
 import jax
 import jax.numpy as jnp
 from jax import lax
+from jax.experimental import pallas as pl
+from jax.experimental.pallas import tpu as pltpu
 from jax.sharding import PartitionSpec as P
+
+MESH = pl.DeviceIdType.MESH
+F32, BF16 = jnp.float32, jnp.bfloat16
 
 HD = 128
 
 
 epsilon = 1e-05
 block_limit = 512
+VMEM_LIMIT = 63 * 2**20
 
 
 def tables(offset, length, half_width):
@@ -50,7 +57,7 @@
     return (value_grad, gain_grad)
 
 
-def on_device(
+def gathered_weights(
     tokens,
     attn_gain,
     query_weight,
@@ -283,6 +290,780 @@
     )
 
 
+class Net:
+    def __init__(self, send, receive):
+        self.send, self.receive, self.copies, self.done = send, receive, [], set()
+
+    def put(self, source, target, device):
+        i = len(self.copies)
+        copy = pltpu.make_async_remote_copy(
+            src_ref=source,
+            dst_ref=target,
+            send_sem=self.send.at[i],
+            recv_sem=self.receive.at[i],
+            device_id=device,
+            device_id_type=MESH,
+        )
+        copy.start()
+        self.copies.append(copy)
+        return copy
+
+    def sent(self, copies=None):
+        for copy in self.copies if copies is None else copies:
+            if id(copy) not in self.done:
+                self.done.add(id(copy))
+                copy.wait_send()
+
+
+class Keep:
+    def __init__(self, sems):
+        self.sems, self.count = sems, 0
+
+    def put(self, source, target):
+        copy = pltpu.make_async_copy(source, target, self.sems.at[self.count])
+        self.count += 1
+        copy.start()
+        return copy
+
+
+class Where:
+    def __init__(self, groups, ranks):
+        self.s, self.h = lax.axis_index("seq"), lax.axis_index("head")
+        self.g, self.r = self.s // ranks, self.s % ranks
+        self.groups, self.ranks = groups, ranks
+
+    def along(self, m):
+        return (self.s ^ (m * self.ranks), self.h)
+
+    def beside(self):
+        return (self.s ^ 1, self.h)
+
+    def across(self):
+        return (self.s, self.h ^ 2)
+
+    def near(self):
+        return (self.s, self.h ^ 1)
+
+
+def lane(start, size):
+    return pl.ds(pl.multiple_of(start, 128), size)
+
+
+def row(start, size):
+    return pl.ds(pl.multiple_of(start, size), size)
+
+
+class Spread:
+    def __init__(self, net, at, buffer, quarter, shared):
+        self.net, self.at, self.buffer, self.quarter, self.shared = net, at, buffer, quarter, shared
+        self.z, self.x, self.c, self.d = {}, {}, {}, {}
+
+    def block(self, m, k):
+        at = self.at
+        return self.buffer.at[row(((at.g ^ m) * 4 + (at.h ^ k)) * self.quarter, self.quarter), :]
+
+    def pass_on(self, m, source=None):
+        block = self.block(m, 0)
+        source = block if source is None else source
+        self.x[m] = self.net.put(source, block, self.at.across())
+        self.c[m] = self.net.put(source, block, self.at.near())
+
+    def start(self, own):
+        block = self.block(0, 0)
+        self.z[2] = self.net.put(own, block, self.at.along(2))
+        self.z[1] = self.net.put(own, block, self.at.along(1))
+        if not self.shared:
+            self.pass_on(0, own)
+
+    def arrive(self, m):
+        self.z[m].wait_recv()
+        if m == 2:
+            block = self.block(2, 0)
+            self.z[3] = self.net.put(block, block, self.at.along(1))
+        self.pass_on(m)
+
+    def second(self, m):
+        self.x[m].wait_recv()
+        block = self.block(m, 2)
+        self.d[m] = self.net.put(block, block, self.at.near())
+
+    def ready(self, m):
+        if m or not self.shared:
+            self.c[m].wait_recv()
+            self.d[m].wait_recv()
+
+    def sent(self, m):
+        if m or not self.shared:
+            self.net.sent([self.x[m], self.c[m], self.d[m]])
+        if m == 2:
+            self.net.sent([self.z[3]])
+
+
+class Collect:
+    def __init__(self, net, at, refs, quarter):
+        self.net, self.at, self.quarter = net, at, quarter
+        self.part, self.near, self.xin, self.zin = refs
+        self.a, self.b, self.z = {}, {}, {}
+        self.own = None
+
+    def rows(self, m, k):
+        at = self.at
+        return row(((at.g ^ m) * 4 + (at.h ^ k)) * self.quarter, self.quarter)
+
+    def first(self, m):
+        d, at = self.at.g ^ m, self.at
+        self.a[m] = (
+            self.net.put(self.part.at[self.rows(m, 3), :], self.near.at[d, 1], at.near()),
+            self.net.put(self.part.at[self.rows(m, 1), :], self.near.at[d, 0], at.near()),
+        )
+
+    def second(self, m):
+        d = self.at.g ^ m
+        rows = self.rows(m, 2)
+        self.a[m][0].wait_recv()
+        self.part[rows, :] = (self.part[rows, :].astype(F32) + self.near[d, 1].astype(F32)).astype(BF16)
+        self.b[m] = self.net.put(self.part.at[rows, :], self.xin.at[d], self.at.across())
+
+    def third(self, m):
+        d = self.at.g ^ m
+        rows = self.rows(m, 0)
+        self.a[m][1].wait_recv()
+        self.b[m].wait_recv()
+        total = self.part[rows, :].astype(F32) + self.near[d, 0].astype(F32) + self.xin[d].astype(F32)
+        if m == 0:
+            return total
+        if m == 2:
+            self.z[3].wait_recv()
+            total += self.zin[0].astype(F32)
+        self.part[rows, :] = total.astype(BF16)
+        slot, hop = {3: (0, 1), 2: (2, 2), 1: (1, 1)}[m]
+        self.z[m] = self.net.put(self.part.at[rows, :], self.zin.at[slot], self.at.along(hop))
+        return None
+
+    def last(self):
+        total = self.third(0)
+        self.z[1].wait_recv()
+        total += self.zin[1].astype(F32)
+        self.z[2].wait_recv()
+        return total + self.zin[2].astype(F32)
+
+    def sent(self):
+        for m in range(4):
+            self.net.sent(list(self.a[m]) + [self.b[m]] + ([self.z[m]] if m else []))
+
+
+class Turn:
+    def __init__(self, net, keep, at, sources, buffer, block, views):
+        self.net, self.keep, self.at = net, keep, at
+        self.sources, self.buffer, self.block, self.views = sources, buffer, block, views
+        self.z, self.y, self.own = {}, [], []
+
+    def start(self, m, i):
+        at = self.at
+        copy = self.net.put(self.sources(i, at.g ^ m), self.views(i, at.s), at.along(m))
+        self.z.setdefault(m, []).append(copy)
+
+    def mine(self, i):
+        at = self.at
+        source = self.sources(i, at.g)
+        self.own.append(self.keep.put(source, self.views(i, at.s)))
+        self.y.append(self.net.put(source, self.views(i, at.s), at.beside()))
+
+    def pass_on(self, m):
+        at = self.at
+        for copy in self.z[m]:
+            copy.wait_recv()
+        block = self.block(at.s ^ (m * at.ranks))
+        self.y.append(self.net.put(block, block, at.beside()))
+
+    def ready(self):
+        for copy in self.own:
+            copy.wait()
+        for copy in self.y:
+            copy.wait_recv()
+
+    def sent(self):
+        self.net.sent(self.y)
+
+
+def dot(a, b):
+    return jnp.dot(a, b, preferred_element_type=F32)
+
+
+def dot_nt(a, b):
+    return lax.dot_general(a, b, (((1,), (1,)), ((), ())), preferred_element_type=F32)
+
+
+def dot_tn(a, b):
+    return lax.dot_general(a, b, (((0,), (0,)), ((), ())), preferred_element_type=F32)
+
+
+def turned(values, cos_table, sin_table):
+    return values * cos_table + pltpu.roll(values, HD // 2, 1) * sin_table
+
+
+def mean_square(values):
+    return jnp.mean(values * values, axis=1, keepdims=True)
+
+
+def layer_body(groups, ranks, *refs):
+    (tok, cot, gains, qw, kw, vw, ow, gw, uw, dw, cosines, sines) = refs[:12]
+    (result_out, rows_out, gains_out, q_out, k_out, v_out, o_out, g_out, u_out, d_out) = refs[12:22]
+    (
+        gains_all, rows_one, rows_cot, rows_two, rows_dh, w_qkv, w_o, w_gu, w_d, queries, pairs, mix, dmix, dqkv, accum, pair_send,
+        pair_in, mixed, dgu, dmixed, own_x, hidden, dhidden, part_a, near_a, xin_a, zin_a, part_b, near_b, xin_b, zin_b, in_gu, in_d,
+        in_qkv, in_o, gain_part, gain_in, gain_mid, gain_near, result_own, rows_own, send, receive, local,
+    ) = refs[22:]
+    at = Where(groups, ranks)
+    s, h, g, r = at.s, at.h, at.g, at.r
+    shards = groups * ranks
+    count, depth = tok.shape
+    quarter = count // 4
+    width = gains.shape[1]
+    units = gw.shape[1] // groups
+    total_rows = count * shards
+    score_scale = 1.0 / math.sqrt(HD)
+    score_shift = math.log(total_rows)
+    peers = [(s ^ m, h) for m in range(1, shards)] + [(s, h ^ m) for m in range(1, 4)]
+    barrier = pltpu.get_barrier_semaphore()
+    for peer in peers:
+        pl.semaphore_signal(barrier, inc=1, device_id=peer, device_id_type=MESH)
+    pl.semaphore_wait(barrier, len(peers))
+    net, keep = Net(send, receive), Keep(local)
+
+    def chunk(m):
+        return row((g ^ m) * count, count)
+
+    def shard_rows(shard):
+        return row(shard * width, width)
+
+    def by_column(size):
+        return lambda refs_: lambda i, group: refs_[i].at[:, lane(group * size, size)]
+
+    def by_row(size):
+        return lambda refs_: lambda i, group: refs_[i].at[row(group * size, size), :]
+
+    turn_qkv = Turn(
+        net, keep, at, by_column(HD)((qw, kw, vw)), w_qkv,
+        lambda shard: w_qkv.at[shard_rows(shard), :],
+        lambda i, shard: w_qkv.at[shard_rows(shard), i * HD : (i + 1) * HD],
+    )
+    turn_gu = Turn(
+        net, keep, at, by_column(units)((gw, uw)), w_gu,
+        lambda shard: w_gu.at[shard_rows(shard), :],
+        lambda i, shard: w_gu.at[shard_rows(shard), i * units : (i + 1) * units],
+    )
+    turn_o = Turn(
+        net, keep, at, by_row(HD)((ow,)), w_o,
+        lambda shard: w_o.at[:, lane(shard * width, width)],
+        lambda i, shard: w_o.at[:, lane(shard * width, width)],
+    )
+    turn_d = Turn(
+        net, keep, at, by_row(units)((dw,)), w_d,
+        lambda shard: w_d.at[:, lane(shard * width, width)],
+        lambda i, shard: w_d.at[:, lane(shard * width, width)],
+    )
+
+    gain_slot = gains_all.at[:, lane(s * width, width)]
+    gain_moves = [net.put(gains, gain_slot, (s ^ m, h)) for m in range(1, shards)]
+    gain_own = keep.put(gains, gain_slot)
+    strip = row(h * quarter, quarter)
+    one = Spread(net, at, rows_one, quarter, True)
+    one.start(tok.at[strip, :])
+    own_rows = keep.put(tok, rows_one.at[chunk(0), :])
+    own_strip = keep.put(tok.at[strip, :], own_x)
+    for m in (3, 2, 1):
+        for i in range(3):
+            turn_qkv.start(m, i)
+    for i in range(3):
+        turn_qkv.mine(i)
+    for m in (3, 2, 1):
+        turn_o.start(m, 0)
+    turn_o.mine(0)
+    for m in (3, 2, 1):
+        turn_d.start(m, 0)
+    turn_d.mine(0)
+    grad = Spread(net, at, rows_cot, quarter, True)
+    grad.start(cot.at[strip, :])
+    own_cot = keep.put(cot, rows_cot.at[chunk(0), :])
+    turn_gu.mine(0)
+    turn_gu.mine(1)
+    gain_part[...] = jnp.zeros_like(gain_part)
+
+    gain_own.wait()
+    for copy in gain_moves:
+        copy.wait_recv()
+
+    def norm_one(m):
+        def some(i, carry):
+            rows = row((g ^ m) * count + i * 64, 64)
+            values = rows_one[rows, :].astype(F32)
+            inverse = lax.rsqrt(mean_square(values) + epsilon)
+            rows_one[rows, :] = (values * inverse * gains_all[0:1, :]).astype(BF16)
+            return carry
+
+        lax.fori_loop(0, count // 64, some, 0)
+
+    own_rows.wait()
+    own_strip.wait()
+    norm_one(0)
+    one.arrive(1)
+    one.arrive(2)
+    one.second(1)
+    one.second(2)
+    one.arrive(3)
+    for m in (3, 2, 1):
+        turn_qkv.pass_on(m)
+    one.second(3)
+    for m in (1, 2, 3):
+        one.ready(m)
+        one.sent(m)
+        norm_one(m)
+    for m in (3, 2, 1):
+        turn_o.pass_on(m)
+    turn_qkv.ready()
+    pair_moves = {}
+    for m in (0, 1, 2, 3):
+        rows = chunk(m)
+        heads = dot(rows_one[rows, :], w_qkv[...])
+        cos_part, sin_part = cosines[rows, :], sines[rows, :]
+        queries[rows, :] = turned(heads[:, :HD], cos_part, sin_part).astype(BF16)
+        place = row(((g ^ m) * ranks + r) * count, count)
+        pairs[place, :HD] = turned(heads[:, HD : 2 * HD], cos_part, sin_part).astype(BF16)
+        pairs[place, HD:] = heads[:, 2 * HD :].astype(BF16)
+        pair_moves[m] = net.put(pairs.at[place, :], pairs.at[place, :], at.beside())
+    for m in (0, 1, 2, 3):
+        pair_moves[m].wait_recv()
+    turn_o.ready()
+    span = ranks * count
+
+    def weights_of(m, j, query):
+        keys = pairs[row(j * span, span), :HD]
+        scores = dot_nt(query, keys) * score_scale - score_shift
+        q_place = ((g ^ m) * ranks + r) * count + lax.broadcasted_iota(jnp.int32, (count, span), 0)
+        k_place = j * span + lax.broadcasted_iota(jnp.int32, (count, span), 1)
+        return jnp.where(k_place <= q_place, jax.nn.sigmoid(scores), 0.0)
+
+    def attend(m, collect):
+        rows = chunk(m)
+        query = queries[rows, :]
+
+        def step(j, total):
+            weight = weights_of(m, j, query).astype(BF16)
+            return total + dot(weight, pairs[row(j * span, span), HD:])
+
+        total = lax.fori_loop(0, (g ^ m) + 1, step, jnp.zeros((count, HD), F32))
+        low = total.astype(BF16)
+        mix[rows, :] = low
+        collect.part[rows, :] = dot(low, w_o[...]).astype(BF16)
+
+    first = Collect(net, at, (part_a, near_a, xin_a, zin_a), quarter)
+    attend(3, first)
+    first.first(3)
+    attend(2, first)
+    first.first(2)
+    first.second(3)
+    attend(1, first)
+    first.first(1)
+    first.second(2)
+    first.third(3)
+    turn_gu.start(3, 0)
+    attend(0, first)
+    first.first(0)
+    first.second(1)
+    first.third(2)
+    turn_gu.start(2, 0)
+    first.second(0)
+    first.third(1)
+    turn_gu.start(1, 0)
+    for m in (3, 2, 1):
+        turn_d.pass_on(m)
+    total = first.last()
+    hidden_rows = own_x[...].astype(F32) + total
+    hidden[...] = hidden_rows
+    inverse = lax.rsqrt(mean_square(hidden_rows) + epsilon)
+    two = Spread(net, at, rows_two, quarter, False)
+    mine = row((g * 4 + h) * quarter, quarter)
+    rows_two[mine, :] = (hidden_rows * inverse * gains_all[1:2, :]).astype(BF16)
+    two.start(rows_two.at[mine, :])
+    turn_gu.start(3, 1)
+    turn_gu.start(2, 1)
+    turn_gu.start(1, 1)
+    grad.arrive(1)
+    grad.arrive(2)
+    grad.second(1)
+    two.second(0)
+    two.arrive(1)
+    two.arrive(2)
+    grad.second(2)
+    grad.arrive(3)
+    two.second(1)
+    two.second(2)
+    two.arrive(3)
+    grad.second(3)
+    two.second(3)
+    turn_d.ready()
+    own_cot.wait()
+    for m in (0, 1, 2, 3):
+        grad.ready(m)
+        dmixed[chunk(m), :] = dot_nt(rows_cot[chunk(m), :], w_d[...])
+    for m in (3, 2, 1):
+        turn_gu.pass_on(m)
+    for m in (0, 1, 2, 3):
+        two.ready(m)
+    turn_gu.ready()
+
+    def feed(m, collect):
+        rows = chunk(m)
+        both = dot(rows_two[rows, :], w_gu[...])
+        gate, up = both[:, :units], both[:, units:]
+        sig = jax.nn.sigmoid(gate)
+        act = gate * sig
+        mixed[rows, :] = (act * up).astype(BF16)
+        back = dmixed[rows, :]
+        dgu[rows, :units] = (back * up * sig * (1.0 + gate * (1.0 - sig))).astype(BF16)
+        dgu[rows, units:] = (back * act).astype(BF16)
+        collect.part[rows, :] = dot_nt(dgu[rows, :], w_gu[...]).astype(BF16)
+
+    first.sent()
+    second = Collect(net, at, (part_a, near_a, xin_a, zin_a), quarter)
+    feed(3, second)
+    second.first(3)
+    feed(2, second)
+    second.first(2)
+    second.second(3)
+    feed(1, second)
+    second.first(1)
+    second.second(2)
+    second.third(3)
+    feed(0, second)
+    second.first(0)
+    second.second(1)
+    second.third(2)
+    turn_gu.sent()
+    turn_d.sent()
+
+    moves_gu, moves_d, moves_qkv, moves_o = {}, {}, {}, {}
+
+    def grads_gu(m):
+        d = g ^ m
+        for k in (1, 0):
+            shard = d * ranks + (r ^ k)
+            w_gu[shard_rows(shard), :] = dot_tn(rows_two[:, lane(shard * width, width)], dgu[...]).astype(BF16)
+            if k:
+                moves_gu[m] = net.put(w_gu.at[shard_rows(shard), :], in_gu.at[d], at.beside())
+
+    def grads_d(m):
+        d = g ^ m
+        for k in (1, 0):
+            shard = d * ranks + (r ^ k)
+            columns = lane(shard * width, width)
+            w_d[:, columns] = dot_tn(mixed[...], rows_cot[:, columns]).astype(BF16)
+            if k:
+                moves_d[m] = net.put(w_d.at[:, columns], in_d.at[d], at.beside())
+
+    grads_gu(3)
+    second.second(0)
+    second.third(1)
+    for m in (0, 1, 2, 3):
+        part_b[chunk(m), :] = dot(mixed[chunk(m), :], w_d[...]).astype(BF16)
+    dn_two = second.last()
+    hidden_rows = hidden[...]
+    inverse = lax.rsqrt(mean_square(hidden_rows) + epsilon)
+    scaled = dn_two * gains_all[1:2, :]
+    gain_part[1:2, :] = jnp.sum(dn_two * hidden_rows * inverse, axis=0, keepdims=True)
+    back = inverse * scaled - hidden_rows * (inverse * inverse * inverse) * jnp.mean(
+        scaled * hidden_rows, axis=1, keepdims=True
+    )
+    dh_rows = rows_cot[mine, :].astype(F32) + back
+    dhidden[...] = dh_rows
+    three = Spread(net, at, rows_dh, quarter, False)
+    rows_dh[mine, :] = dh_rows.astype(BF16)
+    three.start(rows_dh.at[mine, :])
+    grads_gu(2)
+    grads_gu(1)
+    three.second(0)
+    three.arrive(1)
+    three.arrive(2)
+    grads_gu(0)
+    final = []
+
+    def give(source, target, m):
+        if m:
+            final.append(net.put(source, target, at.along(m)))
+        else:
+            final_own.append(keep.put(source, target))
+
+    final_own = []
+
+    def sums_gu(m):
+        d = g ^ m
+        rows = shard_rows(d * ranks + r)
+        moves_gu[m].wait_recv()
+        w_gu[rows, :] = (w_gu[rows, :].astype(F32) + in_gu[d].astype(F32)).astype(BF16)
+        for i, out in enumerate((g_out, u_out)):
+            give(w_gu.at[rows, i * units : (i + 1) * units], out.at[:, lane(g * units, units)], m)
+
+    def sums_d(m):
+        d = g ^ m
+        columns = lane((d * ranks + r) * width, width)
+        moves_d[m].wait_recv()
+        w_d[:, columns] = (w_d[:, columns].astype(F32) + in_d[d].astype(F32)).astype(BF16)
+        give(w_d.at[:, columns], d_out.at[row(g * units, units), :], m)
+
+    three.second(1)
+    three.second(2)
+    three.arrive(3)
+    three.second(3)
+    sums_gu(3)
+    for m in (3, 2, 1, 0):
+        grads_d(m)
+    out_sum = Collect(net, at, (part_b, near_b, xin_b, zin_b), quarter)
+    for m in (3, 2, 1, 0):
+        out_sum.first(m)
+    sums_gu(2)
+    sums_gu(1)
+    sums_gu(0)
+
+    accum[...] = jnp.zeros_like(accum)
+
+    def attend_back(m):
+        rows = chunk(m)
+        query = queries[rows, :]
+        dm = dot_nt(rows_dh[rows, :], w_o[...]).astype(BF16)
+        dmix[rows, :] = dm
+
+        def step(j, total):
+            block = row(j * span, span)
+            weight = weights_of(m, j, query)
+            dweight = dot_nt(dm, pairs[block, HD:])
+            dscore = (dweight * weight * (1.0 - weight)).astype(BF16)
+            accum[block, HD:] += dot_tn(weight.astype(BF16), dm)
+            accum[block, :HD] += dot_tn(dscore, query)
+            return total + dot(dscore, pairs[block, :HD])
+
+        total = lax.fori_loop(0, (g ^ m) + 1, step, jnp.zeros((count, HD), F32))
+        dqkv[rows, :HD] = turned(total * score_scale, cosines[rows, :], -sines[rows, :]).astype(BF16)
+
+    for m in (0, 1, 2, 3):
+        three.ready(m)
+        attend_back(m)
+        out_sum.second((3, 2, 1, 0)[m])
+    pair_back = {}
+    for m in (3, 2, 1, 0):
+        d = g ^ m
+        rows = row((d * ranks + (r ^ 1)) * count, count)
+        pair_send[d] = accum[rows, :].astype(BF16)
+        pair_back[m] = net.put(pair_send.at[d], pair_in.at[d], at.beside())
+    turn_o.sent()
+    for k in (1, 0):
+        for m in (3, 2, 1, 0):
+            d = g ^ m
+            columns = lane((d * ranks + (r ^ k)) * width, width)
+            w_o[:, columns] = dot_tn(mix[...], rows_dh[:, columns]).astype(BF16)
+            if k:
+                moves_o[m] = net.put(w_o.at[:, columns], in_o.at[d], at.beside())
+    for m in (3, 2, 1, 0):
+        sums_d(m)
+    out_sum.third(3)
+    out_sum.third(2)
+    out_sum.third(1)
+    second.sent()
+    third = Collect(net, at, (part_a, near_a, xin_a, zin_a), quarter)
+
+    def back_one(m):
+        d = g ^ m
+        rows = chunk(m)
+        pair_back[m].wait_recv()
+        both = accum[row((d * ranks + r) * count, count), :] + pair_in[d].astype(F32)
+        dqkv[rows, HD : 2 * HD] = turned(both[:, :HD] * score_scale, cosines[rows, :], -sines[rows, :]).astype(BF16)
+        dqkv[rows, 2 * HD :] = both[:, HD:].astype(BF16)
+        third.part[rows, :] = dot_nt(dqkv[rows, :], w_qkv[...]).astype(BF16)
+
+    back_one(3)
+    third.first(3)
+    back_one(2)
+    third.first(2)
+    third.second(3)
+    back_one(1)
+    third.first(1)
+    third.second(2)
+    third.third(3)
+    back_one(0)
+    third.first(0)
+    third.second(1)
+    third.third(2)
+    third.second(0)
+    third.third(1)
+    turn_qkv.sent()
+
+    def grads_qkv(m):
+        d = g ^ m
+        for k in (1, 0):
+            shard = d * ranks + (r ^ k)
+            w_qkv[shard_rows(shard), :] = dot_tn(rows_one[:, lane(shard * width, width)], dqkv[...]).astype(BF16)
+            if k:
+                moves_qkv[m] = net.put(w_qkv.at[shard_rows(shard), :], in_qkv.at[d], at.beside())
+
+    for m in (3, 2, 1, 0):
+        grads_qkv(m)
+    for m in (3, 2, 1, 0):
+        d = g ^ m
+        columns = lane((d * ranks + r) * width, width)
+        moves_o[m].wait_recv()
+        w_o[:, columns] = (w_o[:, columns].astype(F32) + in_o[d].astype(F32)).astype(BF16)
+        give(w_o.at[:, columns], o_out.at[row(g * HD, HD), :], m)
+    result_own[...] = (hidden[...] + out_sum.last()).astype(BF16)
+    ends = []
+
+    def share(source, target):
+        place = target.at[strip, :]
+        final_own.append(keep.put(source, place))
+        final.append(net.put(source, place, at.near()))
+        ends.append((net.put(source, place, at.across()), target))
+
+    def relay():
+        copy, target = ends.pop()
+        copy.wait_recv()
+        block = target.at[row((h ^ 2) * quarter, quarter), :]
+        final.append(net.put(block, block, at.near()))
+
+    share(result_own, result_out)
+    for m in (3, 2, 1, 0):
+        d = g ^ m
+        rows = shard_rows(d * ranks + r)
+        moves_qkv[m].wait_recv()
+        w_qkv[rows, :] = (w_qkv[rows, :].astype(F32) + in_qkv[d].astype(F32)).astype(BF16)
+        for i, out in enumerate((q_out, k_out, v_out)):
+            give(w_qkv.at[rows, i * HD : (i + 1) * HD], out.at[:, lane(g * HD, HD)], m)
+    dn_one = third.last()
+    values = own_x[...].astype(F32)
+    inverse = lax.rsqrt(mean_square(values) + epsilon)
+    scaled = dn_one * gains_all[0:1, :]
+    gain_part[0:1, :] = jnp.sum(dn_one * values * inverse, axis=0, keepdims=True)
+    back = inverse * scaled - values * (inverse * inverse * inverse) * jnp.mean(
+        scaled * values, axis=1, keepdims=True
+    )
+    gain_moves = [
+        net.put(gain_part.at[:, lane((s ^ m) * width, width)], gain_in.at[m - 1], (s ^ m, h))
+        for m in range(1, shards)
+    ]
+    rows_own[...] = (dhidden[...] + back).astype(BF16)
+    relay()
+    share(rows_own, rows_out)
+    total = gain_part[:, lane(s * width, width)]
+    for m in range(1, shards):
+        gain_moves[m - 1].wait_recv()
+        total += gain_in[m - 1]
+    gain_mid[...] = total
+    gain_ends = [net.put(gain_mid, gain_near.at[m - 1], (s, h ^ m)) for m in range(1, 4)]
+    relay()
+    for m in range(1, 4):
+        gain_ends[m - 1].wait_recv()
+        total += gain_near[m - 1]
+    gains_out[...] = total
+    for copy in final:
+        copy.wait_recv()
+    net.sent()
+    for copy in final_own:
+        copy.wait()
+
+
+def rows_plan(
+    groups,
+    ranks,
+    tokens,
+    attn_gain,
+    query_weight,
+    key_weight,
+    value_weight,
+    out_weight,
+    mlp_gain,
+    gate_weight,
+    up_weight,
+    down_weight,
+    cotangent,
+):
+    count, depth = tokens.shape
+    shards = groups * ranks
+    quarter = count // 4
+    width = query_weight.shape[0]
+    units = gate_weight.shape[1] // groups
+    total_rows = count * shards
+    here = groups * count
+    r = lax.axis_index("seq") % ranks
+    gains = jnp.concatenate([attn_gain[None], mlp_gain[None], jnp.zeros((6, width), BF16)]).astype(F32)
+    places = (
+        (jnp.arange(groups, dtype=jnp.int32) * ranks + r)[:, None] * count
+        + jnp.arange(count, dtype=jnp.int32)[None, :]
+    ).reshape(here)
+    lanes = jnp.arange(HD, dtype=jnp.int32)
+    half = HD // 2
+    frequency = jnp.exp((lanes % half).astype(F32) * (-math.log(10000.0) / half))
+    angles = places.astype(F32)[:, None] * frequency[None, :]
+    cosines = jnp.cos(angles)
+    sines = jnp.sin(angles) * jnp.where(lanes < half, -1.0, 1.0)[None, :]
+    ins = (tokens, cotangent, gains, query_weight, key_weight, value_weight, out_weight, gate_weight, up_weight, down_weight, cosines, sines)
+    shape = jax.ShapeDtypeStruct
+    hbm, vmem = pl.BlockSpec(memory_space=pl.ANY), pl.BlockSpec(memory_space=pltpu.VMEM)
+    owners = (query_weight, key_weight, value_weight, out_weight, gate_weight, up_weight, down_weight)
+    outs = [
+        shape((count, depth), BF16),
+        shape((count, depth), BF16),
+        shape((8, width), F32),
+        *(shape(w.shape, BF16) for w in owners),
+    ]
+
+    def low(*extent):
+        return pltpu.VMEM(extent, BF16)
+
+    def full(*extent):
+        return pltpu.VMEM(extent, F32)
+
+    def collector():
+        return [
+            low(here, depth),
+            low(groups, 2, quarter, depth),
+            low(groups, quarter, depth),
+            low(3, quarter, depth),
+        ]
+
+    scratch = [
+        full(8, depth),
+        low(here, depth), low(here, depth), low(here, depth), low(here, depth),
+        low(depth, 3 * HD), low(HD, depth), low(depth, 2 * units), low(units, depth),
+        low(here, HD), low(total_rows, 2 * HD), low(here, HD), low(here, HD), low(here, 3 * HD),
+        full(total_rows, 2 * HD), low(groups, count, 2 * HD), low(groups, count, 2 * HD),
+        low(here, units), low(here, 2 * units), full(here, units),
+        low(quarter, depth), full(quarter, depth), full(quarter, depth),
+        *collector(), *collector(),
+        low(groups, width, 2 * units), low(groups, units, width), low(groups, width, 3 * HD), low(groups, HD, width),
+        full(8, depth), full(shards - 1, 8, width), full(8, width), full(3, 8, width),
+        low(quarter, depth), low(quarter, depth),
+        pltpu.SemaphoreType.DMA((320,)), pltpu.SemaphoreType.DMA((320,)), pltpu.SemaphoreType.DMA((48,)),
+    ]
+    result, rows_grad, gain_grads, *grads = pl.pallas_call(
+        functools.partial(layer_body, groups, ranks),
+        out_shape=outs,
+        in_specs=[hbm] * 10 + [vmem] * 2,
+        out_specs=[hbm, hbm, vmem] + [hbm] * 7,
+        scratch_shapes=scratch,
+        compiler_params=pltpu.CompilerParams(
+            collective_id=1, has_side_effects=True, vmem_limit_bytes=VMEM_LIMIT
+        ),
+    )(*ins)
+    grads = [w.astype(F32) for w in grads]
+    return (result, rows_grad, gain_grads[0], *grads[:4], gain_grads[1], *grads[4:])
+
+
+def on_device(tokens, attn_gain, query_weight, *rest):
+    groups = query_weight.shape[1] // HD
+    ranks = lax.axis_size("seq") // groups
+    fits = lax.axis_size("head") == 4 and groups == 4 and ranks == 2 and query_weight.shape[0] % 128 == 0
+    plan = functools.partial(rows_plan, groups, ranks) if fits else gathered_weights
+    return plan(tokens, attn_gain, query_weight, *rest)
+
+
 def solution(mesh):
     in_specs = (
         P("seq", None),

time: 2390 us -> 442 us (0.18)
  waiting for transfers between devices: 2070 us -> 0 us
  Pallas kernels: 0 us -> 417 us
  matrix products: 129 us -> 0 us
  blocking collectives: 80.6 us -> 0 us
  local copies, waits for them, and re-layouts: 56 us -> 4.71 us
    reduce_scatter x9 -> x0, waiting for transfers between devices: 1360 us -> none  [the longest x1 287 us: on_device(): lax.psum_scatter(grad_gate, 'seq', scatter_dimension=0, tiled=True)]
    all_gather x9 -> x0, waiting for transfers between devices: 600 us -> none  [the longest x1 124 us: on_device(): lax.all_gather(gate_weight, 'seq', axis=0, tiled=True)]
    pallas_call x0 -> x1, Pallas kernels: none -> 417 us  [rows_plan(): pl.pallas_call(functools.partial(layer_body, groups, ranks), out_shape=ou...]
    dot_general x43 -> x0, matrix products: 123 us -> none  [the longest x1 10 us: on_device(): jnp.einsum('tk,tf->kf', normed_two, dup, preferred_element_type=jnp.float32)]
    psum x4 -> x0, waiting for transfers between devices: 111 us -> none  [the longest x1 41.9 us: on_device(): lax.psum(jnp.einsum('tf,kf->tk', dgate, gate_back, preferred_element_type...]
    all_gather x2 -> x0, blocking collectives: 41.7 us -> none  [the longest x1 22.3 us: on_device(): lax.all_gather(attn_gain, 'seq', axis=0, tiled=True)]
    unnamed x1 -> x0, blocking collectives: 38.8 us -> none
  transfers between devices with their start and end apart: 22 -> 0, of which waited for: 22 -> 0; matrix products, arithmetic and copies ran while one was open for 5% -> 0% of each run, Pallas kernels for 0% -> 0%
where the time goes in v2:
time: 442 us; the launch traced here: 436 us
  Pallas kernels  417 us (94%)
  other arithmetic  13.1 us (3%)
  local copies, waits for them, and re-layouts  4.71 us (1%)
    pallas_call x1, Pallas kernels, rows_plan(): pl.pallas_call(functools.partial(layer_body, groups, ranks), out_shape=ou...  417 us
    convert_element_type x7, other arithmetic, rows_plan(): grads = [w.astype(F32) for w in grads]  9.3 us

profile of v2, /device:TPU:0, one launch (start us, length us, event | category | flops | bytes accessed | tf_op | source)
XLA Modules:
  0.0 435.8 jit_solution(15004471188567724172)
XLA Ops:
  0.7 0.1 convert_bitcast_fusion
  0.8 3.1 fusion
  3.8 0.7 broadcast_in_dim.22
  4.5 0.7 broadcast_in_dim.23
  5.1 0.1 pad.2.clone
  5.2 0.7 maximum_convert_fusion.refs_2_
  5.9 417.1 %shard_map.194 = (bf16[256,2048]{1,0:T(8,128)(2,1)}, bf16[256,2048]{1,0:T(8,128)(2,1)}, f32[8,256]{1,0:T(8,128)}, bf16[256,512]{1,0:T(8,128)(2,1)}, bf16[256,512...) custom-call(bf16[256,2048]{1,0:T(8,128)(2,1)} %refs_0_.1, ...), custom_call_target="tpu_custom_call" | custom-call | tf_op jit(solution)/shard_map/pallas_call | solution.py:1045
  423.0 0.0 copy-start.1
  423.0 2.9 convert_element_type.49
  425.8 0.0 copy-start
  425.9 0.0 copy-done.1
  425.9 1.6 convert_element_type.50
  427.4 0.0 copy-start.7
  427.4 0.0 copy-start.6
  427.4 0.0 copy-done
  427.4 0.0 copy-start.5
  427.4 0.0 copy-start.4
  427.4 1.5 convert_element_type.51
  428.9 0.0 copy-start.3
  428.9 0.0 copy-done.7
  428.9 0.9 convert_element_type.45
  429.8 0.0 copy-done.6
  429.8 0.0 copy-start.2
  429.8 0.9 convert_element_type.46
  430.6 0.0 copy-done.5
  430.6 0.9 convert_element_type.47
  431.5 0.0 copy-done.4
  431.5 0.8 convert_element_type.48
  432.3 1.3 fusion.4
  433.7 0.0 copy-done.3
  433.7 1.0 copy.25
  434.6 0.0 copy-done.2
  434.6 1.0 copy.26
  (4 shorter events, 0.0 us)
Async XLA Ops:
  423.0 2.9 copy-start.1
  425.8 1.6 copy-start
  427.4 1.5 copy-start.7
  427.4 2.4 copy-start.6
  427.4 3.2 copy-start.5
  427.4 4.1 copy-start.4
  428.9 4.8 %copy-start.3 = (bf16[256,2048]{1,0:T(8,128)(2,1)S(1)}, bf16[256,2048]{1,0:T(8,128)(2,1)}, u32[]{:S(2)}) copy-start(bf16[256,2048]{1,0:T(8,128)(2,1)} %get-tuple-element.48) | copy-start | bytes 3145732
  429.8 4.9 %copy-start.2 = (bf16[256,2048]{1,0:T(8,128)(2,1)S(1)}, bf16[256,2048]{1,0:T(8,128)(2,1)}, u32[]{:S(2)}) copy-start(bf16[256,2048]{1,0:T(8,128)(2,1)} %get-tuple-element.49) | copy-start | bytes 3145732

commit v3 on v0

--- a/solution.py
+++ b/solution.py
@@ -1,15 +1,22 @@
+import functools
 import math
 
 import jax
 import jax.numpy as jnp
 from jax import lax
+from jax.experimental import pallas as pl
+from jax.experimental.pallas import tpu as pltpu
 from jax.sharding import PartitionSpec as P
+
+MESH = pl.DeviceIdType.MESH
+F32, BF16 = jnp.float32, jnp.bfloat16
 
 HD = 128
 
 
 epsilon = 1e-05
 block_limit = 512
+VMEM_LIMIT = 63 * 2**20
 
 
 def tables(offset, length, half_width):
@@ -50,7 +57,7 @@
     return (value_grad, gain_grad)
 
 
-def on_device(
+def gathered_weights(
     tokens,
     attn_gain,
     query_weight,
@@ -283,6 +290,971 @@
     )
 
 
+class Net:
+    def __init__(self, send, receive):
+        self.send, self.receive, self.count, self.lots = send, receive, 0, []
+
+    def lot(self, size, describe):
+        return Lot(self, size, describe)
+
+    def finish(self):
+        for lot in self.lots:
+            for j in sorted(lot.open):
+                lot.sent(j)
+
+
+class Lot:
+    def __init__(self, net, size, describe):
+        self.net, self.base, self.describe, self.open = net, net.count, describe, set()
+        net.count += size
+        net.lots.append(self)
+
+    def copy(self, j):
+        source, target, device = self.describe(j)
+        return pltpu.make_async_remote_copy(
+            src_ref=source,
+            dst_ref=target,
+            send_sem=self.net.send.at[self.base + j],
+            recv_sem=self.net.receive.at[self.base + j],
+            device_id=device,
+            device_id_type=MESH,
+        )
+
+    def start(self, j):
+        self.copy(j).start()
+        if isinstance(j, int):
+            self.open.add(j)
+
+    def arrived(self, j):
+        self.copy(j).wait_recv()
+
+    def sent(self, j):
+        if j in self.open:
+            self.open.remove(j)
+            self.copy(j).wait_send()
+
+
+class Keep:
+    def __init__(self, sems):
+        self.sems, self.count = sems, 0
+
+    def put(self, source, target):
+        copy = pltpu.make_async_copy(source, target, self.sems.at[self.count])
+        self.count += 1
+        copy.start()
+        return copy
+
+
+class Where:
+    def __init__(self, groups, ranks):
+        self.s, self.h = lax.axis_index("seq"), lax.axis_index("head")
+        self.g, self.r = self.s // ranks, self.s % ranks
+        self.groups, self.ranks = groups, ranks
+
+    def along(self, m):
+        return (self.s ^ (m * self.ranks), self.h)
+
+    def beside(self):
+        return (self.s ^ 1, self.h)
+
+    def across(self):
+        return (self.s, self.h ^ 2)
+
+    def near(self):
+        return (self.s, self.h ^ 1)
+
+
+def lane(start, size):
+    return pl.ds(pl.multiple_of(start, 128), size)
+
+
+def row(start, size):
+    return pl.ds(pl.multiple_of(start, size), size)
+
+
+def each(count, step):
+    def body(i, carry):
+        step(i)
+        return carry
+
+    lax.fori_loop(0, count, body, 0)
+
+
+class Spread:
+    def __init__(self, net, at, buffer, quarter, own=None):
+        self.at, self.buffer, self.quarter, self.shared = at, buffer, quarter, own is not None
+        first = self.block(0, 0) if own is None else own
+        self.z = net.lot(
+            4,
+            lambda m: (self.block(2, 0), self.block(2, 0), at.along(1))
+            if m == 3
+            else (first, self.block(0, 0), at.along(m)),
+        )
+        self.x = net.lot(4, lambda m: (self.block(m, 0), self.block(m, 0), at.across()))
+        self.c = net.lot(4, lambda m: (self.block(m, 0), self.block(m, 0), at.near()))
+        self.d = net.lot(4, lambda m: (self.block(m, 2), self.block(m, 2), at.near()))
+
+    def block(self, m, k):
+        at = self.at
+        return self.buffer.at[row(((at.g ^ m) * 4 + (at.h ^ k)) * self.quarter, self.quarter), :]
+
+    def pass_on(self, m):
+        self.x.start(m)
+        self.c.start(m)
+
+    def start(self):
+        self.z.start(2)
+        self.z.start(1)
+        if not self.shared:
+            self.pass_on(0)
+
+    def arrive(self, m):
+        self.z.arrived(m)
+        if m == 2:
+            self.z.start(3)
+        self.pass_on(m)
+
+    def second(self, m):
+        self.x.arrived(m)
+        self.d.start(m)
+
+    def ready(self, m):
+        self.c.arrived(m)
+        self.d.arrived(m)
+
+    def sent(self, m):
+        for lot in (self.x, self.c, self.d):
+            lot.sent(m)
+        if m == 2:
+            self.z.sent(3)
+
+
+class Collect:
+    def __init__(self, net, at, refs, quarter, out):
+        self.at, self.quarter, self.out = at, quarter, out
+        self.part, self.near, self.xin, self.zin = refs
+        self.a = net.lot(4, lambda m: (self.part.at[self.rows(m, 3), :], self.near.at[at.g ^ m, 1], at.near()))
+        self.e = net.lot(4, lambda m: (self.part.at[self.rows(m, 1), :], self.near.at[at.g ^ m, 0], at.near()))
+        self.b = net.lot(4, lambda m: (self.part.at[self.rows(m, 2), :], self.xin.at[at.g ^ m], at.across()))
+        hops = {3: (0, 1), 2: (2, 2), 1: (1, 1)}
+        self.z = net.lot(
+            4, lambda m: (self.part.at[self.rows(m, 0), :], self.zin.at[hops[m][0]], at.along(hops[m][1]))
+        )
+
+    def rows(self, m, k):
+        at = self.at
+        return row(((at.g ^ m) * 4 + (at.h ^ k)) * self.quarter, self.quarter)
+
+    def first(self, m):
+        self.a.start(m)
+        self.e.start(m)
+
+    def slices(self, m, k, step):
+        at = self.at
+        start = ((at.g ^ m) * 4 + (at.h ^ k)) * self.quarter
+        each(self.quarter // 16, lambda i: step(row(start + i * 16, 16), row(i * 16, 16)))
+
+    def second(self, m):
+        d = self.at.g ^ m
+        self.a.arrived(m)
+
+        def step(rows, few):
+            total = self.part[rows, :].astype(F32) + self.near[d, 1, few, :].astype(F32)
+            self.part[rows, :] = total.astype(BF16)
+
+        self.slices(m, 2, step)
+        self.b.start(m)
+
+    def third(self, m):
+        d = self.at.g ^ m
+        self.e.arrived(m)
+        self.b.arrived(m)
+        if m == 2:
+            self.z.arrived(3)
+
+        def step(rows, few):
+            total = self.part[rows, :].astype(F32) + self.near[d, 0, few, :].astype(F32)
+            total += self.xin[d, few, :].astype(F32)
+            if m == 2:
+                total += self.zin[0, few, :].astype(F32)
+            if m:
+                self.part[rows, :] = total.astype(BF16)
+            else:
+                self.out[few, :] = total
+
+        self.slices(m, 0, step)
+        if m:
+            self.z.start(m)
+
+    def last(self):
+        self.third(0)
+        self.z.arrived(1)
+        self.z.arrived(2)
+
+    def total(self, few):
+        return self.out[few, :] + self.zin[1, few, :].astype(F32) + self.zin[2, few, :].astype(F32)
+
+    def produce(self, work):
+        def step(i):
+            m = 3 - i
+            work(m)
+            self.first(m)
+
+            @pl.when(i > 0)
+            def _():
+                self.second(m + 1)
+
+        each(4, step)
+        for lot in (self.a, self.e):
+            lot.open.update(range(4))
+        self.b.open.update((1, 2, 3))
+
+    def sent(self):
+        for m in range(4):
+            for lot in (self.a, self.e, self.b, self.z):
+                lot.sent(m)
+
+
+class Turn:
+    def __init__(self, net, keep, at, source, view, blocks):
+        self.keep, self.at, self.source, self.view, self.blocks = keep, at, source, view, blocks
+        n = sum(len(items) for items, _ in blocks)
+        self.n = n
+        self.z = net.lot(
+            4 * n,
+            lambda j: (source(j % n, at.g ^ (j // n)), view(j % n, at.s), at.along(j // n)),
+        )
+        self.o = net.lot(n, lambda i: (source(i, at.g), view(i, at.s), at.beside()))
+        self.y = net.lot(4 * len(blocks), self.sent_on)
+        self.own = {}
+
+    def sent_on(self, j):
+        at = self.at
+        block = self.blocks[j // 4][1](at.s ^ (j % 4 * at.ranks))
+        return (block, block, at.beside())
+
+    def start(self, m, b=0):
+        for i in self.blocks[b][0]:
+            self.z.start(m * self.n + i)
+
+    def mine(self, b=0):
+        at = self.at
+        for i in self.blocks[b][0]:
+            self.own[i] = self.keep.put(self.source(i, at.g), self.view(i, at.s))
+            self.o.start(i)
+
+    def pass_on(self, m, b=0):
+        for i in self.blocks[b][0]:
+            self.z.arrived(m * self.n + i)
+        self.y.start(b * 4 + m)
+
+    def ready(self, b=0):
+        for i in self.blocks[b][0]:
+            self.own[i].wait()
+            self.o.arrived(i)
+        for m in (1, 2, 3):
+            self.y.arrived(b * 4 + m)
+
+    def sent(self, b=0):
+        for m in (1, 2, 3):
+            self.y.sent(b * 4 + m)
+
+
+def dot(a, b):
+    return jnp.dot(a, b, preferred_element_type=F32)
+
+
+def dot_nt(a, b):
+    return lax.dot_general(a, b, (((1,), (1,)), ((), ())), preferred_element_type=F32)
+
+
+def dot_tn(a, b):
+    return lax.dot_general(a, b, (((0,), (0,)), ((), ())), preferred_element_type=F32)
+
+
+def turned(values, cos_table, sin_table):
+    return values * cos_table + pltpu.roll(values, HD // 2, 1) * sin_table
+
+
+def mean_square(values):
+    return jnp.mean(values * values, axis=1, keepdims=True)
+
+
+def layer_body(groups, ranks, *refs):
+    (tok, cot, gains, qw, kw, vw, ow, gw, uw, dw, cosines, sines) = refs[:12]
+    (result_out, rows_out, gains_out, q_out, k_out, v_out, o_out, g_out, u_out, d_out) = refs[12:22]
+    (
+        gains_all, rows_one, rows_cot, rows_two, rows_dh, w_qkv, w_o, w_gu, w_d, queries, pairs, mix, dqkv, accum, pair_send,
+        pair_in, mixed, dgu, dmixed, own_x, hidden, dhidden, summed, part_a, near_a, xin_a, zin_a, part_b, near_b, xin_b, zin_b,
+        in_gu, in_d, in_qkv, in_o, gain_part, gain_in, gain_mid, gain_near, result_own, rows_own, send, receive, local,
+    ) = refs[22:]
+    at = Where(groups, ranks)
+    s, h, g, r = at.s, at.h, at.g, at.r
+    shards = groups * ranks
+    count, depth = tok.shape
+    quarter = count // 4
+    width = gains.shape[1]
+    units = gw.shape[1] // groups
+    half = units // 2
+    total_rows = count * shards
+    score_scale = 1.0 / math.sqrt(HD)
+    score_shift = math.log(total_rows)
+    peers = [(s ^ m, h) for m in range(1, shards)] + [(s, h ^ m) for m in range(1, 4)]
+    barrier = pltpu.get_barrier_semaphore()
+    for peer in peers:
+        pl.semaphore_signal(barrier, inc=1, device_id=peer, device_id_type=MESH)
+    pl.semaphore_wait(barrier, len(peers))
+    net, keep = Net(send, receive), Keep(local)
+
+    def chunk(m):
+        return row((g ^ m) * count, count)
+
+    def shard_rows(shard):
+        return row(shard * width, width)
+
+    def columns_of(shard):
+        return lane(shard * width, width)
+
+    turn_qkv = Turn(
+        net, keep, at,
+        lambda i, group: (qw, kw, vw)[i].at[:, lane(group * HD, HD)],
+        lambda i, shard: w_qkv.at[shard_rows(shard), i * HD : (i + 1) * HD],
+        [((0, 1, 2), lambda shard: w_qkv.at[shard_rows(shard), :])],
+    )
+    turn_gu = Turn(
+        net, keep, at,
+        lambda i, group: (gw, uw)[i % 2].at[:, lane(group * units + (i // 2) * half, half)],
+        lambda i, shard: w_gu.at[shard_rows(shard), i * half : (i + 1) * half],
+        [((2 * b, 2 * b + 1), lambda shard, b=b: w_gu.at[shard_rows(shard), b * units : (b + 1) * units]) for b in (0, 1)],
+    )
+    turn_o = Turn(
+        net, keep, at,
+        lambda i, group: ow.at[row(group * HD, HD), :],
+        lambda i, shard: w_o.at[:, columns_of(shard)],
+        [((0,), lambda shard: w_o.at[:, columns_of(shard)])],
+    )
+    turn_d = Turn(
+        net, keep, at,
+        lambda i, group: dw.at[row(group * units + i * half, half), :],
+        lambda i, shard: w_d.at[i * half : (i + 1) * half, columns_of(shard)],
+        [((b,), lambda shard, b=b: w_d.at[b * half : (b + 1) * half, columns_of(shard)]) for b in (0, 1)],
+    )
+
+    gain_slot = gains_all.at[:, columns_of(s)]
+    gain_moves = net.lot(shards, lambda m: (gains, gain_slot, (s ^ m, h)))
+    for m in range(1, shards):
+        gain_moves.start(m)
+    gain_own = keep.put(gains, gain_slot)
+    strip = row(h * quarter, quarter)
+    one = Spread(net, at, rows_one, quarter, tok.at[strip, :])
+    one.start()
+    own_rows = keep.put(tok, rows_one.at[chunk(0), :])
+    own_strip = keep.put(tok.at[strip, :], own_x)
+    turn_qkv.start(3)
+    turn_qkv.mine()
+    turn_o.mine()
+    own_cot = keep.put(cot, rows_cot.at[chunk(0), :])
+    gain_part[...] = jnp.zeros_like(gain_part)
+
+    def clear(i):
+        rows = row(i * 64, 64)
+        accum[rows, :] = jnp.zeros_like(accum[rows, :])
+
+    each(total_rows // 64, clear)
+
+    gain_own.wait()
+    for m in range(1, shards):
+        gain_moves.arrived(m)
+
+    def norm_one(m):
+        def some(i):
+            rows = row((g ^ m) * count + i * 32, 32)
+            values = rows_one[rows, :].astype(F32)
+            inverse = lax.rsqrt(mean_square(values) + epsilon)
+            rows_one[rows, :] = (values * inverse * gains_all[0:1, :]).astype(BF16)
+
+        each(count // 32, some)
+
+    own_rows.wait()
+    own_strip.wait()
+    norm_one(0)
+    one.arrive(1)
+    one.arrive(2)
+    turn_qkv.start(2)
+    turn_qkv.start(1)
+    for m in (3, 2, 1):
+        turn_o.start(m)
+    one.second(1)
+    one.second(2)
+    turn_qkv.pass_on(3)
+    one.arrive(3)
+    grad = Spread(net, at, rows_cot, quarter, cot.at[strip, :])
+    grad.start()
+    one.ready(1)
+    one.sent(1)
+    norm_one(1)
+    one.ready(2)
+    one.sent(2)
+    norm_one(2)
+    turn_qkv.pass_on(1)
+    one.second(3)
+    turn_qkv.pass_on(2)
+    one.ready(3)
+    one.sent(3)
+    norm_one(3)
+    for m in (3, 2, 1):
+        turn_d.start(m, 0)
+    turn_qkv.ready()
+
+    def own_place(m):
+        return row(((g ^ m) * ranks + r) * count, count)
+
+    pair_moves = net.lot(4, lambda m: (pairs.at[own_place(m), :], pairs.at[own_place(m), :], at.beside()))
+
+    def project(m):
+        rows, place = chunk(m), own_place(m)
+        heads = dot(rows_one[rows, :], w_qkv[...])
+        cos_part, sin_part = cosines[rows, :], sines[rows, :]
+        queries[rows, :] = turned(heads[:, :HD], cos_part, sin_part).astype(BF16)
+        pairs[place, :HD] = turned(heads[:, HD : 2 * HD], cos_part, sin_part).astype(BF16)
+        pairs[place, HD:] = heads[:, 2 * HD :].astype(BF16)
+        pair_moves.start(m)
+
+    each(4, project)
+    pair_moves.open.update(range(4))
+    for m in (3, 2, 1):
+        turn_o.pass_on(m)
+    turn_gu.start(3, 0)
+    turn_gu.start(1, 0)
+    for m in (3, 2, 1):
+        turn_d.start(m, 1)
+    grad.arrive(1)
+    grad.arrive(2)
+    turn_d.mine(0)
+    turn_gu.mine(0)
+    for m in (0, 1, 2, 3):
+        pair_moves.arrived(m)
+    turn_o.ready()
+    span = ranks * count
+
+    def weights_of(m, j, query):
+        keys = pairs[row(j * span, span), :HD]
+        scores = dot_nt(query, keys) * score_scale - score_shift
+        q_place = ((g ^ m) * ranks + r) * count + lax.broadcasted_iota(jnp.int32, (count, span), 0)
+        k_place = j * span + lax.broadcasted_iota(jnp.int32, (count, span), 1)
+        return jnp.where(k_place <= q_place, jax.nn.sigmoid(scores), 0.0)
+
+    def attend(m):
+        rows = chunk(m)
+        query = queries[rows, :]
+
+        def step(j, total):
+            weight = weights_of(m, j, query).astype(BF16)
+            return total + dot(weight, pairs[row(j * span, span), HD:])
+
+        total = lax.fori_loop(0, (g ^ m) + 1, step, jnp.zeros((count, HD), F32))
+        low = total.astype(BF16)
+        mix[rows, :] = low
+        part_a[rows, :] = dot(low, w_o[...]).astype(BF16)
+
+    set_a, set_b = (part_a, near_a, xin_a, zin_a), (part_b, near_b, xin_b, zin_b)
+    first = Collect(net, at, set_a, quarter, summed)
+    first.produce(attend)
+    first.third(3)
+    first.second(0)
+    turn_gu.start(1, 1)
+    turn_d.mine(1)
+    turn_gu.mine(1)
+    for m in (3, 2, 1):
+        turn_d.pass_on(m, 0)
+    first.third(2)
+    grad.second(1)
+    grad.second(2)
+    grad.arrive(3)
+    first.third(1)
+    first.last()
+    two = Spread(net, at, rows_two, quarter)
+    mine_start = (g * 4 + h) * quarter
+
+    def norm_two(i):
+        few = row(i * 16, 16)
+        values = own_x[few, :].astype(F32) + first.total(few)
+        hidden[few, :] = values
+        inverse = lax.rsqrt(mean_square(values) + epsilon)
+        rows_two[row(mine_start + i * 16, 16), :] = (values * inverse * gains_all[1:2, :]).astype(BF16)
+
+    each(quarter // 16, norm_two)
+    two.start()
+    turn_gu.start(2, 0)
+    turn_gu.start(3, 1)
+    turn_gu.start(2, 1)
+    turn_gu.pass_on(3, 0)
+    turn_gu.pass_on(1, 0)
+    for m in (3, 2, 1):
+        turn_d.pass_on(m, 1)
+    grad.second(3)
+    two.second(0)
+    two.arrive(1)
+    turn_gu.pass_on(1, 1)
+    turn_d.ready(0)
+    own_cot.wait()
+
+    def early(m, b):
+        lanes = slice(b * half, (b + 1) * half)
+        dmixed[chunk(m), lanes] = dot_nt(rows_cot[chunk(m), :], w_d[lanes, :])
+
+    for m in (1, 2, 3):
+        grad.ready(m)
+    each(4, lambda m: early(m, 0))
+    two.arrive(2)
+    two.second(1)
+    two.second(2)
+    two.arrive(3)
+    turn_gu.pass_on(2, 0)
+    two.second(3)
+    turn_gu.pass_on(3, 1)
+    for m in (0, 1, 2, 3):
+        two.ready(m)
+    turn_gu.ready(0)
+
+    def feed(m, b):
+        rows = chunk(m)
+        lanes, pair = slice(b * half, (b + 1) * half), slice(b * units, (b + 1) * units)
+        both = dot(rows_two[rows, :], w_gu[:, pair])
+        gate, up = both[:, :half], both[:, half:]
+        sig = jax.nn.sigmoid(gate)
+        act = gate * sig
+        mixed[rows, lanes] = (act * up).astype(BF16)
+        back = dmixed[rows, lanes]
+        dgu[rows, b * units : b * units + half] = (back * up * sig * (1.0 + gate * (1.0 - sig))).astype(BF16)
+        dgu[rows, b * units + half : (b + 1) * units] = (back * act).astype(BF16)
+        total = dot_nt(dgu[rows, pair], w_gu[:, pair])
+        if b:
+            total += part_a[rows, :].astype(F32)
+        part_a[rows, :] = total.astype(BF16)
+
+    def out_part(m, b):
+        rows = chunk(m)
+        lanes = slice(b * half, (b + 1) * half)
+        total = dot(mixed[rows, lanes], w_d[lanes, :])
+        if b:
+            total += part_b[rows, :].astype(F32)
+        part_b[rows, :] = total.astype(BF16)
+
+    def halves(m, work, lot):
+        d = g ^ m
+
+        def step(k):
+            work(d * ranks + (r ^ 1 ^ k))
+
+            @pl.when(k == 0)
+            def _():
+                lot.start(m)
+
+        each(2, step)
+
+    def several(groups_, work, lot):
+        first_, last_ = groups_
+        each(first_ - last_ + 1, lambda i: halves(first_ - i, work, lot))
+        lot.open.update(range(last_, first_ + 1))
+
+    def beside(source, target):
+        def describe(m):
+            d = g ^ m
+            return (source(d * ranks + (r ^ 1)), target(d), at.beside())
+
+        return net.lot(4, describe)
+
+    pairs_of = [slice(b * units, (b + 1) * units) for b in (0, 1)]
+    lanes_of = [slice(b * half, (b + 1) * half) for b in (0, 1)]
+    moves_gu = [
+        beside(lambda shard, p=p: w_gu.at[shard_rows(shard), p], lambda d, p=p: in_gu.at[d, :, p]) for p in pairs_of
+    ]
+    moves_d = [
+        beside(lambda shard, p=p: w_d.at[p, columns_of(shard)], lambda d, p=p: in_d.at[d, p, :]) for p in lanes_of
+    ]
+    moves_qkv = beside(lambda shard: w_qkv.at[shard_rows(shard), :], lambda d: in_qkv.at[d])
+    moves_o = beside(lambda shard: w_o.at[:, columns_of(shard)], lambda d: in_o.at[d])
+
+    def grads_gu(groups_, b):
+        def work(shard):
+            w_gu[shard_rows(shard), pairs_of[b]] = dot_tn(rows_two[:, columns_of(shard)], dgu[:, pairs_of[b]]).astype(BF16)
+
+        several(groups_, work, moves_gu[b])
+
+    def grads_d(groups_, b):
+        def work(shard):
+            columns = columns_of(shard)
+            w_d[lanes_of[b], columns] = dot_tn(mixed[:, lanes_of[b]], rows_cot[:, columns]).astype(BF16)
+
+        several(groups_, work, moves_d[b])
+
+    def grads_o(groups_):
+        def work(shard):
+            columns = columns_of(shard)
+            w_o[:, columns] = dot_tn(mix[...], rows_dh[:, columns]).astype(BF16)
+
+        several(groups_, work, moves_o)
+
+    def grads_qkv(groups_):
+        def work(shard):
+            w_qkv[shard_rows(shard), :] = dot_tn(rows_one[:, columns_of(shard)], dqkv[...]).astype(BF16)
+
+        several(groups_, work, moves_qkv)
+
+    final, final_own = [], []
+
+    def give(source, target, m):
+        if m:
+            lot = net.lot(1, lambda j: (source, target, at.along(m)))
+            lot.start(0)
+            final.append(lot)
+        else:
+            final_own.append(keep.put(source, target))
+
+    def sums(m, lot, mine_of, other_of, size):
+        lot.arrived(m)
+
+        def step(i):
+            a, rows, lanes = mine_of(i)
+            b, d, few, others = other_of(i)
+            a[rows, lanes] = (a[rows, lanes].astype(F32) + b[d, few, others].astype(F32)).astype(BF16)
+
+        each(size // 32, step)
+
+    def sums_gu(m, b):
+        d, p = g ^ m, pairs_of[b]
+        start = (d * ranks + r) * width
+        sums(
+            m, moves_gu[b],
+            lambda i: (w_gu, row(start + i * 32, 32), p), lambda i: (in_gu, d, row(i * 32, 32), p), width,
+        )
+        for i, out in enumerate((g_out, u_out)):
+            place = b * units + i * half
+            give(w_gu.at[row(start, width), place : place + half], out.at[:, lane(g * units + b * half, half)], m)
+
+    def sums_d(m, b):
+        d, base = g ^ m, b * half
+        columns = columns_of(d * ranks + r)
+        sums(
+            m, moves_d[b],
+            lambda i: (w_d, row(base + i * 32, 32), columns),
+            lambda i: (in_d, d, row(base + i * 32, 32), slice(None)), half,
+        )
+        give(w_d.at[lanes_of[b], columns], d_out.at[row(g * units + base, half), :], m)
+
+    def sums_o(m):
+        d = g ^ m
+        columns = columns_of(d * ranks + r)
+        sums(
+            m, moves_o,
+            lambda i: (w_o, row(i * 32, 32), columns), lambda i: (in_o, d, row(i * 32, 32), slice(None)), HD,
+        )
+        give(w_o.at[:, columns], o_out.at[row(g * HD, HD), :], m)
+
+    def sums_qkv(m):
+        d = g ^ m
+        start = (d * ranks + r) * width
+        sums(
+            m, moves_qkv,
+            lambda i: (w_qkv, row(start + i * 32, 32), slice(None)),
+            lambda i: (in_qkv, d, row(i * 32, 32), slice(None)), width,
+        )
+        for i, out in enumerate((q_out, k_out, v_out)):
+            give(w_qkv.at[row(start, width), i * HD : (i + 1) * HD], out.at[:, lane(g * HD, HD)], m)
+
+    first.sent()
+    second = Collect(net, at, set_a, quarter, summed)
+    each(4, lambda m: feed(m, 0))
+    turn_gu.sent(0)
+    turn_gu.pass_on(2, 1)
+    grads_gu((3, 2), 0)
+    turn_d.ready(1)
+    each(4, lambda m: early(m, 1))
+    each(4, lambda m: out_part(m, 0))
+    turn_d.sent(0)
+    grads_gu((1, 1), 0)
+    turn_gu.ready(1)
+    second.produce(lambda m: feed(m, 1))
+    second.third(3)
+    sums_gu(3, 0)
+    second.second(0)
+    second.third(2)
+    sums_gu(2, 0)
+    turn_gu.sent(1)
+    turn_d.sent(1)
+    grads_d((3, 1), 0)
+    second.third(1)
+    grads_gu((3, 1), 1)
+    each(4, lambda m: out_part(m, 1))
+    sums_gu(1, 0)
+    second.last()
+    three = Spread(net, at, rows_dh, quarter)
+
+    def back_two(i, gain_grad):
+        few = row(i * 16, 16)
+        own = row(mine_start + i * 16, 16)
+        upstream, values = second.total(few), hidden[few, :]
+        inverse = lax.rsqrt(mean_square(values) + epsilon)
+        scaled = upstream * gains_all[1:2, :]
+        back = inverse * scaled - values * (inverse * inverse * inverse) * jnp.mean(
+            scaled * values, axis=1, keepdims=True
+        )
+        total = rows_cot[own, :].astype(F32) + back
+        dhidden[few, :] = total
+        rows_dh[own, :] = total.astype(BF16)
+        return gain_grad + jnp.sum(upstream * values * inverse, axis=0, keepdims=True)
+
+    gain_part[1:2, :] = lax.fori_loop(0, quarter // 16, back_two, jnp.zeros((1, depth), F32))
+    three.start()
+    for m in (3, 2, 1):
+        sums_d(m, 0)
+    grads_d((3, 1), 1)
+    three.second(0)
+    three.arrive(1)
+    three.arrive(2)
+    sums_gu(3, 1)
+    three.second(1)
+    for b in (0, 1):
+        grads_gu((0, 0), b)
+    sums_gu(2, 1)
+    three.second(2)
+    three.arrive(3)
+    for b in (0, 1):
+        grads_d((0, 0), b)
+    out_sum = Collect(net, at, set_b, quarter, summed)
+    for m in (3, 2, 1, 0):
+        out_sum.first(m)
+    sums_gu(1, 1)
+    three.second(3)
+
+    def attend_back(m):
+        three.ready(m)
+        rows = chunk(m)
+        query = queries[rows, :]
+        dm = dot_nt(rows_dh[rows, :], w_o[...]).astype(BF16)
+
+        def step(j, total):
+            block = row(j * span, span)
+            weight = weights_of(m, j, query)
+            dweight = dot_nt(dm, pairs[block, HD:])
+            dscore = (dweight * weight * (1.0 - weight)).astype(BF16)
+            accum[block, HD:] += dot_tn(weight.astype(BF16), dm)
+            accum[block, :HD] += dot_tn(dscore, query)
+            return total + dot(dscore, pairs[block, :HD])
+
+        total = lax.fori_loop(0, (g ^ m) + 1, step, jnp.zeros((count, HD), F32))
+        dqkv[rows, :HD] = turned(total * score_scale, cosines[rows, :], -sines[rows, :]).astype(BF16)
+
+    each(4, attend_back)
+    pair_back = net.lot(4, lambda m: (pair_send.at[g ^ m], pair_in.at[g ^ m], at.beside()))
+
+    def send_pair(i):
+        m = 3 - i
+        d = g ^ m
+        rows = row((d * ranks + (r ^ 1)) * count, count)
+        pair_send[d] = accum[rows, :].astype(BF16)
+        pair_back.start(m)
+
+    each(4, send_pair)
+    pair_back.open.update(range(4))
+    for m in (3, 2, 1, 0):
+        out_sum.second(m)
+    for m in (3, 2, 1):
+        sums_d(m, 1)
+    turn_o.sent()
+    grads_o((3, 0))
+    out_sum.third(3)
+    out_sum.third(2)
+    out_sum.third(1)
+    second.sent()
+    third = Collect(net, at, set_a, quarter, summed)
+
+    def back_one(m):
+        d = g ^ m
+        rows = chunk(m)
+        pair_back.arrived(m)
+        both = accum[own_place(m), :] + pair_in[d].astype(F32)
+        dqkv[rows, HD : 2 * HD] = turned(both[:, :HD] * score_scale, cosines[rows, :], -sines[rows, :]).astype(BF16)
+        dqkv[rows, 2 * HD :] = both[:, HD:].astype(BF16)
+        part_a[rows, :] = dot_nt(dqkv[rows, :], w_qkv[...]).astype(BF16)
+
+    third.produce(back_one)
+    third.second(0)
+    turn_qkv.sent()
+    grads_qkv((3, 0))
+    third.third(3)
+    for m in (3, 2, 1):
+        sums_o(m)
+    third.third(2)
+    third.third(1)
+    for b in (0, 1):
+        sums_gu(0, b)
+        sums_d(0, b)
+    ends = []
+
+    def share(source, target):
+        place = target.at[strip, :]
+        final_own.append(keep.put(source, place))
+        lot = net.lot(2, lambda j: (source, place, (at.near(), at.across())[j]))
+        lot.start(0)
+        lot.start(1)
+        ends.append((lot, target))
+
+    def relay():
+        lot, target = ends.pop()
+        lot.arrived(1)
+        final.append(lot)
+        block = target.at[row((h ^ 2) * quarter, quarter), :]
+        on = net.lot(1, lambda j: (block, block, at.near()))
+        on.start(0)
+        final.append(on)
+
+    for m in (3, 2, 1, 0):
+        sums_qkv(m)
+    out_sum.last()
+
+    def result_rows(i):
+        few = row(i * 16, 16)
+        result_own[few, :] = (hidden[few, :] + out_sum.total(few)).astype(BF16)
+
+    each(quarter // 16, result_rows)
+    share(result_own, result_out)
+    third.last()
+
+    def back_rows(i, gain_grad):
+        few = row(i * 16, 16)
+        upstream, values = third.total(few), own_x[few, :].astype(F32)
+        inverse = lax.rsqrt(mean_square(values) + epsilon)
+        scaled = upstream * gains_all[0:1, :]
+        back = inverse * scaled - values * (inverse * inverse * inverse) * jnp.mean(
+            scaled * values, axis=1, keepdims=True
+        )
+        rows_own[few, :] = (dhidden[few, :] + back).astype(BF16)
+        return gain_grad + jnp.sum(upstream * values * inverse, axis=0, keepdims=True)
+
+    gain_part[0:1, :] = lax.fori_loop(0, quarter // 16, back_rows, jnp.zeros((1, depth), F32))
+    gain_sums = net.lot(shards, lambda m: (gain_part.at[:, columns_of(s ^ m)], gain_in.at[m - 1], (s ^ m, h)))
+    for m in range(1, shards):
+        gain_sums.start(m)
+    relay()
+    share(rows_own, rows_out)
+    total = gain_part[:, columns_of(s)]
+    for m in range(1, shards):
+        gain_sums.arrived(m)
+        total += gain_in[m - 1]
+    gain_mid[...] = total
+    gain_ends = net.lot(4, lambda m: (gain_mid, gain_near.at[m - 1], (s, h ^ m)))
+    for m in range(1, 4):
+        gain_ends.start(m)
+    sums_o(0)
+    relay()
+    for m in range(1, 4):
+        gain_ends.arrived(m)
+        total += gain_near[m - 1]
+    gains_out[...] = total
+    for lot in final:
+        lot.arrived(0)
+    net.finish()
+    for copy in final_own:
+        copy.wait()
+
+
+def rows_plan(
+    groups,
+    ranks,
+    tokens,
+    attn_gain,
+    query_weight,
+    key_weight,
+    value_weight,
+    out_weight,
+    mlp_gain,
+    gate_weight,
+    up_weight,
+    down_weight,
+    cotangent,
+):
+    count, depth = tokens.shape
+    shards = groups * ranks
+    quarter = count // 4
+    width = query_weight.shape[0]
+    units = gate_weight.shape[1] // groups
+    total_rows = count * shards
+    here = groups * count
+    r = lax.axis_index("seq") % ranks
+    gains = jnp.concatenate([attn_gain[None], mlp_gain[None], jnp.zeros((6, width), BF16)]).astype(F32)
+    places = (
+        (jnp.arange(groups, dtype=jnp.int32) * ranks + r)[:, None] * count
+        + jnp.arange(count, dtype=jnp.int32)[None, :]
+    ).reshape(here)
+    lanes = jnp.arange(HD, dtype=jnp.int32)
+    half = HD // 2
+    frequency = jnp.exp((lanes % half).astype(F32) * (-math.log(10000.0) / half))
+    angles = places.astype(F32)[:, None] * frequency[None, :]
+    cosines = jnp.cos(angles)
+    sines = jnp.sin(angles) * jnp.where(lanes < half, -1.0, 1.0)[None, :]
+    ins = (tokens, cotangent, gains, query_weight, key_weight, value_weight, out_weight, gate_weight, up_weight, down_weight, cosines, sines)
+    shape = jax.ShapeDtypeStruct
+    hbm, vmem = pl.BlockSpec(memory_space=pl.ANY), pl.BlockSpec(memory_space=pltpu.VMEM)
+    owners = (query_weight, key_weight, value_weight, out_weight, gate_weight, up_weight, down_weight)
+    outs = [
+        shape((count, depth), BF16),
+        shape((count, depth), BF16),
+        shape((8, width), F32),
+        *(shape(w.shape, BF16) for w in owners),
+    ]
+
+    def low(*extent):
+        return pltpu.VMEM(extent, BF16)
+
+    def full(*extent):
+        return pltpu.VMEM(extent, F32)
+
+    def collector():
+        return [
+            low(here, depth),
+            low(groups, 2, quarter, depth),
+            low(groups, quarter, depth),
+            low(3, quarter, depth),
+        ]
+
+    scratch = [
+        full(8, depth),
+        low(here, depth), low(here, depth), low(here, depth), low(here, depth),
+        low(depth, 3 * HD), low(HD, depth), low(depth, 2 * units), low(units, depth),
+        low(here, HD), low(total_rows, 2 * HD), low(here, HD), low(here, 3 * HD),
+        full(total_rows, 2 * HD), low(groups, count, 2 * HD), low(groups, count, 2 * HD),
+        low(here, units), low(here, 2 * units), full(here, units),
+        low(quarter, depth), full(quarter, depth), full(quarter, depth), full(quarter, depth),
+        *collector(), *collector(),
+        low(groups, width, 2 * units), low(groups, units, width), low(groups, width, 3 * HD), low(groups, HD, width),
+        full(8, depth), full(shards - 1, 8, width), full(8, width), full(3, 8, width),
+        low(quarter, depth), low(quarter, depth),
+        pltpu.SemaphoreType.DMA((400,)), pltpu.SemaphoreType.DMA((400,)), pltpu.SemaphoreType.DMA((48,)),
+    ]
+    result, rows_grad, gain_grads, *grads = pl.pallas_call(
+        functools.partial(layer_body, groups, ranks),
+        out_shape=outs,
+        in_specs=[hbm] * 10 + [vmem] * 2,
+        out_specs=[hbm, hbm, vmem] + [hbm] * 7,
+        scratch_shapes=scratch,
+        compiler_params=pltpu.CompilerParams(
+            collective_id=1, has_side_effects=True, vmem_limit_bytes=VMEM_LIMIT
+        ),
+    )(*ins)
+    grads = [w.astype(F32) for w in grads]
+    return (result, rows_grad, gain_grads[0], *grads[:4], gain_grads[1], *grads[4:])
+
+
+def on_device(tokens, attn_gain, query_weight, *rest):
+    groups = query_weight.shape[1] // HD
+    ranks = lax.axis_size("seq") // groups
+    fits = lax.axis_size("head") == 4 and groups == 4 and ranks == 2 and query_weight.shape[0] % 128 == 0
+    plan = functools.partial(rows_plan, groups, ranks) if fits else gathered_weights
+    return plan(tokens, attn_gain, query_weight, *rest)
+
+
 def solution(mesh):
     in_specs = (
         P("seq", None),

time: 2390 us -> 364 us (0.15)
  waiting for transfers between devices: 2070 us -> 0 us
  Pallas kernels: 0 us -> 344 us
  matrix products: 129 us -> 0 us
  blocking collectives: 80.6 us -> 0 us
  local copies, waits for them, and re-layouts: 56 us -> 4.71 us
    reduce_scatter x9 -> x0, waiting for transfers between devices: 1360 us -> none  [the longest x1 287 us: on_device(): lax.psum_scatter(grad_gate, 'seq', scatter_dimension=0, tiled=True)]
    all_gather x9 -> x0, waiting for transfers between devices: 600 us -> none  [the longest x1 124 us: on_device(): lax.all_gather(gate_weight, 'seq', axis=0, tiled=True)]
    pallas_call x0 -> x1, Pallas kernels: none -> 344 us  [rows_plan(): pl.pallas_call(functools.partial(layer_body, groups, ranks), out_shape=ou...]
    dot_general x43 -> x0, matrix products: 123 us -> none  [the longest x1 10 us: on_device(): jnp.einsum('tk,tf->kf', normed_two, dup, preferred_element_type=jnp.float32)]
    psum x4 -> x0, waiting for transfers between devices: 111 us -> none  [the longest x1 41.9 us: on_device(): lax.psum(jnp.einsum('tf,kf->tk', dgate, gate_back, preferred_element_type...]
    all_gather x2 -> x0, blocking collectives: 41.7 us -> none  [the longest x1 22.3 us: on_device(): lax.all_gather(attn_gain, 'seq', axis=0, tiled=True)]
    unnamed x1 -> x0, blocking collectives: 38.8 us -> none
  transfers between devices with their start and end apart: 22 -> 0, of which waited for: 22 -> 0; matrix products, arithmetic and copies ran while one was open for 5% -> 0% of each run, Pallas kernels for 0% -> 0%
where the time goes in v3:
time: 364 us; the launch traced here: 363 us
  Pallas kernels  344 us (95%)
  other arithmetic  13.1 us (4%)
  local copies, waits for them, and re-layouts  4.71 us (1%)
    pallas_call x1, Pallas kernels, rows_plan(): pl.pallas_call(functools.partial(layer_body, groups, ranks), out_shape=ou...  344 us
    convert_element_type x7, other arithmetic, rows_plan(): grads = [w.astype(F32) for w in grads]  9.3 us

profile of v3, /device:TPU:0, one launch (start us, length us, event | category | flops | bytes accessed | tf_op | source)
XLA Modules:
  0.0 362.8 jit_solution(14806713174866270015)
XLA Ops:
  0.7 0.1 convert_bitcast_fusion
  0.8 3.1 fusion
  3.8 0.7 broadcast_in_dim.22
  4.5 0.7 broadcast_in_dim.23
  5.1 0.1 pad.2.clone
  5.2 0.7 maximum_convert_fusion.refs_2_
  5.9 344.2 %shard_map.194 = (bf16[256,2048]{1,0:T(8,128)(2,1)}, bf16[256,2048]{1,0:T(8,128)(2,1)}, f32[8,256]{1,0:T(8,128)}, bf16[256,512]{1,0:T(8,128)(2,1)}, bf16[256,512...) custom-call(bf16[256,2048]{1,0:T(8,128)(2,1)} %refs_0_.1, ...), custom_call_target="tpu_custom_call" | custom-call | tf_op jit(solution)/shard_map/pallas_call | solution.py:1236
  350.1 0.0 copy-start.1
  350.1 2.9 convert_element_type.49
  353.0 0.0 copy-start
  353.0 0.0 copy-done.1
  353.0 1.6 convert_element_type.50
  354.6 0.0 copy-start.7
  354.6 0.0 copy-start.6
  354.6 0.0 copy-done
  354.6 0.0 copy-start.5
  354.6 0.0 copy-start.4
  354.6 1.5 convert_element_type.51
  356.1 0.0 copy-start.3
  356.1 0.0 copy-done.7
  356.1 0.9 convert_element_type.45
  356.9 0.0 copy-done.6
  356.9 0.0 copy-start.2
  356.9 0.9 convert_element_type.46
  357.8 0.0 copy-done.5
  357.8 0.9 convert_element_type.47
  358.6 0.0 copy-done.4
  358.6 0.8 convert_element_type.48
  359.5 1.3 fusion.4
  360.8 0.0 copy-done.3
  360.8 1.0 copy.25
  361.8 0.0 copy-done.2
  361.8 1.0 copy.26
  (4 shorter events, 0.0 us)
Async XLA Ops:
  350.1 2.9 copy-start.1
  353.0 1.6 copy-start
  354.6 1.5 copy-start.7
  354.6 2.4 copy-start.6
  354.6 3.2 copy-start.5
  354.6 4.1 %copy-start.4 = (bf16[512,256]{1,0:T(8,128)(2,1)S(1)}, bf16[512,256]{1,0:T(8,128)(2,1)}, u32[]{:S(2)}) copy-start(bf16[512,256]{1,0:T(8,128)(2,1)} %get-tuple-element.27) | copy-start | bytes 786436
  356.1 4.8 %copy-start.3 = (bf16[256,2048]{1,0:T(8,128)(2,1)S(1)}, bf16[256,2048]{1,0:T(8,128)(2,1)}, u32[]{:S(2)}) copy-start(bf16[256,2048]{1,0:T(8,128)(2,1)} %get-tuple-element.48) | copy-start | bytes 3145732
  356.9 4.9 %copy-start.2 = (bf16[256,2048]{1,0:T(8,128)(2,1)S(1)}, bf16[256,2048]{1,0:T(8,128)(2,1)}, u32[]{:S(2)}) copy-start(bf16[256,2048]{1,0:T(8,128)(2,1)} %get-tuple-element.49) | copy-start | bytes 3145732

commit v4 on v3

--- a/solution.py
+++ b/solution.py
@@ -17,6 +17,7 @@
 epsilon = 1e-05
 block_limit = 512
 VMEM_LIMIT = 63 * 2**20
+SENDS, RECEIVES, KEEPS = 103, 213, 26
 
 
 def tables(offset, length, half_width):
@@ -292,46 +293,64 @@
 
 class Net:
     def __init__(self, send, receive):
-        self.send, self.receive, self.count, self.lots = send, receive, 0, []
-
-    def lot(self, size, describe):
-        return Lot(self, size, describe)
+        self.send, self.receive, self.sends, self.receives, self.lots = send, receive, 0, 0, []
+
+    def lot(self, *args, **options):
+        return Lot(self, *args, **options)
 
     def finish(self):
         for lot in self.lots:
-            for j in sorted(lot.open):
-                lot.sent(j)
+            lot.sent()
 
 
 class Lot:
-    def __init__(self, net, size, describe):
-        self.net, self.base, self.describe, self.open = net, net.count, describe, set()
-        net.count += size
+    def __init__(self, net, indices, describe, bulk, arrival=None, apart=False):
+        self.net, self.describe, self.bulk, self.arrival, self.apart = net, describe, bulk, arrival, apart
+        self.place = {j: net.receives + i for i, j in enumerate(indices)}
+        self.low = min(indices)
+        self.send_base, self.receive_base = net.sends, net.receives
+        net.receives += len(indices)
+        net.sends += len(indices) if apart else 1
+        self.started, self.open = set(), set()
         net.lots.append(self)
 
-    def copy(self, j):
-        source, target, device = self.describe(j)
-        return pltpu.make_async_remote_copy(
-            src_ref=source,
-            dst_ref=target,
-            send_sem=self.net.send.at[self.base + j],
-            recv_sem=self.net.receive.at[self.base + j],
-            device_id=device,
-            device_id_type=MESH,
-        )
-
-    def start(self, j):
-        self.copy(j).start()
+    def receive_at(self, j):
+        return self.net.receive.at[self.receive_base + (j - self.low)]
+
+    def send_at(self, j):
+        return self.net.send.at[self.send_base + (j - self.low if self.apart else 0)]
+
+    def start(self, j, pieces=None):
+        described = self.describe(j)
+        for i, (source, target, device) in enumerate(described if isinstance(described, list) else [described]):
+            if pieces is None or i in pieces:
+                pltpu.make_async_remote_copy(
+                    src_ref=source,
+                    dst_ref=target,
+                    send_sem=self.send_at(j),
+                    recv_sem=self.receive_at(j),
+                    device_id=device,
+                    device_id_type=MESH,
+                ).start()
         if isinstance(j, int):
-            self.open.add(j)
+            self.mark((j,))
+
+    def mark(self, indices):
+        self.started.update(indices)
+        self.open.update(indices if self.apart else (self.low,))
 
     def arrived(self, j):
-        self.copy(j).wait_recv()
-
-    def sent(self, j):
-        if j in self.open:
-            self.open.remove(j)
-            self.copy(j).wait_send()
+        described = self.describe(j)
+        target = self.arrival(j) if self.arrival else described[1]
+        self.wait(target, self.receive_at(j))
+
+    def wait(self, like, sem):
+        pltpu.make_async_copy(like, like, sem).wait()
+
+    def sent(self, j=None):
+        for k in sorted(self.open) if j is None else [j] if j in self.open else []:
+            self.open.remove(k)
+            self.wait(self.bulk(k) if self.apart else self.bulk, self.send_at(k))
 
 
 class Keep:
@@ -350,6 +369,7 @@
         self.s, self.h = lax.axis_index("seq"), lax.axis_index("head")
         self.g, self.r = self.s // ranks, self.s % ranks
         self.groups, self.ranks = groups, ranks
+        self.q = self.h % 2 * 2 + self.h // 2
 
     def along(self, m):
         return (self.s ^ (m * self.ranks), self.h)
@@ -385,18 +405,24 @@
         self.at, self.buffer, self.quarter, self.shared = at, buffer, quarter, own is not None
         first = self.block(0, 0) if own is None else own
         self.z = net.lot(
-            4,
+            (1, 2, 3),
             lambda m: (self.block(2, 0), self.block(2, 0), at.along(1))
             if m == 3
             else (first, self.block(0, 0), at.along(m)),
+            self.some(3),
         )
-        self.x = net.lot(4, lambda m: (self.block(m, 0), self.block(m, 0), at.across()))
-        self.c = net.lot(4, lambda m: (self.block(m, 0), self.block(m, 0), at.near()))
-        self.d = net.lot(4, lambda m: (self.block(m, 2), self.block(m, 2), at.near()))
+        indices = (1, 2, 3) if self.shared else (0, 1, 2, 3)
+        size = len(indices)
+        self.x = net.lot(indices, lambda m: (self.block(m, 0), self.block(m, 0), at.across()), self.some(size))
+        self.c = net.lot(indices, lambda m: (self.block(m, 0), self.block(m, 0), at.near()), self.some(size))
+        self.d = net.lot(indices, lambda m: (self.block(m, 1), self.block(m, 1), at.near()), self.some(size))
+
+    def some(self, size):
+        return self.buffer.at[0 : size * self.quarter, :]
 
     def block(self, m, k):
         at = self.at
-        return self.buffer.at[row(((at.g ^ m) * 4 + (at.h ^ k)) * self.quarter, self.quarter), :]
+        return self.buffer.at[row(((at.g ^ m) * 4 + (at.q ^ k)) * self.quarter, self.quarter), :]
 
     def pass_on(self, m):
         self.x.start(m)
@@ -422,36 +448,45 @@
         self.c.arrived(m)
         self.d.arrived(m)
 
-    def sent(self, m):
-        for lot in (self.x, self.c, self.d):
-            lot.sent(m)
-        if m == 2:
-            self.z.sent(3)
+    def sent(self):
+        for lot in (self.z, self.x, self.c, self.d):
+            lot.sent()
 
 
 class Collect:
     def __init__(self, net, at, refs, quarter, out):
         self.at, self.quarter, self.out = at, quarter, out
         self.part, self.near, self.xin, self.zin = refs
-        self.a = net.lot(4, lambda m: (self.part.at[self.rows(m, 3), :], self.near.at[at.g ^ m, 1], at.near()))
-        self.e = net.lot(4, lambda m: (self.part.at[self.rows(m, 1), :], self.near.at[at.g ^ m, 0], at.near()))
-        self.b = net.lot(4, lambda m: (self.part.at[self.rows(m, 2), :], self.xin.at[at.g ^ m], at.across()))
+        every = (0, 1, 2, 3)
+        self.a = net.lot(every, lambda m: (self.pair(m), self.near.at[at.g ^ m], at.near()), self.near)
+        self.b = net.lot(
+            every, lambda m: (self.part.at[self.rows(m, 1), :], self.xin.at[at.g ^ m], at.across()), self.xin
+        )
         hops = {3: (0, 1), 2: (2, 2), 1: (1, 1)}
         self.z = net.lot(
-            4, lambda m: (self.part.at[self.rows(m, 0), :], self.zin.at[hops[m][0]], at.along(hops[m][1]))
+            (1, 2, 3),
+            lambda m: (self.part.at[self.rows(m, 0), :], self.zin.at[hops[m][0]], at.along(hops[m][1])),
+            self.zin,
         )
 
     def rows(self, m, k):
         at = self.at
-        return row(((at.g ^ m) * 4 + (at.h ^ k)) * self.quarter, self.quarter)
+        return row(((at.g ^ m) * 4 + (at.q ^ k)) * self.quarter, self.quarter)
+
+    def pair(self, m):
+        at = self.at
+        return self.part.at[row(((at.g ^ m) * 2 + (1 - at.h % 2)) * 2 * self.quarter, 2 * self.quarter), :]
 
     def first(self, m):
         self.a.start(m)
-        self.e.start(m)
+
+    def lines(self, few, k):
+        start = (self.at.h // 2 ^ k) * self.quarter
+        return pl.ds(pl.multiple_of(start + few.start, 16), few.size)
 
     def slices(self, m, k, step):
         at = self.at
-        start = ((at.g ^ m) * 4 + (at.h ^ k)) * self.quarter
+        start = ((at.g ^ m) * 4 + (at.q ^ k)) * self.quarter
         each(self.quarter // 16, lambda i: step(row(start + i * 16, 16), row(i * 16, 16)))
 
     def second(self, m):
@@ -459,21 +494,20 @@
         self.a.arrived(m)
 
         def step(rows, few):
-            total = self.part[rows, :].astype(F32) + self.near[d, 1, few, :].astype(F32)
+            total = self.part[rows, :].astype(F32) + self.near[d, self.lines(few, 1), :].astype(F32)
             self.part[rows, :] = total.astype(BF16)
 
-        self.slices(m, 2, step)
+        self.slices(m, 1, step)
         self.b.start(m)
 
     def third(self, m):
         d = self.at.g ^ m
-        self.e.arrived(m)
         self.b.arrived(m)
         if m == 2:
             self.z.arrived(3)
 
         def step(rows, few):
-            total = self.part[rows, :].astype(F32) + self.near[d, 0, few, :].astype(F32)
+            total = self.part[rows, :].astype(F32) + self.near[d, self.lines(few, 0), :].astype(F32)
             total += self.xin[d, few, :].astype(F32)
             if m == 2:
                 total += self.zin[0, few, :].astype(F32)
@@ -505,59 +539,59 @@
                 self.second(m + 1)
 
         each(4, step)
-        for lot in (self.a, self.e):
-            lot.open.update(range(4))
-        self.b.open.update((1, 2, 3))
+        self.a.mark(range(4))
+        self.b.mark((1, 2, 3))
 
     def sent(self):
-        for m in range(4):
-            for lot in (self.a, self.e, self.b, self.z):
-                lot.sent(m)
+        for lot in (self.a, self.b, self.z):
+            lot.sent()
 
 
 class Turn:
     def __init__(self, net, keep, at, source, view, blocks):
         self.keep, self.at, self.source, self.view, self.blocks = keep, at, source, view, blocks
-        n = sum(len(items) for items, _ in blocks)
-        self.n = n
-        self.z = net.lot(
-            4 * n,
-            lambda j: (source(j % n, at.g ^ (j // n)), view(j % n, at.s), at.along(j // n)),
-        )
-        self.o = net.lot(n, lambda i: (source(i, at.g), view(i, at.s), at.beside()))
-        self.y = net.lot(4 * len(blocks), self.sent_on)
-        self.own = {}
-
-    def sent_on(self, j):
-        at = self.at
-        block = self.blocks[j // 4][1](at.s ^ (j % 4 * at.ranks))
-        return (block, block, at.beside())
-
-    def start(self, m, b=0):
-        for i in self.blocks[b][0]:
-            self.z.start(m * self.n + i)
+        self.z, self.o, self.y, self.own = [], [], [], {}
+        for b, (items, place) in enumerate(blocks):
+
+            def out(m, items=items):
+                return [(source(i, at.g ^ m), view(i, at.s), at.along(m)) for i in items]
+
+            def beside(m, items=items):
+                return [(source(i, at.g), view(i, at.s), at.beside()) for i in items]
+
+            def on(m, place=place):
+                block = place(at.s ^ (m * at.ranks))
+                return (block, block, at.beside())
+
+            def arrival(m, place=place):
+                return place(at.s ^ (m * at.ranks))
+
+            self.z.append(net.lot((1, 2, 3), out, lambda m, place=place: place(at.s), arrival, apart=True))
+            self.o.append(net.lot((0,), beside, place(at.s), arrival))
+            self.y.append(net.lot((1, 2, 3), on, lambda m, place=place: place(at.s), apart=True))
+
+    def start(self, m, b=0, pieces=None):
+        self.z[b].start(m, pieces)
 
     def mine(self, b=0):
         at = self.at
         for i in self.blocks[b][0]:
             self.own[i] = self.keep.put(self.source(i, at.g), self.view(i, at.s))
-            self.o.start(i)
+        self.o[b].start(0)
 
     def pass_on(self, m, b=0):
-        for i in self.blocks[b][0]:
-            self.z.arrived(m * self.n + i)
-        self.y.start(b * 4 + m)
+        self.z[b].arrived(m)
+        self.y[b].start(m)
 
     def ready(self, b=0):
         for i in self.blocks[b][0]:
             self.own[i].wait()
-            self.o.arrived(i)
+        self.o[b].arrived(0)
         for m in (1, 2, 3):
-            self.y.arrived(b * 4 + m)
+            self.y[b].arrived(m)
 
     def sent(self, b=0):
-        for m in (1, 2, 3):
-            self.y.sent(b * 4 + m)
+        self.y[b].sent()
 
 
 def dot(a, b):
@@ -581,13 +615,13 @@
 
 
 def layer_body(groups, ranks, *refs):
-    (tok, cot, gains, qw, kw, vw, ow, gw, uw, dw, cosines, sines) = refs[:12]
-    (result_out, rows_out, gains_out, q_out, k_out, v_out, o_out, g_out, u_out, d_out) = refs[12:22]
+    (tok, cot, gain_one, gain_two, qw, kw, vw, ow, gw, uw, dw) = refs[:11]
+    (result_out, rows_out, gains_out, q_out, k_out, v_out, o_out, g_out, u_out, d_out) = refs[11:21]
     (
-        gains_all, rows_one, rows_cot, rows_two, rows_dh, w_qkv, w_o, w_gu, w_d, queries, pairs, mix, dqkv, accum, pair_send,
+        gains, gains_all, cosines, sines, rows_one, rows_cot, rows_two, rows_dh, w_qkv, w_o, w_gu, w_d, queries, pairs, mix, dqkv, accum, pair_send,
         pair_in, mixed, dgu, dmixed, own_x, hidden, dhidden, summed, part_a, near_a, xin_a, zin_a, part_b, near_b, xin_b, zin_b,
         in_gu, in_d, in_qkv, in_o, gain_part, gain_in, gain_mid, gain_near, result_own, rows_own, send, receive, local,
-    ) = refs[22:]
+    ) = refs[21:]
     at = Where(groups, ranks)
     s, h, g, r = at.s, at.h, at.g, at.r
     shards = groups * ranks
@@ -640,17 +674,21 @@
         [((b,), lambda shard, b=b: w_d.at[b * half : (b + 1) * half, columns_of(shard)]) for b in (0, 1)],
     )
 
+    gains[...] = jnp.zeros_like(gains)
+    gains[0:1, :] = gain_one[...].astype(F32).reshape(1, width)
+    gains[1:2, :] = gain_two[...].astype(F32).reshape(1, width)
     gain_slot = gains_all.at[:, columns_of(s)]
-    gain_moves = net.lot(shards, lambda m: (gains, gain_slot, (s ^ m, h)))
+    gain_moves = net.lot(range(1, shards), lambda m: (gains, gain_slot, (s ^ m, h)), gain_in)
     for m in range(1, shards):
         gain_moves.start(m)
     gain_own = keep.put(gains, gain_slot)
-    strip = row(h * quarter, quarter)
+    strip = row(at.q * quarter, quarter)
     one = Spread(net, at, rows_one, quarter, tok.at[strip, :])
     one.start()
     own_rows = keep.put(tok, rows_one.at[chunk(0), :])
     own_strip = keep.put(tok.at[strip, :], own_x)
     turn_qkv.start(3)
+    turn_qkv.start(2)
     turn_qkv.mine()
     turn_o.mine()
     own_cot = keep.put(cot, rows_cot.at[chunk(0), :])
@@ -661,6 +699,19 @@
         accum[rows, :] = jnp.zeros_like(accum[rows, :])
 
     each(total_rows // 64, clear)
+
+    def tables(i):
+        rows = row(i * 64, 64)
+        first_row = (i // (count // 64) * ranks + r) * count + i % (count // 64) * 64
+        places = (first_row + lax.broadcasted_iota(jnp.int32, (64, HD), 0)).astype(F32)
+        lanes = lax.broadcasted_iota(jnp.int32, (64, HD), 1)
+        low_half = lanes < HD // 2
+        order = jnp.where(low_half, lanes, lanes - HD // 2).astype(F32)
+        angles = places * jnp.exp(order * (-math.log(10000.0) / (HD // 2)))
+        cosines[rows, :] = jnp.cos(angles)
+        sines[rows, :] = jnp.where(low_half, -jnp.sin(angles), jnp.sin(angles))
+
+    each(groups * count // 64, tables)
 
     gain_own.wait()
     for m in range(1, shards):
@@ -680,7 +731,6 @@
     norm_one(0)
     one.arrive(1)
     one.arrive(2)
-    turn_qkv.start(2)
     turn_qkv.start(1)
     for m in (3, 2, 1):
         turn_o.start(m)
@@ -688,20 +738,16 @@
     one.second(2)
     turn_qkv.pass_on(3)
     one.arrive(3)
+    turn_qkv.pass_on(2)
+    turn_qkv.pass_on(1)
     grad = Spread(net, at, rows_cot, quarter, cot.at[strip, :])
     grad.start()
-    one.ready(1)
-    one.sent(1)
-    norm_one(1)
-    one.ready(2)
-    one.sent(2)
-    norm_one(2)
-    turn_qkv.pass_on(1)
     one.second(3)
-    turn_qkv.pass_on(2)
-    one.ready(3)
-    one.sent(3)
-    norm_one(3)
+    for m in (1, 2, 3):
+        one.ready(m)
+    one.sent()
+    for m in (1, 2, 3):
+        norm_one(m)
     for m in (3, 2, 1):
         turn_d.start(m, 0)
     turn_qkv.ready()
@@ -709,7 +755,11 @@
     def own_place(m):
         return row(((g ^ m) * ranks + r) * count, count)
 
-    pair_moves = net.lot(4, lambda m: (pairs.at[own_place(m), :], pairs.at[own_place(m), :], at.beside()))
+    pair_moves = net.lot(
+        range(4),
+        lambda m: (pairs.at[own_place(m), :], pairs.at[own_place(m), :], at.beside()),
+        pairs.at[0 : groups * count, :],
+    )
 
     def project(m):
         rows, place = chunk(m), own_place(m)
@@ -721,20 +771,18 @@
         pair_moves.start(m)
 
     each(4, project)
-    pair_moves.open.update(range(4))
+    pair_moves.mark(range(4))
     for m in (3, 2, 1):
         turn_o.pass_on(m)
-    turn_gu.start(3, 0)
-    turn_gu.start(1, 0)
     for m in (3, 2, 1):
         turn_d.start(m, 1)
+    turn_gu.start(3, 0, (0,))
     grad.arrive(1)
     grad.arrive(2)
     turn_d.mine(0)
     turn_gu.mine(0)
     for m in (0, 1, 2, 3):
         pair_moves.arrived(m)
-    turn_o.ready()
     span = ranks * count
 
     def weights_of(m, j, query):
@@ -755,6 +803,11 @@
         total = lax.fori_loop(0, (g ^ m) + 1, step, jnp.zeros((count, HD), F32))
         low = total.astype(BF16)
         mix[rows, :] = low
+
+        @pl.when(m == 3)
+        def _():
+            turn_o.ready()
+
         part_a[rows, :] = dot(low, w_o[...]).astype(BF16)
 
     set_a, set_b = (part_a, near_a, xin_a, zin_a), (part_b, near_b, xin_b, zin_b)
@@ -762,19 +815,24 @@
     first.produce(attend)
     first.third(3)
     first.second(0)
-    turn_gu.start(1, 1)
+    turn_gu.start(1, 0)
     turn_d.mine(1)
     turn_gu.mine(1)
     for m in (3, 2, 1):
         turn_d.pass_on(m, 0)
     first.third(2)
+    turn_gu.start(3, 0, (1,))
     grad.second(1)
     grad.second(2)
     grad.arrive(3)
     first.third(1)
+    turn_gu.start(1, 1)
+    for m in (3, 2, 1):
+        turn_d.pass_on(m, 1)
+    turn_gu.pass_on(1, 0)
     first.last()
     two = Spread(net, at, rows_two, quarter)
-    mine_start = (g * 4 + h) * quarter
+    mine_start = (g * 4 + at.q) * quarter
 
     def norm_two(i):
         few = row(i * 16, 16)
@@ -786,15 +844,10 @@
     each(quarter // 16, norm_two)
     two.start()
     turn_gu.start(2, 0)
-    turn_gu.start(3, 1)
-    turn_gu.start(2, 1)
-    turn_gu.pass_on(3, 0)
-    turn_gu.pass_on(1, 0)
-    for m in (3, 2, 1):
-        turn_d.pass_on(m, 1)
     grad.second(3)
     two.second(0)
     two.arrive(1)
+    turn_gu.pass_on(3, 0)
     turn_gu.pass_on(1, 1)
     turn_d.ready(0)
     own_cot.wait()
@@ -807,12 +860,13 @@
         grad.ready(m)
     each(4, lambda m: early(m, 0))
     two.arrive(2)
+    for m in (3, 2):
+        turn_gu.start(m, 1)
     two.second(1)
     two.second(2)
     two.arrive(3)
     turn_gu.pass_on(2, 0)
     two.second(3)
-    turn_gu.pass_on(3, 1)
     for m in (0, 1, 2, 3):
         two.ready(m)
     turn_gu.ready(0)
@@ -856,25 +910,27 @@
     def several(groups_, work, lot):
         first_, last_ = groups_
         each(first_ - last_ + 1, lambda i: halves(first_ - i, work, lot))
-        lot.open.update(range(last_, first_ + 1))
-
-    def beside(source, target):
+        lot.mark(range(last_, first_ + 1))
+
+    def beside(source, target, bulk):
         def describe(m):
             d = g ^ m
             return (source(d * ranks + (r ^ 1)), target(d), at.beside())
 
-        return net.lot(4, describe)
+        return net.lot(range(4), describe, bulk)
 
     pairs_of = [slice(b * units, (b + 1) * units) for b in (0, 1)]
     lanes_of = [slice(b * half, (b + 1) * half) for b in (0, 1)]
     moves_gu = [
-        beside(lambda shard, p=p: w_gu.at[shard_rows(shard), p], lambda d, p=p: in_gu.at[d, :, p]) for p in pairs_of
+        beside(lambda shard, p=p: w_gu.at[shard_rows(shard), p], lambda d, p=p: in_gu.at[d, :, p], in_gu.at[:, :, p])
+        for p in pairs_of
     ]
     moves_d = [
-        beside(lambda shard, p=p: w_d.at[p, columns_of(shard)], lambda d, p=p: in_d.at[d, p, :]) for p in lanes_of
+        beside(lambda shard, p=p: w_d.at[p, columns_of(shard)], lambda d, p=p: in_d.at[d, p, :], in_d.at[:, p, :])
+        for p in lanes_of
     ]
-    moves_qkv = beside(lambda shard: w_qkv.at[shard_rows(shard), :], lambda d: in_qkv.at[d])
-    moves_o = beside(lambda shard: w_o.at[:, columns_of(shard)], lambda d: in_o.at[d])
+    moves_qkv = beside(lambda shard: w_qkv.at[shard_rows(shard), :], lambda d: in_qkv.at[d], in_qkv)
+    moves_o = beside(lambda shard: w_o.at[:, columns_of(shard)], lambda d: in_o.at[d], in_o)
 
     def grads_gu(groups_, b):
         def work(shard):
@@ -904,13 +960,13 @@
 
     final, final_own = [], []
 
-    def give(source, target, m):
+    def give(moves, whole_, m):
         if m:
-            lot = net.lot(1, lambda j: (source, target, at.along(m)))
+            lot = net.lot((0,), lambda j: [(a, b, at.along(m)) for a, b in moves], whole_, lambda j: whole_)
             lot.start(0)
             final.append(lot)
         else:
-            final_own.append(keep.put(source, target))
+            final_own.extend(keep.put(a, b) for a, b in moves)
 
     def sums(m, lot, mine_of, other_of, size):
         lot.arrived(m)
@@ -929,9 +985,11 @@
             m, moves_gu[b],
             lambda i: (w_gu, row(start + i * 32, 32), p), lambda i: (in_gu, d, row(i * 32, 32), p), width,
         )
+        moves = []
         for i, out in enumerate((g_out, u_out)):
             place = b * units + i * half
-            give(w_gu.at[row(start, width), place : place + half], out.at[:, lane(g * units + b * half, half)], m)
+            moves.append((w_gu.at[row(start, width), place : place + half], out.at[:, lane(g * units + b * half, half)]))
+        give(moves, w_gu.at[row(start, width), p], m)
 
     def sums_d(m, b):
         d, base = g ^ m, b * half
@@ -941,7 +999,8 @@
             lambda i: (w_d, row(base + i * 32, 32), columns),
             lambda i: (in_d, d, row(base + i * 32, 32), slice(None)), half,
         )
-        give(w_d.at[lanes_of[b], columns], d_out.at[row(g * units + base, half), :], m)
+        block = w_d.at[lanes_of[b], columns]
+        give([(block, d_out.at[row(g * units + base, half), :])], block, m)
 
     def sums_o(m):
         d = g ^ m
@@ -950,7 +1009,7 @@
             m, moves_o,
             lambda i: (w_o, row(i * 32, 32), columns), lambda i: (in_o, d, row(i * 32, 32), slice(None)), HD,
         )
-        give(w_o.at[:, columns], o_out.at[row(g * HD, HD), :], m)
+        give([(w_o.at[:, columns], o_out.at[row(g * HD, HD), :])], w_o.at[:, columns], m)
 
     def sums_qkv(m):
         d = g ^ m
@@ -960,34 +1019,42 @@
             lambda i: (w_qkv, row(start + i * 32, 32), slice(None)),
             lambda i: (in_qkv, d, row(i * 32, 32), slice(None)), width,
         )
-        for i, out in enumerate((q_out, k_out, v_out)):
-            give(w_qkv.at[row(start, width), i * HD : (i + 1) * HD], out.at[:, lane(g * HD, HD)], m)
+        moves = [
+            (w_qkv.at[row(start, width), i * HD : (i + 1) * HD], out.at[:, lane(g * HD, HD)])
+            for i, out in enumerate((q_out, k_out, v_out))
+        ]
+        give(moves, w_qkv.at[row(start, width), :], m)
 
     first.sent()
     second = Collect(net, at, set_a, quarter, summed)
     each(4, lambda m: feed(m, 0))
+    turn_gu.pass_on(3, 1)
     turn_gu.sent(0)
-    turn_gu.pass_on(2, 1)
-    grads_gu((3, 2), 0)
+    grads_gu((3, 3), 0)
     turn_d.ready(1)
     each(4, lambda m: early(m, 1))
+    turn_gu.pass_on(2, 1)
+    grads_gu((2, 1), 0)
     each(4, lambda m: out_part(m, 0))
     turn_d.sent(0)
-    grads_gu((1, 1), 0)
+    grads_d((3, 1), 0)
+    sums_gu(3, 0)
     turn_gu.ready(1)
     second.produce(lambda m: feed(m, 1))
+    sums_gu(2, 0)
     second.third(3)
-    sums_gu(3, 0)
     second.second(0)
+    sums_gu(1, 0)
     second.third(2)
-    sums_gu(2, 0)
     turn_gu.sent(1)
     turn_d.sent(1)
-    grads_d((3, 1), 0)
+    grads_gu((3, 2), 1)
     second.third(1)
-    grads_gu((3, 1), 1)
+    grads_gu((1, 1), 1)
     each(4, lambda m: out_part(m, 1))
-    sums_gu(1, 0)
+    out_sum = Collect(net, at, set_b, quarter, summed)
+    for m in (3, 2, 1, 0):
+        out_sum.first(m)
     second.last()
     three = Spread(net, at, rows_dh, quarter)
 
@@ -1011,20 +1078,22 @@
         sums_d(m, 0)
     grads_d((3, 1), 1)
     three.second(0)
+    out_sum.second(3)
+    out_sum.second(2)
+    for b in (0, 1):
+        grads_gu((0, 0), b)
     three.arrive(1)
+    for b in (0, 1):
+        grads_d((0, 0), b)
     three.arrive(2)
     sums_gu(3, 1)
+    out_sum.third(3)
     three.second(1)
-    for b in (0, 1):
-        grads_gu((0, 0), b)
+    three.second(2)
     sums_gu(2, 1)
-    three.second(2)
     three.arrive(3)
-    for b in (0, 1):
-        grads_d((0, 0), b)
-    out_sum = Collect(net, at, set_b, quarter, summed)
-    for m in (3, 2, 1, 0):
-        out_sum.first(m)
+    out_sum.second(1)
+    out_sum.second(0)
     sums_gu(1, 1)
     three.second(3)
 
@@ -1046,27 +1115,27 @@
         total = lax.fori_loop(0, (g ^ m) + 1, step, jnp.zeros((count, HD), F32))
         dqkv[rows, :HD] = turned(total * score_scale, cosines[rows, :], -sines[rows, :]).astype(BF16)
 
-    each(4, attend_back)
-    pair_back = net.lot(4, lambda m: (pair_send.at[g ^ m], pair_in.at[g ^ m], at.beside()))
-
-    def send_pair(i):
-        m = 3 - i
+    pair_back = net.lot(range(4), lambda m: (pair_send.at[g ^ m], pair_in.at[g ^ m], at.beside()), pair_send)
+
+    def send_pair(m):
         d = g ^ m
         rows = row((d * ranks + (r ^ 1)) * count, count)
         pair_send[d] = accum[rows, :].astype(BF16)
         pair_back.start(m)
 
-    each(4, send_pair)
-    pair_back.open.update(range(4))
-    for m in (3, 2, 1, 0):
-        out_sum.second(m)
+    def back_from_end(i):
+        m = g ^ (groups - 1 - i)
+        attend_back(m)
+        send_pair(m)
+
+    each(4, back_from_end)
+    pair_back.mark(range(4))
+    out_sum.third(2)
     for m in (3, 2, 1):
         sums_d(m, 1)
+    out_sum.third(1)
     turn_o.sent()
     grads_o((3, 0))
-    out_sum.third(3)
-    out_sum.third(2)
-    out_sum.third(1)
     second.sent()
     third = Collect(net, at, set_a, quarter, summed)
 
@@ -1081,13 +1150,16 @@
 
     third.produce(back_one)
     third.second(0)
+    third.third(3)
     turn_qkv.sent()
-    grads_qkv((3, 0))
-    third.third(3)
+    grads_qkv((3, 2))
     for m in (3, 2, 1):
         sums_o(m)
     third.third(2)
+    grads_qkv((1, 0))
     third.third(1)
+    for m in (3, 2):
+        sums_qkv(m)
     for b in (0, 1):
         sums_gu(0, b)
         sums_d(0, b)
@@ -1096,7 +1168,7 @@
     def share(source, target):
         place = target.at[strip, :]
         final_own.append(keep.put(source, place))
-        lot = net.lot(2, lambda j: (source, place, (at.near(), at.across())[j]))
+        lot = net.lot((0, 1), lambda j: (source, place, (at.near(), at.across())[j]), target.at[0 : 2 * quarter, :])
         lot.start(0)
         lot.start(1)
         ends.append((lot, target))
@@ -1105,13 +1177,11 @@
         lot, target = ends.pop()
         lot.arrived(1)
         final.append(lot)
-        block = target.at[row((h ^ 2) * quarter, quarter), :]
-        on = net.lot(1, lambda j: (block, block, at.near()))
+        block = target.at[row((at.q ^ 1) * quarter, quarter), :]
+        on = net.lot((0,), lambda j: (block, block, at.near()), block)
         on.start(0)
         final.append(on)
 
-    for m in (3, 2, 1, 0):
-        sums_qkv(m)
     out_sum.last()
 
     def result_rows(i):
@@ -1120,6 +1190,9 @@
 
     each(quarter // 16, result_rows)
     share(result_own, result_out)
+    sums_qkv(1)
+    sums_o(0)
+    sums_qkv(0)
     third.last()
 
     def back_rows(i, gain_grad):
@@ -1134,7 +1207,9 @@
         return gain_grad + jnp.sum(upstream * values * inverse, axis=0, keepdims=True)
 
     gain_part[0:1, :] = lax.fori_loop(0, quarter // 16, back_rows, jnp.zeros((1, depth), F32))
-    gain_sums = net.lot(shards, lambda m: (gain_part.at[:, columns_of(s ^ m)], gain_in.at[m - 1], (s ^ m, h)))
+    gain_sums = net.lot(
+        range(1, shards), lambda m: (gain_part.at[:, columns_of(s ^ m)], gain_in.at[m - 1], (s ^ m, h)), gain_in
+    )
     for m in range(1, shards):
         gain_sums.start(m)
     relay()
@@ -1144,10 +1219,9 @@
         gain_sums.arrived(m)
         total += gain_in[m - 1]
     gain_mid[...] = total
-    gain_ends = net.lot(4, lambda m: (gain_mid, gain_near.at[m - 1], (s, h ^ m)))
+    gain_ends = net.lot(range(1, 4), lambda m: (gain_mid, gain_near.at[m - 1], (s, h ^ m)), gain_near)
     for m in range(1, 4):
         gain_ends.start(m)
-    sums_o(0)
     relay()
     for m in range(1, 4):
         gain_ends.arrived(m)
@@ -1182,19 +1256,10 @@
     units = gate_weight.shape[1] // groups
     total_rows = count * shards
     here = groups * count
-    r = lax.axis_index("seq") % ranks
-    gains = jnp.concatenate([attn_gain[None], mlp_gain[None], jnp.zeros((6, width), BF16)]).astype(F32)
-    places = (
-        (jnp.arange(groups, dtype=jnp.int32) * ranks + r)[:, None] * count
-        + jnp.arange(count, dtype=jnp.int32)[None, :]
-    ).reshape(here)
-    lanes = jnp.arange(HD, dtype=jnp.int32)
-    half = HD // 2
-    frequency = jnp.exp((lanes % half).astype(F32) * (-math.log(10000.0) / half))
-    angles = places.astype(F32)[:, None] * frequency[None, :]
-    cosines = jnp.cos(angles)
-    sines = jnp.sin(angles) * jnp.where(lanes < half, -1.0, 1.0)[None, :]
-    ins = (tokens, cotangent, gains, query_weight, key_weight, value_weight, out_weight, gate_weight, up_weight, down_weight, cosines, sines)
+    ins = (
+        tokens, cotangent, attn_gain, mlp_gain,
+        query_weight, key_weight, value_weight, out_weight, gate_weight, up_weight, down_weight,
+    )
     shape = jax.ShapeDtypeStruct
     hbm, vmem = pl.BlockSpec(memory_space=pl.ANY), pl.BlockSpec(memory_space=pltpu.VMEM)
     owners = (query_weight, key_weight, value_weight, out_weight, gate_weight, up_weight, down_weight)
@@ -1214,13 +1279,13 @@
     def collector():
         return [
             low(here, depth),
-            low(groups, 2, quarter, depth),
+            low(groups, 2 * quarter, depth),
             low(groups, quarter, depth),
             low(3, quarter, depth),
         ]
 
     scratch = [
-        full(8, depth),
+        full(8, width), full(8, depth), full(here, HD), full(here, HD),
         low(here, depth), low(here, depth), low(here, depth), low(here, depth),
         low(depth, 3 * HD), low(HD, depth), low(depth, 2 * units), low(units, depth),
         low(here, HD), low(total_rows, 2 * HD), low(here, HD), low(here, 3 * HD),
@@ -1231,20 +1296,46 @@
         low(groups, width, 2 * units), low(groups, units, width), low(groups, width, 3 * HD), low(groups, HD, width),
         full(8, depth), full(shards - 1, 8, width), full(8, width), full(3, 8, width),
         low(quarter, depth), low(quarter, depth),
-        pltpu.SemaphoreType.DMA((400,)), pltpu.SemaphoreType.DMA((400,)), pltpu.SemaphoreType.DMA((48,)),
+        pltpu.SemaphoreType.DMA((SENDS,)), pltpu.SemaphoreType.DMA((RECEIVES,)), pltpu.SemaphoreType.DMA((KEEPS,)),
     ]
-    result, rows_grad, gain_grads, *grads = pl.pallas_call(
+    moved = pl.pallas_call(
         functools.partial(layer_body, groups, ranks),
         out_shape=outs,
-        in_specs=[hbm] * 10 + [vmem] * 2,
+        in_specs=[hbm] * 2 + [vmem] * 2 + [hbm] * 7,
         out_specs=[hbm, hbm, vmem] + [hbm] * 7,
         scratch_shapes=scratch,
         compiler_params=pltpu.CompilerParams(
             collective_id=1, has_side_effects=True, vmem_limit_bytes=VMEM_LIMIT
         ),
     )(*ins)
-    grads = [w.astype(F32) for w in grads]
-    return (result, rows_grad, gain_grads[0], *grads[:4], gain_grads[1], *grads[4:])
+    steps = 8
+
+    def sliced(array):
+        rows, columns = array.shape
+        return pl.BlockSpec((rows // steps, columns), lambda i: (i, 0))
+
+    gain_specs = [pl.BlockSpec((8, width), lambda i: (0, 0))]
+    row_spec = pl.BlockSpec((width,), lambda i: (0,))
+    specs = [sliced(moved[0]), sliced(moved[1]), *(sliced(w) for w in moved[3:])]
+    gain_row = shape((width,), F32)
+    one, two, result, rows_grad, *grads = pl.pallas_call(
+        cast_body,
+        grid=(steps,),
+        out_shape=[gain_row, gain_row, moved[0], moved[1], *(shape(w.shape, F32) for w in owners)],
+        in_specs=gain_specs + specs,
+        out_specs=[row_spec, row_spec] + specs,
+        compiler_params=pltpu.CompilerParams(vmem_limit_bytes=VMEM_LIMIT),
+    )(moved[2], moved[0], moved[1], *moved[3:])
+    return (result, rows_grad, one, *grads[:4], two, *grads[4:])
+
+
+def cast_body(*refs):
+    inputs = len(refs) // 2
+    gains, sources, (one, two, *targets) = refs[0], refs[1:inputs], refs[inputs:]
+    one[...] = gains[0, :]
+    two[...] = gains[1, :]
+    for source, target in zip(sources, targets):
+        target[...] = source[...].astype(target.dtype)
 
 
 def on_device(tokens, attn_gain, query_weight, *rest):

time: 364 us -> 336 us (0.923)
  other arithmetic: 13.1 us -> 0 us
  Pallas kernels: 344 us -> 335 us
  local copies, waits for them, and re-layouts: 4.71 us -> 0 us
    pallas_call x1, Pallas kernels: 344 us -> 326 us  [rows_plan(): pl.pallas_call(functools.partial(layer_body, groups, ranks), out_shape=ou...]
    convert_element_type x8 -> x0, other arithmetic: 9.98 us -> none  [the longest x7 9.3 us: rows_plan(): grads = [w.astype(F32) for w in grads]]
    pallas_call x0 -> x1, Pallas kernels: none -> 8.77 us  [rows_plan(): pl.pallas_call(cast_body, grid=(steps,), out_shape=[gain_row, gain_row, m...]
where the time goes in v4:
time: 336 us; the launch traced here: 335 us
  Pallas kernels  335 us (100%)
    pallas_call x1, Pallas kernels, rows_plan(): pl.pallas_call(functools.partial(layer_body, groups, ranks), out_shape=ou...  326 us
    pallas_call x1, Pallas kernels, rows_plan(): pl.pallas_call(cast_body, grid=(steps,), out_shape=[gain_row, gain_row, m...  8.77 us

profile of v4, /device:TPU:0, one launch (start us, length us, event | category | flops | bytes accessed | tf_op | source)
XLA Modules:
  0.0 335.3 jit_solution(10692111836569600492)
XLA Ops:
  0.6 325.9 %shard_map.194 = (bf16[256,2048]{1,0:T(8,128)(2,1)}, bf16[256,2048]{1,0:T(8,128)(2,1)}, f32[8,256]{1,0:T(8,128)}, bf16[256,512]{1,0:T(8,128)(2,1)}, bf16[256,512...) custom-call(bf16[256,2048]{1,0:T(8,128)(2,1)} %refs_0_.1, ...), custom_call_target="tpu_custom_call" | custom-call | tf_op jit(solution)/shard_map/pallas_call | solution.py:1301
  326.6 8.8 %shard_map.195 = (f32[256]{0:T(256)}, f32[256]{0:T(256)}, bf16[256,2048]{1,0:T(8,128)(2,1)}, bf16[256,2048]{1,0:T(8,128)(2,1)}, f32[256,512]{1,0:T(8,128)}, /*in...) custom-call(f32[8,256]{1,0:T(8,128)} %get-tuple-element.32.refs_0_, ...), custom_call_target="tpu_custom_call" | custom-call | tf_op jit(solution)/shard_map/pallas_call | solution.py:1321

commit v5 on v4

--- a/solution.py
+++ b/solution.py
@@ -17,7 +17,8 @@
 epsilon = 1e-05
 block_limit = 512
 VMEM_LIMIT = 63 * 2**20
-SENDS, RECEIVES, KEEPS = 103, 213, 26
+SENDS, RECEIVES, KEEPS = 103, 295, 26
+PIECES = 2
 
 
 def tables(offset, length, half_width):
@@ -403,50 +404,64 @@
 class Spread:
     def __init__(self, net, at, buffer, quarter, own=None):
         self.at, self.buffer, self.quarter, self.shared = at, buffer, quarter, own is not None
-        first = self.block(0, 0) if own is None else own
-        self.z = net.lot(
-            (1, 2, 3),
-            lambda m: (self.block(2, 0), self.block(2, 0), at.along(1))
-            if m == 3
-            else (first, self.block(0, 0), at.along(m)),
-            self.some(3),
-        )
-        indices = (1, 2, 3) if self.shared else (0, 1, 2, 3)
-        size = len(indices)
-        self.x = net.lot(indices, lambda m: (self.block(m, 0), self.block(m, 0), at.across()), self.some(size))
-        self.c = net.lot(indices, lambda m: (self.block(m, 0), self.block(m, 0), at.near()), self.some(size))
-        self.d = net.lot(indices, lambda m: (self.block(m, 1), self.block(m, 1), at.near()), self.some(size))
-
-    def some(self, size):
-        return self.buffer.at[0 : size * self.quarter, :]
-
-    def block(self, m, k):
+        self.size = quarter // PIECES
+
+        def along(j):
+            m, p = j // PIECES, j % PIECES
+            if m == 3:
+                return (self.block(2, 0, p), self.block(2, 0, p), at.along(1))
+            first = self.block(0, 0, p) if own is None else own.at[row(at.q * quarter + p * self.size, self.size), :]
+            return (first, self.block(0, 0, p), at.along(m))
+
+        def moved(k, device):
+            def describe(j):
+                block = self.block(j // PIECES, k, j % PIECES)
+                return (block, block, device)
+
+            return describe
+
+        low = 1 if self.shared else 0
+        indices = range(low * PIECES, 4 * PIECES)
+        some = buffer.at[0 : (4 - low) * quarter, :]
+        self.z = net.lot(range(PIECES, 4 * PIECES), along, buffer.at[0 : 3 * quarter, :])
+        self.x = net.lot(indices, moved(0, at.across()), some)
+        self.c = net.lot(indices, moved(0, at.near()), some)
+        self.d = net.lot(indices, moved(1, at.near()), some)
+
+    def block(self, m, k, p):
         at = self.at
-        return self.buffer.at[row(((at.g ^ m) * 4 + (at.q ^ k)) * self.quarter, self.quarter), :]
-
-    def pass_on(self, m):
-        self.x.start(m)
-        self.c.start(m)
+        start = ((at.g ^ m) * 4 + (at.q ^ k)) * self.quarter + p * self.size
+        return self.buffer.at[row(start, self.size), :]
+
+    def pass_on(self, j):
+        self.x.start(j)
+        self.c.start(j)
 
     def start(self):
-        self.z.start(2)
-        self.z.start(1)
+        for m in (2, 1):
+            for p in range(PIECES):
+                self.z.start(m * PIECES + p)
         if not self.shared:
-            self.pass_on(0)
+            for p in range(PIECES):
+                self.pass_on(p)
 
     def arrive(self, m):
-        self.z.arrived(m)
-        if m == 2:
-            self.z.start(3)
-        self.pass_on(m)
+        for p in range(PIECES):
+            j = m * PIECES + p
+            self.z.arrived(j)
+            if m == 2:
+                self.z.start(3 * PIECES + p)
+            self.pass_on(j)
 
     def second(self, m):
-        self.x.arrived(m)
-        self.d.start(m)
+        for p in range(PIECES):
+            self.x.arrived(m * PIECES + p)
+            self.d.start(m * PIECES + p)
 
     def ready(self, m):
-        self.c.arrived(m)
-        self.d.arrived(m)
+        for p in range(PIECES):
+            self.c.arrived(m * PIECES + p)
+            self.d.arrived(m * PIECES + p)
 
     def sent(self):
         for lot in (self.z, self.x, self.c, self.d):
@@ -456,22 +471,29 @@
 class Collect:
     def __init__(self, net, at, refs, quarter, out):
         self.at, self.quarter, self.out = at, quarter, out
+        self.size = quarter // PIECES
         self.part, self.near, self.xin, self.zin = refs
-        every = (0, 1, 2, 3)
-        self.a = net.lot(every, lambda m: (self.pair(m), self.near.at[at.g ^ m], at.near()), self.near)
-        self.b = net.lot(
-            every, lambda m: (self.part.at[self.rows(m, 1), :], self.xin.at[at.g ^ m], at.across()), self.xin
-        )
+        self.a = net.lot(range(4), lambda m: (self.pair(m), self.near.at[at.g ^ m], at.near()), self.near)
+
+        def across(j):
+            m, few = j // PIECES, row(j % PIECES * self.size, self.size)
+            return (self.part.at[self.rows(m, 1, j % PIECES), :], self.xin.at[at.g ^ m, few, :], at.across())
+
         hops = {3: (0, 1), 2: (2, 2), 1: (1, 1)}
-        self.z = net.lot(
-            (1, 2, 3),
-            lambda m: (self.part.at[self.rows(m, 0), :], self.zin.at[hops[m][0]], at.along(hops[m][1])),
-            self.zin,
-        )
-
-    def rows(self, m, k):
+
+        def along(j):
+            (slot, hop), few = hops[j // PIECES], row(j % PIECES * self.size, self.size)
+            return (self.part.at[self.rows(j // PIECES, 0, j % PIECES), :], self.zin.at[slot, few, :], at.along(hop))
+
+        self.b = net.lot(range(4 * PIECES), across, self.xin)
+        self.z = net.lot(range(PIECES, 4 * PIECES), along, self.zin)
+
+    def start_of(self, m, k, p):
         at = self.at
-        return row(((at.g ^ m) * 4 + (at.q ^ k)) * self.quarter, self.quarter)
+        return ((at.g ^ m) * 4 + (at.q ^ k)) * self.quarter + p * self.size
+
+    def rows(self, m, k, p):
+        return row(self.start_of(m, k, p), self.size)
 
     def pair(self, m):
         at = self.at
@@ -484,10 +506,9 @@
         start = (self.at.h // 2 ^ k) * self.quarter
         return pl.ds(pl.multiple_of(start + few.start, 16), few.size)
 
-    def slices(self, m, k, step):
-        at = self.at
-        start = ((at.g ^ m) * 4 + (at.q ^ k)) * self.quarter
-        each(self.quarter // 16, lambda i: step(row(start + i * 16, 16), row(i * 16, 16)))
+    def slices(self, m, k, p, step):
+        start = self.start_of(m, k, p)
+        each(self.size // 16, lambda i: step(row(start + i * 16, 16), row(p * self.size + i * 16, 16)))
 
     def second(self, m):
         d = self.at.g ^ m
@@ -497,14 +518,12 @@
             total = self.part[rows, :].astype(F32) + self.near[d, self.lines(few, 1), :].astype(F32)
             self.part[rows, :] = total.astype(BF16)
 
-        self.slices(m, 1, step)
-        self.b.start(m)
+        for p in range(PIECES):
+            self.slices(m, 1, p, step)
+            self.b.start(m * PIECES + p)
 
     def third(self, m):
         d = self.at.g ^ m
-        self.b.arrived(m)
-        if m == 2:
-            self.z.arrived(3)
 
         def step(rows, few):
             total = self.part[rows, :].astype(F32) + self.near[d, self.lines(few, 0), :].astype(F32)
@@ -516,14 +535,19 @@
             else:
                 self.out[few, :] = total
 
-        self.slices(m, 0, step)
-        if m:
-            self.z.start(m)
+        for p in range(PIECES):
+            self.b.arrived(m * PIECES + p)
+            if m == 2:
+                self.z.arrived(3 * PIECES + p)
+            self.slices(m, 0, p, step)
+            if m:
+                self.z.start(m * PIECES + p)
 
     def last(self):
         self.third(0)
-        self.z.arrived(1)
-        self.z.arrived(2)
+        for m in (1, 2):
+            for p in range(PIECES):
+                self.z.arrived(m * PIECES + p)
 
     def total(self, few):
         return self.out[few, :] + self.zin[1, few, :].astype(F32) + self.zin[2, few, :].astype(F32)
@@ -540,7 +564,7 @@
 
         each(4, step)
         self.a.mark(range(4))
-        self.b.mark((1, 2, 3))
+        self.b.mark(range(PIECES, 4 * PIECES))
 
     def sent(self):
         for lot in (self.a, self.b, self.z):
@@ -683,7 +707,7 @@
         gain_moves.start(m)
     gain_own = keep.put(gains, gain_slot)
     strip = row(at.q * quarter, quarter)
-    one = Spread(net, at, rows_one, quarter, tok.at[strip, :])
+    one = Spread(net, at, rows_one, quarter, tok)
     one.start()
     own_rows = keep.put(tok, rows_one.at[chunk(0), :])
     own_strip = keep.put(tok.at[strip, :], own_x)
@@ -740,7 +764,7 @@
     one.arrive(3)
     turn_qkv.pass_on(2)
     turn_qkv.pass_on(1)
-    grad = Spread(net, at, rows_cot, quarter, cot.at[strip, :])
+    grad = Spread(net, at, rows_cot, quarter, cot)
     grad.start()
     one.second(3)
     for m in (1, 2, 3):
@@ -774,9 +798,7 @@
     pair_moves.mark(range(4))
     for m in (3, 2, 1):
         turn_o.pass_on(m)
-    for m in (3, 2, 1):
-        turn_d.start(m, 1)
-    turn_gu.start(3, 0, (0,))
+    turn_gu.start(3, 0)
     grad.arrive(1)
     grad.arrive(2)
     turn_d.mine(0)
@@ -821,14 +843,12 @@
     for m in (3, 2, 1):
         turn_d.pass_on(m, 0)
     first.third(2)
-    turn_gu.start(3, 0, (1,))
+    turn_gu.pass_on(3, 0)
     grad.second(1)
     grad.second(2)
     grad.arrive(3)
     first.third(1)
-    turn_gu.start(1, 1)
-    for m in (3, 2, 1):
-        turn_d.pass_on(m, 1)
+    turn_gu.start(2, 0)
     turn_gu.pass_on(1, 0)
     first.last()
     two = Spread(net, at, rows_two, quarter)
@@ -843,12 +863,12 @@
 
     each(quarter // 16, norm_two)
     two.start()
-    turn_gu.start(2, 0)
+    for m in (3, 2, 1):
+        turn_d.start(m, 1)
     grad.second(3)
     two.second(0)
+    turn_gu.pass_on(2, 0)
     two.arrive(1)
-    turn_gu.pass_on(3, 0)
-    turn_gu.pass_on(1, 1)
     turn_d.ready(0)
     own_cot.wait()
 
@@ -860,12 +880,13 @@
         grad.ready(m)
     each(4, lambda m: early(m, 0))
     two.arrive(2)
-    for m in (3, 2):
+    for m in (3, 2, 1):
         turn_gu.start(m, 1)
     two.second(1)
     two.second(2)
     two.arrive(3)
-    turn_gu.pass_on(2, 0)
+    for m in (3, 2, 1):
+        turn_d.pass_on(m, 1)
     two.second(3)
     for m in (0, 1, 2, 3):
         two.ready(m)
@@ -1033,12 +1054,13 @@
     grads_gu((3, 3), 0)
     turn_d.ready(1)
     each(4, lambda m: early(m, 1))
+    each(4, lambda m: out_part(m, 0))
+    turn_gu.pass_on(1, 1)
     turn_gu.pass_on(2, 1)
+    turn_d.sent(0)
+    sums_gu(3, 0)
     grads_gu((2, 1), 0)
-    each(4, lambda m: out_part(m, 0))
-    turn_d.sent(0)
     grads_d((3, 1), 0)
-    sums_gu(3, 0)
     turn_gu.ready(1)
     second.produce(lambda m: feed(m, 1))
     sums_gu(2, 0)

time: 336 us -> 331 us (0.985)
  Pallas kernels: 335 us -> 330 us
    pallas_call x1, Pallas kernels: 326 us -> 321 us  [rows_plan(): pl.pallas_call(functools.partial(layer_body, groups, ranks), out_shape=ou...]
where the time goes in v5:
time: 331 us; the launch traced here: 330 us
  Pallas kernels  330 us (100%)
    pallas_call x1, Pallas kernels, rows_plan(): pl.pallas_call(functools.partial(layer_body, groups, ranks), out_shape=ou...  321 us
    pallas_call x1, Pallas kernels, rows_plan(): pl.pallas_call(cast_body, grid=(steps,), out_shape=[gain_row, gain_row, m...  8.77 us

profile of v5, /device:TPU:0, one launch (start us, length us, event | category | flops | bytes accessed | tf_op | source)
XLA Modules:
  0.0 330.5 jit_solution(726430575742070705)
XLA Ops:
  0.6 320.9 %shard_map.194 = (bf16[256,2048]{1,0:T(8,128)(2,1)}, bf16[256,2048]{1,0:T(8,128)(2,1)}, f32[8,256]{1,0:T(8,128)}, bf16[256,512]{1,0:T(8,128)(2,1)}, bf16[256,512...) custom-call(bf16[256,2048]{1,0:T(8,128)(2,1)} %refs_0_.1, ...), custom_call_target="tpu_custom_call" | custom-call | tf_op jit(solution)/shard_map/pallas_call | solution.py:1323
  321.5 8.8 %shard_map.195 = (f32[256]{0:T(256)}, f32[256]{0:T(256)}, bf16[256,2048]{1,0:T(8,128)(2,1)}, bf16[256,2048]{1,0:T(8,128)(2,1)}, f32[256,512]{1,0:T(8,128)}, /*in...) custom-call(f32[8,256]{1,0:T(8,128)} %get-tuple-element.32.refs_0_, ...), custom_call_target="tpu_custom_call" | custom-call | tf_op jit(solution)/shard_map/pallas_call | solution.py:1343

commit v6 on v5

--- a/solution.py
+++ b/solution.py
@@ -698,31 +698,24 @@
         [((b,), lambda shard, b=b: w_d.at[b * half : (b + 1) * half, columns_of(shard)]) for b in (0, 1)],
     )
 
-    gains[...] = jnp.zeros_like(gains)
-    gains[0:1, :] = gain_one[...].astype(F32).reshape(1, width)
-    gains[1:2, :] = gain_two[...].astype(F32).reshape(1, width)
     gain_slot = gains_all.at[:, columns_of(s)]
     gain_moves = net.lot(range(1, shards), lambda m: (gains, gain_slot, (s ^ m, h)), gain_in)
-    for m in range(1, shards):
-        gain_moves.start(m)
-    gain_own = keep.put(gains, gain_slot)
     strip = row(at.q * quarter, quarter)
+    mine_start = (g * 4 + at.q) * quarter
+    span = ranks * count
     one = Spread(net, at, rows_one, quarter, tok)
-    one.start()
-    own_rows = keep.put(tok, rows_one.at[chunk(0), :])
-    own_strip = keep.put(tok.at[strip, :], own_x)
-    turn_qkv.start(3)
-    turn_qkv.start(2)
-    turn_qkv.mine()
-    turn_o.mine()
-    own_cot = keep.put(cot, rows_cot.at[chunk(0), :])
-    gain_part[...] = jnp.zeros_like(gain_part)
+    grad = Spread(net, at, rows_cot, quarter, cot)
+    two = Spread(net, at, rows_two, quarter)
+    three = Spread(net, at, rows_dh, quarter)
+    set_a, set_b = (part_a, near_a, xin_a, zin_a), (part_b, near_b, xin_b, zin_b)
+    first = Collect(net, at, set_a, quarter, summed)
+    second = Collect(net, at, set_a, quarter, summed)
+    out_sum = Collect(net, at, set_b, quarter, summed)
+    third = Collect(net, at, set_a, quarter, summed)
 
     def clear(i):
         rows = row(i * 64, 64)
         accum[rows, :] = jnp.zeros_like(accum[rows, :])
-
-    each(total_rows // 64, clear)
 
     def tables(i):
         rows = row(i * 64, 64)
@@ -735,12 +728,6 @@
         cosines[rows, :] = jnp.cos(angles)
         sines[rows, :] = jnp.where(low_half, -jnp.sin(angles), jnp.sin(angles))
 
-    each(groups * count // 64, tables)
-
-    gain_own.wait()
-    for m in range(1, shards):
-        gain_moves.arrived(m)
-
     def norm_one(m):
         def some(i):
             rows = row((g ^ m) * count + i * 32, 32)
@@ -749,32 +736,6 @@
             rows_one[rows, :] = (values * inverse * gains_all[0:1, :]).astype(BF16)
 
         each(count // 32, some)
-
-    own_rows.wait()
-    own_strip.wait()
-    norm_one(0)
-    one.arrive(1)
-    one.arrive(2)
-    turn_qkv.start(1)
-    for m in (3, 2, 1):
-        turn_o.start(m)
-    one.second(1)
-    one.second(2)
-    turn_qkv.pass_on(3)
-    one.arrive(3)
-    turn_qkv.pass_on(2)
-    turn_qkv.pass_on(1)
-    grad = Spread(net, at, rows_cot, quarter, cot)
-    grad.start()
-    one.second(3)
-    for m in (1, 2, 3):
-        one.ready(m)
-    one.sent()
-    for m in (1, 2, 3):
-        norm_one(m)
-    for m in (3, 2, 1):
-        turn_d.start(m, 0)
-    turn_qkv.ready()
 
     def own_place(m):
         return row(((g ^ m) * ranks + r) * count, count)
@@ -794,19 +755,6 @@
         pairs[place, HD:] = heads[:, 2 * HD :].astype(BF16)
         pair_moves.start(m)
 
-    each(4, project)
-    pair_moves.mark(range(4))
-    for m in (3, 2, 1):
-        turn_o.pass_on(m)
-    turn_gu.start(3, 0)
-    grad.arrive(1)
-    grad.arrive(2)
-    turn_d.mine(0)
-    turn_gu.mine(0)
-    for m in (0, 1, 2, 3):
-        pair_moves.arrived(m)
-    span = ranks * count
-
     def weights_of(m, j, query):
         keys = pairs[row(j * span, span), :HD]
         scores = dot_nt(query, keys) * score_scale - score_shift
@@ -832,28 +780,6 @@
 
         part_a[rows, :] = dot(low, w_o[...]).astype(BF16)
 
-    set_a, set_b = (part_a, near_a, xin_a, zin_a), (part_b, near_b, xin_b, zin_b)
-    first = Collect(net, at, set_a, quarter, summed)
-    first.produce(attend)
-    first.third(3)
-    first.second(0)
-    turn_gu.start(1, 0)
-    turn_d.mine(1)
-    turn_gu.mine(1)
-    for m in (3, 2, 1):
-        turn_d.pass_on(m, 0)
-    first.third(2)
-    turn_gu.pass_on(3, 0)
-    grad.second(1)
-    grad.second(2)
-    grad.arrive(3)
-    first.third(1)
-    turn_gu.start(2, 0)
-    turn_gu.pass_on(1, 0)
-    first.last()
-    two = Spread(net, at, rows_two, quarter)
-    mine_start = (g * 4 + at.q) * quarter
-
     def norm_two(i):
         few = row(i * 16, 16)
         values = own_x[few, :].astype(F32) + first.total(few)
@@ -861,36 +787,9 @@
         inverse = lax.rsqrt(mean_square(values) + epsilon)
         rows_two[row(mine_start + i * 16, 16), :] = (values * inverse * gains_all[1:2, :]).astype(BF16)
 
-    each(quarter // 16, norm_two)
-    two.start()
-    for m in (3, 2, 1):
-        turn_d.start(m, 1)
-    grad.second(3)
-    two.second(0)
-    turn_gu.pass_on(2, 0)
-    two.arrive(1)
-    turn_d.ready(0)
-    own_cot.wait()
-
     def early(m, b):
         lanes = slice(b * half, (b + 1) * half)
         dmixed[chunk(m), lanes] = dot_nt(rows_cot[chunk(m), :], w_d[lanes, :])
-
-    for m in (1, 2, 3):
-        grad.ready(m)
-    each(4, lambda m: early(m, 0))
-    two.arrive(2)
-    for m in (3, 2, 1):
-        turn_gu.start(m, 1)
-    two.second(1)
-    two.second(2)
-    two.arrive(3)
-    for m in (3, 2, 1):
-        turn_d.pass_on(m, 1)
-    two.second(3)
-    for m in (0, 1, 2, 3):
-        two.ready(m)
-    turn_gu.ready(0)
 
     def feed(m, b):
         rows = chunk(m)
@@ -1046,40 +945,6 @@
         ]
         give(moves, w_qkv.at[row(start, width), :], m)
 
-    first.sent()
-    second = Collect(net, at, set_a, quarter, summed)
-    each(4, lambda m: feed(m, 0))
-    turn_gu.pass_on(3, 1)
-    turn_gu.sent(0)
-    grads_gu((3, 3), 0)
-    turn_d.ready(1)
-    each(4, lambda m: early(m, 1))
-    each(4, lambda m: out_part(m, 0))
-    turn_gu.pass_on(1, 1)
-    turn_gu.pass_on(2, 1)
-    turn_d.sent(0)
-    sums_gu(3, 0)
-    grads_gu((2, 1), 0)
-    grads_d((3, 1), 0)
-    turn_gu.ready(1)
-    second.produce(lambda m: feed(m, 1))
-    sums_gu(2, 0)
-    second.third(3)
-    second.second(0)
-    sums_gu(1, 0)
-    second.third(2)
-    turn_gu.sent(1)
-    turn_d.sent(1)
-    grads_gu((3, 2), 1)
-    second.third(1)
-    grads_gu((1, 1), 1)
-    each(4, lambda m: out_part(m, 1))
-    out_sum = Collect(net, at, set_b, quarter, summed)
-    for m in (3, 2, 1, 0):
-        out_sum.first(m)
-    second.last()
-    three = Spread(net, at, rows_dh, quarter)
-
     def back_two(i, gain_grad):
         few = row(i * 16, 16)
         own = row(mine_start + i * 16, 16)
@@ -1094,31 +959,6 @@
         rows_dh[own, :] = total.astype(BF16)
         return gain_grad + jnp.sum(upstream * values * inverse, axis=0, keepdims=True)
 
-    gain_part[1:2, :] = lax.fori_loop(0, quarter // 16, back_two, jnp.zeros((1, depth), F32))
-    three.start()
-    for m in (3, 2, 1):
-        sums_d(m, 0)
-    grads_d((3, 1), 1)
-    three.second(0)
-    out_sum.second(3)
-    out_sum.second(2)
-    for b in (0, 1):
-        grads_gu((0, 0), b)
-    three.arrive(1)
-    for b in (0, 1):
-        grads_d((0, 0), b)
-    three.arrive(2)
-    sums_gu(3, 1)
-    out_sum.third(3)
-    three.second(1)
-    three.second(2)
-    sums_gu(2, 1)
-    three.arrive(3)
-    out_sum.second(1)
-    out_sum.second(0)
-    sums_gu(1, 1)
-    three.second(3)
-
     def attend_back(m):
         three.ready(m)
         rows = chunk(m)
@@ -1150,17 +990,6 @@
         attend_back(m)
         send_pair(m)
 
-    each(4, back_from_end)
-    pair_back.mark(range(4))
-    out_sum.third(2)
-    for m in (3, 2, 1):
-        sums_d(m, 1)
-    out_sum.third(1)
-    turn_o.sent()
-    grads_o((3, 0))
-    second.sent()
-    third = Collect(net, at, set_a, quarter, summed)
-
     def back_one(m):
         d = g ^ m
         rows = chunk(m)
@@ -1170,21 +999,6 @@
         dqkv[rows, 2 * HD :] = both[:, HD:].astype(BF16)
         part_a[rows, :] = dot_nt(dqkv[rows, :], w_qkv[...]).astype(BF16)
 
-    third.produce(back_one)
-    third.second(0)
-    third.third(3)
-    turn_qkv.sent()
-    grads_qkv((3, 2))
-    for m in (3, 2, 1):
-        sums_o(m)
-    third.third(2)
-    grads_qkv((1, 0))
-    third.third(1)
-    for m in (3, 2):
-        sums_qkv(m)
-    for b in (0, 1):
-        sums_gu(0, b)
-        sums_d(0, b)
     ends = []
 
     def share(source, target):
@@ -1204,18 +1018,9 @@
         on.start(0)
         final.append(on)
 
-    out_sum.last()
-
     def result_rows(i):
         few = row(i * 16, 16)
         result_own[few, :] = (hidden[few, :] + out_sum.total(few)).astype(BF16)
-
-    each(quarter // 16, result_rows)
-    share(result_own, result_out)
-    sums_qkv(1)
-    sums_o(0)
-    sums_qkv(0)
-    third.last()
 
     def back_rows(i, gain_grad):
         few = row(i * 16, 16)
@@ -1228,23 +1033,227 @@
         rows_own[few, :] = (dhidden[few, :] + back).astype(BF16)
         return gain_grad + jnp.sum(upstream * values * inverse, axis=0, keepdims=True)
 
-    gain_part[0:1, :] = lax.fori_loop(0, quarter // 16, back_rows, jnp.zeros((1, depth), F32))
     gain_sums = net.lot(
         range(1, shards), lambda m: (gain_part.at[:, columns_of(s ^ m)], gain_in.at[m - 1], (s ^ m, h)), gain_in
     )
+    gain_ends = net.lot(range(1, 4), lambda m: (gain_mid, gain_near.at[m - 1], (s, h ^ m)), gain_near)
+    gains[...] = jnp.zeros_like(gains)
+    gains[0:1, :] = gain_one[...].astype(F32).reshape(1, width)
+    gains[1:2, :] = gain_two[...].astype(F32).reshape(1, width)
+    for m in range(1, shards):
+        gain_moves.start(m)
+    gain_own = keep.put(gains, gain_slot)
+    turn_qkv.start(1)
+    turn_o.start(3)
+    one.start()
+    own_rows = keep.put(tok, rows_one.at[chunk(0), :])
+    own_strip = keep.put(tok.at[strip, :], own_x)
+    own_cot = keep.put(cot, rows_cot.at[chunk(0), :])
+    turn_qkv.start(3)
+    one.arrive(1)
+    turn_o.start(2)
+    turn_o.pass_on(3)
+    turn_qkv.start(2)
+    turn_o.mine()
+    turn_qkv.mine()
+    one.arrive(2)
+    gain_part[...] = jnp.zeros_like(gain_part)
+    each(total_rows // 64, clear)
+    each(groups * count // 64, tables)
+    gain_own.wait()
+    for m in range(1, shards):
+        gain_moves.arrived(m)
+    own_rows.wait()
+    own_strip.wait()
+    norm_one(0)
+    turn_qkv.pass_on(1)
+    grad.start()
+    turn_o.start(1)
+    turn_d.start(3, 1)
+    turn_gu.start(1, 1)
+    one.arrive(3)
+    turn_qkv.pass_on(3)
+    turn_qkv.pass_on(2)
+    one.second(2)
+    one.second(3)
+    turn_d.mine(1)
+    turn_gu.start(3, 0)
+    turn_d.start(2, 1)
+    one.second(1)
+    for m in (1, 2, 3):
+        one.ready(m)
+    one.sent()
+    for m in (1, 2, 3):
+        norm_one(m)
+    turn_d.start(3, 0)
+    turn_o.pass_on(2)
+    turn_qkv.ready()
+    turn_d.start(1, 0)
+    each(4, project)
+    pair_moves.mark(range(4))
+    grad.arrive(2)
+    turn_o.pass_on(1)
+    grad.arrive(1)
+    for m in (0, 1, 2, 3):
+        pair_moves.arrived(m)
+    turn_d.start(2, 0)
+    turn_gu.mine(0)
+    first.produce(attend)
+    first.third(3)
+    turn_d.start(1, 1)
+    turn_gu.pass_on(3, 0)
+    turn_d.pass_on(1, 0)
+    first.third(2)
+    first.third(1)
+    turn_gu.pass_on(1, 1)
+    turn_gu.start(2, 0)
+    turn_gu.mine(1)
+    turn_d.pass_on(2, 0)
+    turn_gu.start(1, 0)
+    first.second(0)
+    turn_d.pass_on(3, 1)
+    turn_d.pass_on(2, 1)
+    turn_d.pass_on(1, 1)
+    first.last()
+    each(quarter // 16, norm_two)
+    grad.arrive(3)
+    turn_d.mine(0)
+    two.start()
+    turn_gu.pass_on(1, 0)
+    grad.second(3)
+    grad.second(2)
+    turn_gu.start(2, 1)
+    grad.second(1)
+    two.arrive(1)
+    two.arrive(2)
+    turn_d.pass_on(3, 0)
+    turn_gu.pass_on(2, 0)
+    own_cot.wait()
+    for m in (1, 2, 3):
+        grad.ready(m)
+    turn_d.ready(1)
+    each(4, lambda m: early(m, 1))
+    turn_gu.start(3, 1)
+    two.arrive(3)
+    two.second(0)
+    turn_d.ready(0)
+    turn_gu.pass_on(2, 1)
+    each(4, lambda m: early(m, 0))
+    two.second(1)
+    two.second(3)
+    two.second(2)
+    turn_gu.pass_on(3, 1)
+    for m in (0, 1, 2, 3):
+        two.ready(m)
+    turn_gu.ready(0)
+    first.sent()
+    each(4, lambda m: feed(m, 0))
+    turn_gu.sent(0)
+    grads_gu((3, 3), 0)
+    turn_gu.ready(1)
+    second.produce(lambda m: feed(m, 1))
+    sums_gu(3, 0)
+    turn_gu.sent(1)
+    grads_gu((3, 3), 1)
+    second.third(3)
+    each(4, lambda m: out_part(m, 0))
+    second.second(0)
+    grads_gu((2, 2), 0)
+    second.third(2)
+    turn_d.sent(0)
+    grads_d((1, 1), 0)
+    second.third(1)
+    grads_d((0, 0), 0)
+    each(4, lambda m: out_part(m, 1))
+    for m in (3, 2, 1, 0):
+        out_sum.first(m)
+    grads_gu((1, 1), 1)
+    sums_gu(2, 0)
+    grads_gu((2, 2), 1)
+    out_sum.second(2)
+    turn_d.sent(1)
+    grads_d((2, 2), 1)
+    out_sum.second(3)
+    grads_gu((0, 0), 1)
+    grads_gu((1, 1), 0)
+    grads_d((3, 3), 0)
+    second.last()
+    gain_part[1:2, :] = lax.fori_loop(0, quarter // 16, back_two, jnp.zeros((1, depth), F32))
+    three.start()
+    out_sum.third(3)
+    grads_d((3, 3), 1)
+    grads_gu((0, 0), 0)
+    sums_gu(3, 1)
+    grads_d((1, 1), 1)
+    three.arrive(2)
+    three.arrive(1)
+    out_sum.third(2)
+    sums_d(3, 1)
+    three.arrive(3)
+    three.second(1)
+    grads_d((2, 2), 0)
+    sums_gu(2, 1)
+    three.second(0)
+    sums_d(2, 1)
+    sums_d(1, 0)
+    out_sum.second(1)
+    sums_gu(0, 0)
+    out_sum.second(0)
+    sums_gu(1, 1)
+    three.second(2)
+    three.second(3)
+    each(4, back_from_end)
+    pair_back.mark(range(4))
+    out_sum.third(1)
+    sums_d(1, 1)
+    sums_d(2, 0)
+    second.sent()
+    third.produce(back_one)
+    turn_o.sent()
+    grads_o((1, 1))
+    third.third(3)
+    sums_d(3, 0)
+    turn_qkv.sent()
+    grads_qkv((2, 2))
+    third.second(0)
+    third.third(2)
+    grads_o((3, 3))
+    third.third(1)
+    grads_d((0, 0), 1)
+    grads_o((0, 0))
+    sums_qkv(2)
+    sums_gu(1, 0)
+    grads_qkv((1, 1))
+    grads_o((2, 2))
+    grads_qkv((3, 3))
+    sums_d(0, 0)
+    sums_o(3)
+    grads_qkv((0, 0))
+    out_sum.last()
+    each(quarter // 16, result_rows)
+    share(result_own, result_out)
+    sums_o(1)
+    sums_o(0)
+    sums_o(2)
+    relay()
+    third.last()
+    gain_part[0:1, :] = lax.fori_loop(0, quarter // 16, back_rows, jnp.zeros((1, depth), F32))
     for m in range(1, shards):
         gain_sums.start(m)
+    share(rows_own, rows_out)
+    sums_gu(0, 1)
+    sums_qkv(3)
+    sums_qkv(1)
+    sums_d(0, 1)
+    sums_qkv(0)
     relay()
-    share(rows_own, rows_out)
     total = gain_part[:, columns_of(s)]
     for m in range(1, shards):
         gain_sums.arrived(m)
         total += gain_in[m - 1]
     gain_mid[...] = total
-    gain_ends = net.lot(range(1, 4), lambda m: (gain_mid, gain_near.at[m - 1], (s, h ^ m)), gain_near)
     for m in range(1, 4):
         gain_ends.start(m)
-    relay()
     for m in range(1, 4):
         gain_ends.arrived(m)
         total += gain_near[m - 1]

time: 331 us -> 318 us (0.961)
  Pallas kernels: 330 us -> 317 us
    pallas_call x1, Pallas kernels: 321 us -> 308 us  [rows_plan(): pl.pallas_call(functools.partial(layer_body, groups, ranks), out_shape=ou...]
where the time goes in v6:
time: 318 us
  Pallas kernels  317 us (100%)
    pallas_call x1, Pallas kernels, rows_plan(): pl.pallas_call(functools.partial(layer_body, groups, ranks), out_shape=ou...  308 us
    pallas_call x1, Pallas kernels, rows_plan(): pl.pallas_call(cast_body, grid=(steps,), out_shape=[gain_row, gain_row, m...  8.77 us

profile of v6, /device:TPU:0, one launch (start us, length us, event | category | flops | bytes accessed | tf_op | source)
XLA Modules:
  0.0 317.7 jit_solution(8557586965371652001)
XLA Ops:
  0.6 308.1 %shard_map.194 = (bf16[256,2048]{1,0:T(8,128)(2,1)}, bf16[256,2048]{1,0:T(8,128)(2,1)}, f32[8,256]{1,0:T(8,128)}, bf16[256,512]{1,0:T(8,128)(2,1)}, bf16[256,512...) custom-call(bf16[256,2048]{1,0:T(8,128)(2,1)} %refs_0_.1, ...), custom_call_target="tpu_custom_call" | custom-call | tf_op jit(solution)/shard_map/pallas_call | solution.py:1332
  308.8 8.8 %shard_map.195 = (f32[256]{0:T(256)}, f32[256]{0:T(256)}, bf16[256,2048]{1,0:T(8,128)(2,1)}, bf16[256,2048]{1,0:T(8,128)(2,1)}, f32[256,512]{1,0:T(8,128)}, /*in...) custom-call(f32[8,256]{1,0:T(8,128)} %get-tuple-element.32.refs_0_, ...), custom_call_target="tpu_custom_call" | custom-call | tf_op jit(solution)/shard_map/pallas_call | solution.py:1352

commit v7 on v6

--- a/solution.py
+++ b/solution.py
@@ -17,8 +17,9 @@
 epsilon = 1e-05
 block_limit = 512
 VMEM_LIMIT = 63 * 2**20
-SENDS, RECEIVES, KEEPS = 103, 295, 26
+SENDS, RECEIVES, KEEPS = 59, 217, 30
 PIECES = 2
+PARTS = (2, 2)
 
 
 def tables(offset, length, half_width):
@@ -425,8 +426,14 @@
         some = buffer.at[0 : (4 - low) * quarter, :]
         self.z = net.lot(range(PIECES, 4 * PIECES), along, buffer.at[0 : 3 * quarter, :])
         self.x = net.lot(indices, moved(0, at.across()), some)
-        self.c = net.lot(indices, moved(0, at.near()), some)
-        self.d = net.lot(indices, moved(1, at.near()), some)
+
+        def near(m):
+            blocks = [self.block(m, k, p) for k in (0, 1) for p in range(PIECES)]
+            return [(block, block, at.near()) for block in blocks]
+
+        self.n = net.lot(
+            range(low, 4), near, buffer.at[0 : 2 * (4 - low) * quarter, :], lambda m: buffer.at[0 : 2 * quarter, :]
+        )
 
     def block(self, m, k, p):
         at = self.at
@@ -435,15 +442,15 @@
 
     def pass_on(self, j):
         self.x.start(j)
-        self.c.start(j)
-
-    def start(self):
-        for m in (2, 1):
-            for p in range(PIECES):
-                self.z.start(m * PIECES + p)
-        if not self.shared:
-            for p in range(PIECES):
-                self.pass_on(p)
+        self.n.start(j // PIECES, (j % PIECES,))
+
+    def start(self, m):
+        for p in range(PIECES):
+            self.z.start(m * PIECES + p)
+
+    def start_own(self):
+        for p in range(PIECES):
+            self.pass_on(p)
 
     def arrive(self, m):
         for p in range(PIECES):
@@ -456,15 +463,13 @@
     def second(self, m):
         for p in range(PIECES):
             self.x.arrived(m * PIECES + p)
-            self.d.start(m * PIECES + p)
+            self.n.start(m, (PIECES + p,))
 
     def ready(self, m):
-        for p in range(PIECES):
-            self.c.arrived(m * PIECES + p)
-            self.d.arrived(m * PIECES + p)
+        self.n.arrived(m)
 
     def sent(self):
-        for lot in (self.z, self.x, self.c, self.d):
+        for lot in (self.z, self.x, self.n):
             lot.sent()
 
 
@@ -574,45 +579,40 @@
 class Turn:
     def __init__(self, net, keep, at, source, view, blocks):
         self.keep, self.at, self.source, self.view, self.blocks = keep, at, source, view, blocks
-        self.z, self.o, self.y, self.own = [], [], [], {}
-        for b, (items, place) in enumerate(blocks):
+        self.z, self.y, self.own = [], [], {}
+        for b, (items, place, several) in enumerate(blocks):
 
             def out(m, items=items):
                 return [(source(i, at.g ^ m), view(i, at.s), at.along(m)) for i in items]
 
-            def beside(m, items=items):
-                return [(source(i, at.g), view(i, at.s), at.beside()) for i in items]
-
-            def on(m, place=place):
-                block = place(at.s ^ (m * at.ranks))
-                return (block, block, at.beside())
+            def beside(_, items=items, place=place):
+                own = [(source(i, at.g), view(i, at.s), at.beside()) for i in items]
+                others = [place(at.s ^ (m * at.ranks)) for m in (1, 2, 3)]
+                return own + [(block, block, at.beside()) for block in others]
 
             def arrival(m, place=place):
                 return place(at.s ^ (m * at.ranks))
 
-            self.z.append(net.lot((1, 2, 3), out, lambda m, place=place: place(at.s), arrival, apart=True))
-            self.o.append(net.lot((0,), beside, place(at.s), arrival))
-            self.y.append(net.lot((1, 2, 3), on, lambda m, place=place: place(at.s), apart=True))
+            self.z.append(net.lot((1, 2, 3), out, several(3), arrival))
+            self.y.append(net.lot((0,), beside, several(4), lambda _, several=several: several(4)))
 
     def start(self, m, b=0, pieces=None):
         self.z[b].start(m, pieces)
 
     def mine(self, b=0):
-        at = self.at
-        for i in self.blocks[b][0]:
-            self.own[i] = self.keep.put(self.source(i, at.g), self.view(i, at.s))
-        self.o[b].start(0)
+        items = self.blocks[b][0]
+        for i in items:
+            self.own[i] = self.keep.put(self.source(i, self.at.g), self.view(i, self.at.s))
+        self.y[b].start(0, range(len(items)))
 
     def pass_on(self, m, b=0):
         self.z[b].arrived(m)
-        self.y[b].start(m)
+        self.y[b].start(0, (len(self.blocks[b][0]) + m - 1,))
 
     def ready(self, b=0):
         for i in self.blocks[b][0]:
             self.own[i].wait()
-        self.o[b].arrived(0)
-        for m in (1, 2, 3):
-            self.y[b].arrived(m)
+        self.y[b].arrived(0)
 
     def sent(self, b=0):
         self.y[b].sent()
@@ -653,7 +653,15 @@
     quarter = count // 4
     width = gains.shape[1]
     units = gw.shape[1] // groups
-    half = units // 2
+    bounds = [units * sum(PARTS[:b]) // sum(PARTS) for b in range(len(PARTS) + 1)]
+    lanes_of = [slice(a, b) for a, b in zip(bounds, bounds[1:])]
+    pairs_of = [slice(2 * a, 2 * b) for a, b in zip(bounds, bounds[1:])]
+    size_of = [b - a for a, b in zip(bounds, bounds[1:])]
+
+    def gate_up(b, i):
+        start = pairs_of[b].start + i * size_of[b]
+        return slice(start, start + size_of[b])
+
     total_rows = count * shards
     score_scale = 1.0 / math.sqrt(HD)
     score_shift = math.log(total_rows)
@@ -677,33 +685,44 @@
         net, keep, at,
         lambda i, group: (qw, kw, vw)[i].at[:, lane(group * HD, HD)],
         lambda i, shard: w_qkv.at[shard_rows(shard), i * HD : (i + 1) * HD],
-        [((0, 1, 2), lambda shard: w_qkv.at[shard_rows(shard), :])],
-    )
+        [((0, 1, 2), lambda shard: w_qkv.at[shard_rows(shard), :], lambda n: w_qkv.at[0 : n * width, :])],
+    )
+    few = width // 2
     turn_gu = Turn(
         net, keep, at,
-        lambda i, group: (gw, uw)[i % 2].at[:, lane(group * units + (i // 2) * half, half)],
-        lambda i, shard: w_gu.at[shard_rows(shard), i * half : (i + 1) * half],
-        [((2 * b, 2 * b + 1), lambda shard, b=b: w_gu.at[shard_rows(shard), b * units : (b + 1) * units]) for b in (0, 1)],
+        lambda i, group: (gw, uw)[i // 2 % 2].at[
+            i % 2 * few : (i % 2 + 1) * few, lane(group * units + lanes_of[i // 4].start, size_of[i // 4])
+        ],
+        lambda i, shard: w_gu.at[row(shard * width + i % 2 * few, few), gate_up(i // 4, i // 2 % 2)],
+        [
+            (range(4 * b, 4 * b + 4), lambda shard, p=p: w_gu.at[shard_rows(shard), p], lambda n, p=p: w_gu.at[0 : n * width, p])
+            for b, p in enumerate(pairs_of)
+        ],
     )
     turn_o = Turn(
         net, keep, at,
         lambda i, group: ow.at[row(group * HD, HD), :],
         lambda i, shard: w_o.at[:, columns_of(shard)],
-        [((0,), lambda shard: w_o.at[:, columns_of(shard)])],
+        [((0,), lambda shard: w_o.at[:, columns_of(shard)], lambda n: w_o.at[:, 0 : n * width])],
     )
     turn_d = Turn(
         net, keep, at,
-        lambda i, group: dw.at[row(group * units + i * half, half), :],
-        lambda i, shard: w_d.at[i * half : (i + 1) * half, columns_of(shard)],
-        [((b,), lambda shard, b=b: w_d.at[b * half : (b + 1) * half, columns_of(shard)]) for b in (0, 1)],
+        lambda i, group: dw.at[lane(group * units + lanes_of[i].start, size_of[i]), :],
+        lambda i, shard: w_d.at[lanes_of[i], columns_of(shard)],
+        [
+            ((b,), lambda shard, p=p: w_d.at[p, columns_of(shard)], lambda n, p=p: w_d.at[p, 0 : n * width])
+            for b, p in enumerate(lanes_of)
+        ],
     )
 
     gain_slot = gains_all.at[:, columns_of(s)]
-    gain_moves = net.lot(range(1, shards), lambda m: (gains, gain_slot, (s ^ m, h)), gain_in)
+    gain_moves = net.lot(
+        (0,), lambda _: [(gains, gain_slot, (s ^ m, h)) for m in range(1, shards)], gain_in, lambda _: gain_in
+    )
     strip = row(at.q * quarter, quarter)
     mine_start = (g * 4 + at.q) * quarter
     span = ranks * count
-    one = Spread(net, at, rows_one, quarter, tok)
+    one = Spread(net, at, rows_dh, quarter, tok)
     grad = Spread(net, at, rows_cot, quarter, cot)
     two = Spread(net, at, rows_two, quarter)
     three = Spread(net, at, rows_dh, quarter)
@@ -731,7 +750,7 @@
     def norm_one(m):
         def some(i):
             rows = row((g ^ m) * count + i * 32, 32)
-            values = rows_one[rows, :].astype(F32)
+            values = rows_dh[rows, :].astype(F32)
             inverse = lax.rsqrt(mean_square(values) + epsilon)
             rows_one[rows, :] = (values * inverse * gains_all[0:1, :]).astype(BF16)
 
@@ -774,10 +793,8 @@
         low = total.astype(BF16)
         mix[rows, :] = low
 
-        @pl.when(m == 3)
-        def _():
+        if m == 3:
             turn_o.ready()
-
         part_a[rows, :] = dot(low, w_o[...]).astype(BF16)
 
     def norm_two(i):
@@ -788,20 +805,20 @@
         rows_two[row(mine_start + i * 16, 16), :] = (values * inverse * gains_all[1:2, :]).astype(BF16)
 
     def early(m, b):
-        lanes = slice(b * half, (b + 1) * half)
+        lanes = lanes_of[b]
         dmixed[chunk(m), lanes] = dot_nt(rows_cot[chunk(m), :], w_d[lanes, :])
 
     def feed(m, b):
         rows = chunk(m)
-        lanes, pair = slice(b * half, (b + 1) * half), slice(b * units, (b + 1) * units)
+        lanes, pair, size = lanes_of[b], pairs_of[b], size_of[b]
         both = dot(rows_two[rows, :], w_gu[:, pair])
-        gate, up = both[:, :half], both[:, half:]
+        gate, up = both[:, :size], both[:, size:]
         sig = jax.nn.sigmoid(gate)
         act = gate * sig
         mixed[rows, lanes] = (act * up).astype(BF16)
         back = dmixed[rows, lanes]
-        dgu[rows, b * units : b * units + half] = (back * up * sig * (1.0 + gate * (1.0 - sig))).astype(BF16)
-        dgu[rows, b * units + half : (b + 1) * units] = (back * act).astype(BF16)
+        dgu[rows, gate_up(b, 0)] = (back * up * sig * (1.0 + gate * (1.0 - sig))).astype(BF16)
+        dgu[rows, gate_up(b, 1)] = (back * act).astype(BF16)
         total = dot_nt(dgu[rows, pair], w_gu[:, pair])
         if b:
             total += part_a[rows, :].astype(F32)
@@ -809,7 +826,7 @@
 
     def out_part(m, b):
         rows = chunk(m)
-        lanes = slice(b * half, (b + 1) * half)
+        lanes = lanes_of[b]
         total = dot(mixed[rows, lanes], w_d[lanes, :])
         if b:
             total += part_b[rows, :].astype(F32)
@@ -839,11 +856,12 @@
 
         return net.lot(range(4), describe, bulk)
 
-    pairs_of = [slice(b * units, (b + 1) * units) for b in (0, 1)]
-    lanes_of = [slice(b * half, (b + 1) * half) for b in (0, 1)]
     moves_gu = [
-        beside(lambda shard, p=p: w_gu.at[shard_rows(shard), p], lambda d, p=p: in_gu.at[d, :, p], in_gu.at[:, :, p])
-        for p in pairs_of
+        [
+            beside(lambda shard, p=p: w_gu.at[shard_rows(shard), p], lambda d, p=p: in_gu.at[d, :, p], in_gu.at[:, :, p])
+            for p in (gate_up(b, 0), gate_up(b, 1))
+        ]
+        for b in range(len(PARTS))
     ]
     moves_d = [
         beside(lambda shard, p=p: w_d.at[p, columns_of(shard)], lambda d, p=p: in_d.at[d, p, :], in_d.at[:, p, :])
@@ -852,11 +870,13 @@
     moves_qkv = beside(lambda shard: w_qkv.at[shard_rows(shard), :], lambda d: in_qkv.at[d], in_qkv)
     moves_o = beside(lambda shard: w_o.at[:, columns_of(shard)], lambda d: in_o.at[d], in_o)
 
-    def grads_gu(groups_, b):
+    def grads_gu(groups_, b, i):
         def work(shard):
-            w_gu[shard_rows(shard), pairs_of[b]] = dot_tn(rows_two[:, columns_of(shard)], dgu[:, pairs_of[b]]).astype(BF16)
-
-        several(groups_, work, moves_gu[b])
+            w_gu[shard_rows(shard), gate_up(b, i)] = dot_tn(
+                rows_two[:, columns_of(shard)], dgu[:, gate_up(b, i)]
+            ).astype(BF16)
+
+        several(groups_, work, moves_gu[b][i])
 
     def grads_d(groups_, b):
         def work(shard):
@@ -880,13 +900,49 @@
 
     final, final_own = [], []
 
-    def give(moves, whole_, m):
-        if m:
-            lot = net.lot((0,), lambda j: [(a, b, at.along(m)) for a, b in moves], whole_, lambda j: whole_)
-            lot.start(0)
-            final.append(lot)
-        else:
-            final_own.extend(keep.put(a, b) for a, b in moves)
+    def owners(moves, several):
+        pieces = [(a, b, at.along(m)) for m in (1, 2, 3) for a, b in moves(m)]
+        lot = net.lot((0,), lambda _: pieces, several, lambda _: several)
+        final.append(lot)
+
+        def give(m, i=None):
+            blocks = moves(m)
+            for k in range(len(blocks)) if i is None else (i,):
+                if m:
+                    lot.start(0, ((m - 1) * len(blocks) + k,))
+                else:
+                    final_own.append(keep.put(*blocks[k]))
+
+        return give
+
+    def shard_of(m):
+        return (g ^ m) * ranks + r
+
+    def gate_up_moves(b):
+        def moves(m):
+            for i, out in enumerate((g_out, u_out)):
+                place = out.at[:, lane(g * units + lanes_of[b].start, size_of[b])]
+                yield (w_gu.at[shard_rows(shard_of(m)), gate_up(b, i)], place)
+
+        return lambda m: list(moves(m))
+
+    def down_moves(b):
+        place = d_out.at[lane(g * units + lanes_of[b].start, size_of[b]), :]
+        return lambda m: [(w_d.at[lanes_of[b], columns_of(shard_of(m))], place)]
+
+    def qkv_moves(m):
+        rows = shard_rows(shard_of(m))
+        return [
+            (w_qkv.at[rows, i * HD : (i + 1) * HD], out.at[:, lane(g * HD, HD)])
+            for i, out in enumerate((q_out, k_out, v_out))
+        ]
+
+    give_gu = [owners(gate_up_moves(b), w_gu.at[0 : 3 * width, p]) for b, p in enumerate(pairs_of)]
+    give_d = [owners(down_moves(b), w_d.at[p, 0 : 3 * width]) for b, p in enumerate(lanes_of)]
+    give_qkv = owners(qkv_moves, w_qkv.at[0 : 3 * width, :])
+    give_o = owners(
+        lambda m: [(w_o.at[:, columns_of(shard_of(m))], o_out.at[row(g * HD, HD), :])], w_o.at[:, 0 : 3 * width]
+    )
 
     def sums(m, lot, mine_of, other_of, size):
         lot.arrived(m)
@@ -898,29 +954,24 @@
 
         each(size // 32, step)
 
-    def sums_gu(m, b):
-        d, p = g ^ m, pairs_of[b]
+    def sums_gu(m, b, i):
+        d, p = g ^ m, gate_up(b, i)
         start = (d * ranks + r) * width
         sums(
-            m, moves_gu[b],
-            lambda i: (w_gu, row(start + i * 32, 32), p), lambda i: (in_gu, d, row(i * 32, 32), p), width,
+            m, moves_gu[b][i],
+            lambda k: (w_gu, row(start + k * 32, 32), p), lambda k: (in_gu, d, row(k * 32, 32), p), width,
         )
-        moves = []
-        for i, out in enumerate((g_out, u_out)):
-            place = b * units + i * half
-            moves.append((w_gu.at[row(start, width), place : place + half], out.at[:, lane(g * units + b * half, half)]))
-        give(moves, w_gu.at[row(start, width), p], m)
+        give_gu[b](m, i)
 
     def sums_d(m, b):
-        d, base = g ^ m, b * half
+        d, base = g ^ m, lanes_of[b].start
         columns = columns_of(d * ranks + r)
         sums(
             m, moves_d[b],
             lambda i: (w_d, row(base + i * 32, 32), columns),
-            lambda i: (in_d, d, row(base + i * 32, 32), slice(None)), half,
+            lambda i: (in_d, d, row(base + i * 32, 32), slice(None)), size_of[b],
         )
-        block = w_d.at[lanes_of[b], columns]
-        give([(block, d_out.at[row(g * units + base, half), :])], block, m)
+        give_d[b](m)
 
     def sums_o(m):
         d = g ^ m
@@ -929,7 +980,7 @@
             m, moves_o,
             lambda i: (w_o, row(i * 32, 32), columns), lambda i: (in_o, d, row(i * 32, 32), slice(None)), HD,
         )
-        give([(w_o.at[:, columns], o_out.at[row(g * HD, HD), :])], w_o.at[:, columns], m)
+        give_o(m)
 
     def sums_qkv(m):
         d = g ^ m
@@ -939,11 +990,7 @@
             lambda i: (w_qkv, row(start + i * 32, 32), slice(None)),
             lambda i: (in_qkv, d, row(i * 32, 32), slice(None)), width,
         )
-        moves = [
-            (w_qkv.at[row(start, width), i * HD : (i + 1) * HD], out.at[:, lane(g * HD, HD)])
-            for i, out in enumerate((q_out, k_out, v_out))
-        ]
-        give(moves, w_qkv.at[row(start, width), :], m)
+        give_qkv(m)
 
     def back_two(i, gain_grad):
         few = row(i * 16, 16)
@@ -999,18 +1046,18 @@
         dqkv[rows, 2 * HD :] = both[:, HD:].astype(BF16)
         part_a[rows, :] = dot_nt(dqkv[rows, :], w_qkv[...]).astype(BF16)
 
-    ends = []
-
-    def share(source, target):
+    ends = {}
+
+    def share(i, source, target):
         place = target.at[strip, :]
         final_own.append(keep.put(source, place))
         lot = net.lot((0, 1), lambda j: (source, place, (at.near(), at.across())[j]), target.at[0 : 2 * quarter, :])
         lot.start(0)
         lot.start(1)
-        ends.append((lot, target))
-
-    def relay():
-        lot, target = ends.pop()
+        ends[i] = (lot, target)
+
+    def relay(i):
+        lot, target = ends[i]
         lot.arrived(1)
         final.append(lot)
         block = target.at[row((at.q ^ 1) * quarter, quarter), :]
@@ -1034,228 +1081,295 @@
         return gain_grad + jnp.sum(upstream * values * inverse, axis=0, keepdims=True)
 
     gain_sums = net.lot(
-        range(1, shards), lambda m: (gain_part.at[:, columns_of(s ^ m)], gain_in.at[m - 1], (s ^ m, h)), gain_in
-    )
-    gain_ends = net.lot(range(1, 4), lambda m: (gain_mid, gain_near.at[m - 1], (s, h ^ m)), gain_near)
+        (0,),
+        lambda _: [(gain_part.at[:, columns_of(s ^ m)], gain_in.at[m - 1], (s ^ m, h)) for m in range(1, shards)],
+        gain_in,
+        lambda _: gain_in,
+    )
+    gain_ends = net.lot(
+        (0,),
+        lambda _: [(gain_mid, gain_near.at[m - 1], (s, h ^ m)) for m in range(1, 4)],
+        gain_near,
+        lambda _: gain_near,
+    )
     gains[...] = jnp.zeros_like(gains)
     gains[0:1, :] = gain_one[...].astype(F32).reshape(1, width)
     gains[1:2, :] = gain_two[...].astype(F32).reshape(1, width)
-    for m in range(1, shards):
-        gain_moves.start(m)
+    gain_moves.start(0)
     gain_own = keep.put(gains, gain_slot)
-    turn_qkv.start(1)
-    turn_o.start(3)
-    one.start()
-    own_rows = keep.put(tok, rows_one.at[chunk(0), :])
+    own_rows = keep.put(tok, rows_dh.at[chunk(0), :])
     own_strip = keep.put(tok.at[strip, :], own_x)
     own_cot = keep.put(cot, rows_cot.at[chunk(0), :])
     turn_qkv.start(3)
+    one.start(2)
+    one.start(1)
+    turn_qkv.start(1)
+    turn_o.start(1)
     one.arrive(1)
-    turn_o.start(2)
-    turn_o.pass_on(3)
+    turn_qkv.mine()
     turn_qkv.start(2)
-    turn_o.mine()
-    turn_qkv.mine()
-    one.arrive(2)
     gain_part[...] = jnp.zeros_like(gain_part)
     each(total_rows // 64, clear)
     each(groups * count // 64, tables)
+    grad.z.start(2 * PIECES + 0)
+    one.arrive(2)
+    turn_o.pass_on(1)
+    turn_gu.start(1, 0, (1,))
+    turn_gu.start(3, 0, (2,))
+    turn_o.start(3)
     gain_own.wait()
-    for m in range(1, shards):
-        gain_moves.arrived(m)
+    gain_moves.arrived(0)
     own_rows.wait()
     own_strip.wait()
     norm_one(0)
+    turn_qkv.pass_on(3)
+    one.second(2)
+    turn_o.start(2)
     turn_qkv.pass_on(1)
-    grad.start()
-    turn_o.start(1)
-    turn_d.start(3, 1)
-    turn_gu.start(1, 1)
+    grad.z.start(2 * PIECES + 1)
+    turn_gu.start(2, 0, (3,))
+    turn_d.start(1, 0)
+    one.ready(2)
+    norm_one(2)
+    grad.z.start(1 * PIECES + 1)
+    turn_qkv.pass_on(2)
+    turn_gu.start(1, 0, (2,))
     one.arrive(3)
-    turn_qkv.pass_on(3)
-    turn_qkv.pass_on(2)
-    one.second(2)
+    turn_o.mine()
+    one.second(1)
+    turn_qkv.ready()
+    project(0)
+    turn_d.start(2, 1)
+    one.ready(1)
+    norm_one(1)
+    project(1)
+    project(2)
     one.second(3)
-    turn_d.mine(1)
-    turn_gu.start(3, 0)
-    turn_d.start(2, 1)
-    one.second(1)
-    for m in (1, 2, 3):
-        one.ready(m)
-    one.sent()
-    for m in (1, 2, 3):
-        norm_one(m)
+    one.ready(3)
+    norm_one(3)
+    project(3)
     turn_d.start(3, 0)
+    turn_gu.start(1, 0, (0,))
     turn_o.pass_on(2)
-    turn_qkv.ready()
-    turn_d.start(1, 0)
-    each(4, project)
-    pair_moves.mark(range(4))
+    turn_d.start(2, 0)
+    turn_o.pass_on(3)
     grad.arrive(2)
-    turn_o.pass_on(1)
-    grad.arrive(1)
     for m in (0, 1, 2, 3):
         pair_moves.arrived(m)
-    turn_d.start(2, 0)
-    turn_gu.mine(0)
-    first.produce(attend)
+    attend(3)
+    first.first(3)
+    attend(2)
+    first.first(2)
+    grad.z.start(1 * PIECES + 0)
+    first.second(3)
+    turn_d.start(3, 1)
+    turn_d.mine(1)
+    first.second(2)
+    attend(1)
+    first.first(1)
+    turn_gu.mine(1)
+    turn_gu.start(3, 0, (0,))
     first.third(3)
+    grad.arrive(3)
+    turn_d.pass_on(2, 1)
+    turn_d.pass_on(1, 0)
+    first.second(1)
+    first.third(2)
+    grad.second(2)
+    attend(0)
+    first.first(0)
+    turn_d.pass_on(2, 0)
+    turn_gu.start(3, 0, (3,))
+    first.third(1)
+    turn_gu.start(2, 0, (1,))
+    turn_d.pass_on(3, 1)
+    turn_gu.start(3, 0, (1,))
+    turn_gu.start(2, 0, (2,))
+    turn_d.mine(0)
     turn_d.start(1, 1)
-    turn_gu.pass_on(3, 0)
-    turn_d.pass_on(1, 0)
-    first.third(2)
-    first.third(1)
-    turn_gu.pass_on(1, 1)
-    turn_gu.start(2, 0)
-    turn_gu.mine(1)
-    turn_d.pass_on(2, 0)
-    turn_gu.start(1, 0)
+    turn_gu.start(2, 0, (0,))
+    turn_gu.start(1, 0, (3,))
+    turn_gu.start(1, 1, (1, 0))
     first.second(0)
-    turn_d.pass_on(3, 1)
-    turn_d.pass_on(2, 1)
-    turn_d.pass_on(1, 1)
+    grad.arrive(1)
+    turn_d.pass_on(3, 0)
     first.last()
     each(quarter // 16, norm_two)
-    grad.arrive(3)
-    turn_d.mine(0)
-    two.start()
+    two.start(1)
+    turn_gu.mine(0)
+    two.start(2)
+    two.start_own()
+    turn_d.pass_on(1, 1)
+    turn_gu.start(2, 1, (3,))
     turn_gu.pass_on(1, 0)
+    turn_gu.start(1, 1, (2,))
     grad.second(3)
-    grad.second(2)
-    turn_gu.start(2, 1)
+    turn_gu.start(1, 1, (3,))
+    two.second(0)
+    turn_d.ready(0)
+    turn_d.ready(1)
+    turn_gu.pass_on(2, 0)
     grad.second(1)
-    two.arrive(1)
-    two.arrive(2)
-    turn_d.pass_on(3, 0)
-    turn_gu.pass_on(2, 0)
+    turn_gu.start(2, 1, (1, 0))
+    turn_gu.pass_on(3, 0)
+    turn_gu.start(2, 1, (2,))
     own_cot.wait()
     for m in (1, 2, 3):
         grad.ready(m)
-    turn_d.ready(1)
+    each(4, lambda m: early(m, 0))
+    two.arrive(1)
+    two.arrive(2)
+    turn_gu.pass_on(1, 1)
+    two.second(1)
+    two.ready(1)
+    turn_gu.start(3, 1, (1,))
+    two.ready(0)
+    two.second(2)
+    turn_gu.start(3, 1, (2, 0, 3))
+    two.ready(2)
+    turn_gu.pass_on(2, 1)
     each(4, lambda m: early(m, 1))
-    turn_gu.start(3, 1)
     two.arrive(3)
-    two.second(0)
-    turn_d.ready(0)
-    turn_gu.pass_on(2, 1)
-    each(4, lambda m: early(m, 0))
-    two.second(1)
-    two.second(3)
-    two.second(2)
-    turn_gu.pass_on(3, 1)
-    for m in (0, 1, 2, 3):
-        two.ready(m)
     turn_gu.ready(0)
     first.sent()
-    each(4, lambda m: feed(m, 0))
+    one.sent()
+    each(2, lambda i: feed(1 - i, 0))
+    turn_gu.pass_on(3, 1)
+    two.second(3)
+    feed(2, 0)
+    two.ready(3)
+    feed(3, 0)
     turn_gu.sent(0)
-    grads_gu((3, 3), 0)
+    grads_gu((3, 3), 0, 0)
+    grads_gu((3, 3), 0, 1)
     turn_gu.ready(1)
-    second.produce(lambda m: feed(m, 1))
-    sums_gu(3, 0)
-    turn_gu.sent(1)
-    grads_gu((3, 3), 1)
-    second.third(3)
+    each(2, lambda i: (feed(3 - i, 1), second.first(3 - i)))
+    second.a.mark((3, 2))
+    sums_gu(3, 0, 0)
+    grads_gu((2, 2), 0, 0)
+    second.second(3)
     each(4, lambda m: out_part(m, 0))
-    second.second(0)
-    grads_gu((2, 2), 0)
-    second.third(2)
+    sums_gu(3, 0, 1)
+    second.second(2)
     turn_d.sent(0)
     grads_d((1, 1), 0)
-    second.third(1)
-    grads_d((0, 0), 0)
+    feed(1, 1)
+    second.first(1)
+    second.third(3)
+    feed(0, 1)
+    second.first(0)
+    second.second(1)
+    turn_gu.sent(1)
+    grads_gu((3, 3), 1, 1)
+    sums_d(1, 0)
     each(4, lambda m: out_part(m, 1))
     for m in (3, 2, 1, 0):
         out_sum.first(m)
-    grads_gu((1, 1), 1)
-    sums_gu(2, 0)
-    grads_gu((2, 2), 1)
-    out_sum.second(2)
+    grads_gu((2, 2), 0, 1)
+    second.third(2)
+    grads_gu((3, 3), 1, 0)
+    second.second(0)
+    second.third(1)
+    out_sum.second(1)
+    sums_gu(2, 0, 0)
+    sums_gu(2, 0, 1)
     turn_d.sent(1)
-    grads_d((2, 2), 1)
-    out_sum.second(3)
-    grads_gu((0, 0), 1)
-    grads_gu((1, 1), 0)
-    grads_d((3, 3), 0)
+    grads_d((3, 3), 1)
+    grads_gu((0, 0), 1, 1)
     second.last()
     gain_part[1:2, :] = lax.fori_loop(0, quarter // 16, back_two, jnp.zeros((1, depth), F32))
-    three.start()
+    three.start(1)
+    grads_gu((1, 1), 1, 1)
+    three.start(2)
+    grads_gu((1, 1), 0, 1)
+    out_sum.second(3)
+    grads_d((2, 2), 1)
+    three.start_own()
+    grads_gu((2, 2), 1, 1)
+    grads_d((3, 3), 0)
+    sums_gu(3, 1, 0)
+    grads_gu((1, 1), 1, 0)
+    grads_gu((2, 2), 1, 0)
     out_sum.third(3)
-    grads_d((3, 3), 1)
-    grads_gu((0, 0), 0)
-    sums_gu(3, 1)
-    grads_d((1, 1), 1)
+    three.arrive(1)
     three.arrive(2)
-    three.arrive(1)
-    out_sum.third(2)
     sums_d(3, 1)
+    grads_d((0, 0), 0)
+    sums_d(3, 0)
+    three.second(0)
+    grads_gu((0, 0), 0, 1)
+    grads_gu((0, 0), 1, 0)
+    grads_d((0, 0), 1)
+    sums_gu(1, 1, 1)
+    sums_gu(3, 1, 1)
+    sums_d(2, 1)
+    sums_gu(2, 1, 0)
+    sums_gu(1, 0, 1)
+    sums_gu(2, 1, 1)
     three.arrive(3)
+    three.second(2)
+    sums_gu(1, 1, 0)
+    grads_gu((0, 0), 0, 0)
     three.second(1)
+    out_sum.second(2)
     grads_d((2, 2), 0)
-    sums_gu(2, 1)
-    three.second(0)
-    sums_d(2, 1)
-    sums_d(1, 0)
-    out_sum.second(1)
-    sums_gu(0, 0)
-    out_sum.second(0)
-    sums_gu(1, 1)
-    three.second(2)
     three.second(3)
     each(4, back_from_end)
     pair_back.mark(range(4))
+    out_sum.second(0)
+    out_sum.third(2)
+    sums_gu(0, 1, 1)
+    grads_gu((1, 1), 0, 0)
     out_sum.third(1)
-    sums_d(1, 1)
-    sums_d(2, 0)
+    turn_o.sent()
+    grads_o((1, 0))
+    grads_o((3, 3))
     second.sent()
     third.produce(back_one)
-    turn_o.sent()
-    grads_o((1, 1))
-    third.third(3)
-    sums_d(3, 0)
+    sums_gu(0, 0, 0)
     turn_qkv.sent()
     grads_qkv((2, 2))
+    grads_qkv((3, 3))
+    grads_d((1, 1), 1)
+    grads_o((2, 2))
+    third.third(3)
+    sums_o(3)
     third.second(0)
+    grads_qkv((1, 1))
+    sums_d(2, 0)
+    sums_gu(1, 0, 0)
+    sums_o(1)
     third.third(2)
-    grads_o((3, 3))
     third.third(1)
-    grads_d((0, 0), 1)
-    grads_o((0, 0))
-    sums_qkv(2)
-    sums_gu(1, 0)
-    grads_qkv((1, 1))
-    grads_o((2, 2))
-    grads_qkv((3, 3))
-    sums_d(0, 0)
-    sums_o(3)
-    grads_qkv((0, 0))
+    sums_qkv(3)
     out_sum.last()
     each(quarter // 16, result_rows)
-    share(result_own, result_out)
-    sums_o(1)
+    share(0, result_own, result_out)
+    sums_d(1, 1)
     sums_o(0)
-    sums_o(2)
-    relay()
+    sums_qkv(2)
+    grads_qkv((0, 0))
     third.last()
     gain_part[0:1, :] = lax.fori_loop(0, quarter // 16, back_rows, jnp.zeros((1, depth), F32))
+    gain_sums.start(0)
+    share(1, rows_own, rows_out)
+    sums_o(2)
+    sums_qkv(0)
+    relay(0)
+    sums_gu(0, 1, 0)
+    sums_qkv(1)
+    sums_gu(0, 0, 1)
+    sums_d(0, 1)
+    sums_d(0, 0)
+    relay(1)
+    total = gain_part[:, columns_of(s)]
+    gain_sums.arrived(0)
     for m in range(1, shards):
-        gain_sums.start(m)
-    share(rows_own, rows_out)
-    sums_gu(0, 1)
-    sums_qkv(3)
-    sums_qkv(1)
-    sums_d(0, 1)
-    sums_qkv(0)
-    relay()
-    total = gain_part[:, columns_of(s)]
-    for m in range(1, shards):
-        gain_sums.arrived(m)
         total += gain_in[m - 1]
     gain_mid[...] = total
+    gain_ends.start(0)
+    gain_ends.arrived(0)
     for m in range(1, 4):
-        gain_ends.start(m)
-    for m in range(1, 4):
-        gain_ends.arrived(m)
         total += gain_near[m - 1]
     gains_out[...] = total
     for lot in final:

time: 318 us -> 313 us (0.984)
  Pallas kernels: 317 us -> 312 us
    pallas_call x1, Pallas kernels: 308 us -> 303 us  [rows_plan(): pl.pallas_call(functools.partial(layer_body, groups, ranks), out_shape=ou...]
where the time goes in v7:
time: 313 us
  Pallas kernels  312 us (100%)
    pallas_call x1, Pallas kernels, rows_plan(): pl.pallas_call(functools.partial(layer_body, groups, ranks), out_shape=ou...  303 us
    pallas_call x1, Pallas kernels, rows_plan(): pl.pallas_call(cast_body, grid=(steps,), out_shape=[gain_row, gain_row, m...  8.77 us

profile of v7, /device:TPU:0, one launch (start us, length us, event | category | flops | bytes accessed | tf_op | source)
XLA Modules:
  0.0 312.8 jit_solution(5290403323023010764)
XLA Ops:
  0.6 303.2 %shard_map.194 = (bf16[256,2048]{1,0:T(8,128)(2,1)}, bf16[256,2048]{1,0:T(8,128)(2,1)}, f32[8,256]{1,0:T(8,128)}, bf16[256,512]{1,0:T(8,128)(2,1)}, bf16[256,512...) custom-call(bf16[256,2048]{1,0:T(8,128)(2,1)} %refs_0_.1, ...), custom_call_target="tpu_custom_call" | custom-call | tf_op jit(solution)/shard_map/pallas_call | solution.py:1446
  303.8 8.8 %shard_map.195 = (f32[256]{0:T(256)}, f32[256]{0:T(256)}, bf16[256,2048]{1,0:T(8,128)(2,1)}, bf16[256,2048]{1,0:T(8,128)(2,1)}, f32[256,512]{1,0:T(8,128)}, /*in...) custom-call(f32[8,256]{1,0:T(8,128)} %get-tuple-element.32.refs_0_, ...), custom_call_target="tpu_custom_call" | custom-call | tf_op jit(solution)/shard_map/pallas_call | solution.py:1466

commit v8 on v7

--- a/solution.py
+++ b/solution.py
@@ -1453,7 +1453,7 @@
             collective_id=1, has_side_effects=True, vmem_limit_bytes=VMEM_LIMIT
         ),
     )(*ins)
-    steps = 8
+    steps = 2
 
     def sliced(array):
         rows, columns = array.shape

time: 313 us -> 311 us (level)
  no operation moved by 1% of the time
where the time goes in v8:
time: 311 us; the launch traced here: 310 us
  Pallas kernels  310 us (100%)
    pallas_call x1, Pallas kernels, rows_plan(): pl.pallas_call(functools.partial(layer_body, groups, ranks), out_shape=ou...  303 us
    pallas_call x1, Pallas kernels, rows_plan(): pl.pallas_call(cast_body, grid=(steps,), out_shape=[gain_row, gain_row, m...  6.45 us

profile of v8, /device:TPU:0, one launch (start us, length us, event | category | flops | bytes accessed | tf_op | source)
XLA Modules:
  0.0 310.5 jit_solution(11260543131750586510)
XLA Ops:
  0.6 303.2 %shard_map.194 = (bf16[256,2048]{1,0:T(8,128)(2,1)}, bf16[256,2048]{1,0:T(8,128)(2,1)}, f32[8,256]{1,0:T(8,128)}, bf16[256,512]{1,0:T(8,128)(2,1)}, bf16[256,512...) custom-call(bf16[256,2048]{1,0:T(8,128)(2,1)} %refs_0_.1, ...), custom_call_target="tpu_custom_call" | custom-call | tf_op jit(solution)/shard_map/pallas_call | solution.py:1446
  303.8 6.5 %shard_map.195 = (f32[256]{0:T(256)}, f32[256]{0:T(256)}, bf16[256,2048]{1,0:T(8,128)(2,1)}, bf16[256,2048]{1,0:T(8,128)(2,1)}, f32[256,512]{1,0:T(8,128)}, /*in...) custom-call(f32[8,256]{1,0:T(8,128)} %get-tuple-element.32.refs_0_, ...), custom_call_target="tpu_custom_call" | custom-call | tf_op jit(solution)/shard_map/pallas_call | solution.py:1466

commit v9 on v8

--- a/solution.py
+++ b/solution.py
@@ -1195,9 +1195,9 @@
     turn_d.pass_on(3, 0)
     first.last()
     each(quarter // 16, norm_two)
+    two.start(2)
     two.start(1)
     turn_gu.mine(0)
-    two.start(2)
     two.start_own()
     turn_d.pass_on(1, 1)
     turn_gu.start(2, 1, (3,))
@@ -1278,9 +1278,9 @@
     grads_gu((0, 0), 1, 1)
     second.last()
     gain_part[1:2, :] = lax.fori_loop(0, quarter // 16, back_two, jnp.zeros((1, depth), F32))
+    three.start(2)
     three.start(1)
     grads_gu((1, 1), 1, 1)
-    three.start(2)
     grads_gu((1, 1), 0, 1)
     out_sum.second(3)
     grads_d((2, 2), 1)

time: 311 us -> 310 us (level)
  no operation moved by 1% of the time
where the time goes in v9:
time: 310 us
  Pallas kernels  309 us (100%)
    pallas_call x1, Pallas kernels, rows_plan(): pl.pallas_call(functools.partial(layer_body, groups, ranks), out_shape=ou...  303 us
    pallas_call x1, Pallas kernels, rows_plan(): pl.pallas_call(cast_body, grid=(steps,), out_shape=[gain_row, gain_row, m...  6.45 us

profile of v9, /device:TPU:0, one launch (start us, length us, event | category | flops | bytes accessed | tf_op | source)
XLA Modules:
  0.0 310.2 jit_solution(3397266300496155286)
XLA Ops:
  0.6 302.9 %shard_map.194 = (bf16[256,2048]{1,0:T(8,128)(2,1)}, bf16[256,2048]{1,0:T(8,128)(2,1)}, f32[8,256]{1,0:T(8,128)}, bf16[256,512]{1,0:T(8,128)(2,1)}, bf16[256,512...) custom-call(bf16[256,2048]{1,0:T(8,128)(2,1)} %refs_0_.1, ...), custom_call_target="tpu_custom_call" | custom-call | tf_op jit(solution)/shard_map/pallas_call | solution.py:1446
  303.5 6.5 %shard_map.195 = (f32[256]{0:T(256)}, f32[256]{0:T(256)}, bf16[256,2048]{1,0:T(8,128)(2,1)}, bf16[256,2048]{1,0:T(8,128)(2,1)}, f32[256,512]{1,0:T(8,128)}, /*in...) custom-call(f32[8,256]{1,0:T(8,128)} %get-tuple-element.32.refs_0_, ...), custom_call_target="tpu_custom_call" | custom-call | tf_op jit(solution)/shard_map/pallas_call | solution.py:1466
